TPU v7x, 128 devices: a whole 4x4x4 slice. The times are simulated.
128 devices in a mesh: ctx: 8 (over x_lo, y), exp: 16 (over x_hi, z, core).
Axes of the slice: x: 4 (x_hi: 2, x_lo: 2; x = x_hi * 2 + x_lo), y: 4, z: 4, core: 2. Of those that a mesh axis runs over, the one named last changes fastest.
Arguments:
- q_heads: bfloat16 [8192, 2048], P('ctx', 'exp'), may hold values from -5 to 5
- k_heads: bfloat16 [8192, 2048], P('ctx', 'exp'), may hold values from -5 to 5
- v_heads: bfloat16 [8192, 2048], P('ctx', 'exp'), may hold values from -6 to 6
- doc_ids: int32 [8192], P('ctx'), may hold values from 0 to 3, never falling along the last dimension, each value on 1 to 4096 neighbouring positions
- w_out: bfloat16 [2048, 2048], P('exp'), may hold values from -0.125 to 0.125
- hidden_rows: bfloat16 [8192, 2048], P(('ctx', 'exp')), may hold values from -6 to 6
- out_grad: bfloat16 [8192, 2048], P(('ctx', 'exp')), may hold values from -6 to 6
- picks: int32 [128, 16, 6], P(('ctx', 'exp')), may hold values from 0 to 63, as said below
- gates: bfloat16 [128, 16, 6], P(('ctx', 'exp')), may hold values from 0.099609375 to 1
- w_gate: bfloat16 [16, 2048, 1408], P('exp'), may hold values from -0.125 to 0.125
- w_up: bfloat16 [16, 2048, 1408], P('exp'), may hold values from -0.125 to 0.125
- w_down: bfloat16 [16, 1408, 2048], P('exp'), may hold values from -0.15625 to 0.15625
Outputs:
- d_queries: bfloat16 [8192, 2048], P('ctx', 'exp')
- d_keys: bfloat16 [8192, 2048], P('ctx', 'exp')
- d_values: bfloat16 [8192, 2048], P('ctx', 'exp')
- d_hidden: bfloat16 [8192, 2048], P(('ctx', 'exp'))
- d_gates: bfloat16 [128, 16, 6], P(('ctx', 'exp'))
Inputs may be any that keep to these rules, and one draw needn't show every extreme that they name: `picks`: for each row block and expert the 6 offsets are distinct.
All inputs are finite; a program needn't handle non-finite values.
Results may differ from a plain program's by a relative error of at most 0.017.
Values may be sent and summed in bfloat16 or wider, within the bound.
A program may use at most 192 MiB of HBM per device.

v0:
```python
import math

import jax
import jax.numpy as jnp
from jax import lax
from jax.sharding import PartitionSpec as P

NEG = -1e30


def from_behind(value, axis, by):
    devices = lax.axis_size(axis)
    pairs = [(i, i + by) for i in range(devices) if 0 <= i + by < devices]
    return lax.ppermute(value, axis, pairs)


def passed_along(block, axis, distance):
    devices = range(lax.axis_size(axis))
    route = [((i - distance) % len(devices), i) for i in devices]
    return lax.ppermute(block, axis, route)


def score_block(queries, keys, query_place, key_place, query_doc, key_doc):
    scale = 1.0 / math.sqrt(queries.shape[1])
    scores = (
        lax.dot_general(queries, keys, (((1,), (1,)), ((), ())), preferred_element_type=jnp.float32)
        * scale
    )
    allowed = (key_place[None, :] <= query_place[:, None]) & (
        key_doc[None, :] == query_doc[:, None]
    )
    return (scores, allowed)


def stats_step(carry, queries, d_out, piece, query_place, query_doc, key_place, key_doc):
    top, total, weighted = carry
    scores, allowed = score_block(queries, piece[0], query_place, key_place, query_doc, key_doc)
    new_top = jnp.maximum(top, jnp.max(jnp.where(allowed, scores, NEG), axis=1))
    probs = jnp.where(allowed, jnp.exp(scores - new_top[:, None]), 0.0)
    d_probs = lax.dot_general(
        d_out, piece[1], (((1,), (1,)), ((), ())), preferred_element_type=jnp.float32
    )
    total = jnp.sum(probs, axis=1)
    weighted = jnp.sum(probs * d_probs, axis=1)
    return (new_top, total, weighted)


def grad_step(queries, d_out, lse, delta, piece, query_place, query_doc, key_place, key_doc):
    scores, allowed = score_block(queries, piece[0], query_place, key_place, query_doc, key_doc)
    probs = jnp.where(allowed, jnp.exp(scores - lse[:, None]), 0.0)
    probs_low = probs.astype(jnp.bfloat16)
    d_values = lax.dot_general(
        probs_low, d_out, (((0,), (0,)), ((), ())), preferred_element_type=jnp.float32
    )
    d_probs = lax.dot_general(
        d_out, piece[1], (((1,), (1,)), ((), ())), preferred_element_type=jnp.float32
    )
    d_scores = (probs * (d_probs - delta[:, None])).astype(jnp.bfloat16)
    d_query_part = jnp.dot(d_scores, piece[0], preferred_element_type=jnp.float32)
    d_keys = lax.dot_general(
        d_scores, queries, (((0,), (0,)), ((), ())), preferred_element_type=jnp.float32
    )
    return (d_query_part, jnp.stack([d_keys, d_values]))


def per_device(
    q_heads,
    k_heads,
    v_heads,
    doc_ids,
    w_out,
    hidden_rows,
    out_grad,
    picks,
    gates,
    w_gate,
    w_up,
    w_down,
):
    tok = q_heads.shape[0]
    width = q_heads.shape[1]
    rows = hidden_rows.shape[0]
    model = hidden_rows.shape[1]
    experts = picks.shape[1]
    slots = picks.shape[2]
    ncx = lax.axis_size("ctx")
    me = lax.axis_index("ctx")
    index = picks[0].reshape(-1)
    chosen_h = jnp.take(hidden_rows, index, axis=0).reshape(experts, 1, slots, model)
    chosen_g = jnp.take(out_grad, index, axis=0).reshape(experts, 1, slots, model)
    chosen_w = gates.reshape(experts, 1, slots)
    xs = lax.all_to_all(chosen_h, "exp", split_axis=0, concat_axis=1, tiled=True)
    gs = lax.all_to_all(chosen_g, "exp", split_axis=0, concat_axis=1, tiled=True)
    ws = lax.all_to_all(chosen_w, "exp", split_axis=0, concat_axis=1, tiled=True)
    local = xs.shape[0]
    x_rows = xs.reshape(local, -1, model)
    g_rows = gs.reshape(local, -1, model)
    weight = ws.reshape(local, -1).astype(jnp.float32)
    a = jnp.einsum("erd,edf->erf", x_rows, w_gate, preferred_element_type=jnp.float32)
    b = jnp.einsum("erd,edf->erf", x_rows, w_up, preferred_element_type=jnp.float32)
    u = jnp.einsum("erd,efd->erf", g_rows, w_down, preferred_element_type=jnp.float32)
    sig = jax.nn.sigmoid(a)
    act_gate = a * sig
    d_gate = jnp.sum(act_gate * b * u, axis=2).astype(jnp.bfloat16)
    d_act = weight[..., None] * u
    da = (d_act * b * sig * (1.0 + a * (1.0 - sig))).astype(jnp.bfloat16)
    db = (d_act * act_gate).astype(jnp.bfloat16)
    d_x = jnp.einsum("erf,edf->erd", da, w_gate, preferred_element_type=jnp.float32)
    d_x = d_x + jnp.einsum("erf,edf->erd", db, w_up, preferred_element_type=jnp.float32)
    d_x = d_x.astype(jnp.bfloat16).reshape(xs.shape)
    d_gate = d_gate.reshape(ws.shape)
    back_rows = lax.all_to_all(d_x, "exp", split_axis=1, concat_axis=0, tiled=True)
    back_gates = lax.all_to_all(d_gate, "exp", split_axis=1, concat_axis=0, tiled=True)
    flat_rows = back_rows.reshape(experts * slots, model)
    one_hot = (index[:, None] == jnp.arange(rows)[None, :]).astype(jnp.bfloat16)
    summed = lax.dot_general(
        one_hot, flat_rows, (((0,), (0,)), ((), ())), preferred_element_type=jnp.float32
    )
    d_hidden = (out_grad.astype(jnp.float32) + summed).astype(jnp.bfloat16)
    d_gates = back_gates.reshape(1, experts, slots)
    d_out = lax.dot_general(
        lax.all_gather(d_hidden, "exp", axis=0, tiled=True),
        w_out,
        (((1,), (1,)), ((), ())),
        preferred_element_type=jnp.float32,
    ).astype(jnp.bfloat16)
    doc_all = lax.all_gather(doc_ids, "ctx", axis=0, tiled=True)
    query_place = me * tok + jnp.arange(tok)
    kv_pair = jnp.stack([k_heads, v_heads])
    start_stats = (
        jnp.full((tok,), NEG, jnp.float32),
        jnp.zeros((tok,), jnp.float32),
        jnp.zeros((tok,), jnp.float32),
    )

    def key_info(start, count):
        return (start + jnp.arange(count), lax.dynamic_slice_in_dim(doc_all, start, count))

    piece = lax.all_gather(kv_pair, "ctx", axis=1, tiled=True)
    key_place, key_doc = key_info(jnp.int32(0), piece.shape[1])
    top, total, weighted = stats_step(
        start_stats, q_heads, d_out, piece, query_place, doc_ids, key_place, key_doc
    )
    finish_lse = top + jnp.log(total)
    finish_delta = weighted / total

    def cycle_turn(turn, carry):
        kv_now, grads, d_query = carry
        owner = (me - turn) % ncx
        key_place, key_doc = key_info(owner * tok, tok)
        d_query_part, d_pair = grad_step(
            q_heads,
            d_out,
            finish_lse,
            finish_delta,
            kv_now,
            query_place,
            doc_ids,
            key_place,
            key_doc,
        )
        kv_next = from_behind(kv_now, "ctx", 1)
        grads_next = passed_along((grads + d_pair).astype(jnp.bfloat16), "ctx", 1).astype(
            jnp.float32
        )
        return (kv_next, grads_next, d_query + d_query_part)

    start_cycle = (
        kv_pair,
        jnp.zeros((2, tok, width), jnp.float32),
        jnp.zeros((tok, width), jnp.float32),
    )
    _, grads, d_query = lax.fori_loop(0, ncx, cycle_turn, start_cycle)
    scale = 1.0 / math.sqrt(width)
    d_queries = (d_query * scale).astype(jnp.bfloat16)
    d_keys = (grads[0] * scale).astype(jnp.bfloat16)
    d_values = grads[1].astype(jnp.bfloat16)
    return (d_queries, d_keys, d_values, d_hidden, d_gates)


def solution(mesh):
    return jax.shard_map(
        per_device,
        mesh=mesh,
        in_specs=(
            P("ctx", "exp"),
            P("ctx", "exp"),
            P("ctx", "exp"),
            P("ctx"),
            P("exp", None),
            P(("ctx", "exp"), None),
            P(("ctx", "exp"), None),
            P(("ctx", "exp"), None, None),
            P(("ctx", "exp"), None, None),
            P("exp", None, None),
            P("exp", None, None),
            P("exp", None, None),
        ),
        out_specs=(
            P("ctx", "exp"),
            P("ctx", "exp"),
            P("ctx", "exp"),
            P(("ctx", "exp"), None),
            P(("ctx", "exp"), None, None),
        ),
        check_vma=False,
    )
```

profile of v0, /device:TPU:3, one launch (start us, length us, event | category | flops | bytes accessed | tf_op | source)
XLA Modules:
  0.0 460.3 jit_solution(10414109736766357753)
XLA Ops:
  10.6 7.6 %all-to-all-start = ((bf16[16,1,6]{2,1,0:T(2,128)(2,1)}), bf16[16,1,6]{2,1,0:T(2,128)(2,1)S(1)}, u32[]{:S(2)}, u32[]{:S(2)}) async-start(bf16[16,1,6]{2,1,0:T(2,128)(2,1)} %copy.26), calls=%async_computation | async-start | bytes 16384 | tf_op jit(solution)/shard_map/all_to_all | solution.py:94
  25.1 5.3 %all-to-all-start.2 = ((bf16[16,1,6,2048]{3,2,1,0:T(8,128)(2,1)}), bf16[16,1,6,2048]{3,2,1,0:T(8,128)(2,1)S(1)}, u32[]{:S(2)}, u32[]{:S(2)}) async-start(bf16[16,1,6,2048]{3,2,1,0:T(8,128)(2,1)} %bitcast.7), calls=%async_computation.2 | async-start | bytes 1048576 | tf_op jit(solution)/shard_map/all_to_all | solution.py:92
  31.3 16.5 %all-to-all-done.2 = bf16[16,1,6,2048]{3,2,1,0:T(8,128)(2,1)S(1)} async-done(((bf16[16,1,6,2048]{3,2,1,0:T(8,128)(2,1)}), bf16[16,1,6,2048]{3,2,1,0:T(8,128)(2,1)S(1)}, u32[]{:S(2)}, u32[]{:S(2)}) %all-to-all-start.2) | async-done | bytes 393248 | tf_op jit(solution)/shard_map/all_to_all | solution.py:92
  47.8 4.0 all-to-all-start.1
  52.1 16.9 %all-to-all-done.1 = bf16[16,1,6,2048]{3,2,1,0:T(8,128)(2,1)S(1)} async-done(((bf16[16,1,6,2048]{3,2,1,0:T(8,128)(2,1)}), bf16[16,1,6,2048]{3,2,1,0:T(8,128)(2,1)S(1)}, u32[]{:S(2)}, u32[]{:S(2)}) %all-to-all-start.1) | async-done | bytes 393248 | tf_op jit(solution)/shard_map/all_to_all | solution.py:93
  69.8 3.8 fusion.25
  73.7 3.8 fusion.29
  83.6 14.8 %all_to_all.20 = bf16[1,16,6,2048]{3,2,0,1:T(8,128)(2,1)S(1)} all-to-all(bf16[1,16,6,2048]{3,2,0,1:T(8,128)(2,1)S(1)} %bitcast.106), channel_id=1, replica_groups=mesh['ctx'=8,'exp'=16] {'exp'}, dimensions={1} | all-to-all | bytes 786432 | tf_op jit(solution)/shard_map/all_to_all | solution.py:112
  99.6 22.6 %all_gather.9 = s32[8192]{0:T(1024)S(1)} all-gather(s32[1024]{0:T(1024)S(1)} %copy-done.8), channel_id=1, replica_groups=mesh['ctx'=8,'exp'=16] {'ctx'}, dimensions={0}, use_global_device_ids=true | all-gather | bytes 36864 | tf_op jit(solution)/shard_map/all_gather | solution.py:127
  122.9 10.4 %all-to-all-start.4 = ((bf16[1,16,6]{2,0,1:T(2,128)(2,1)}), bf16[1,16,6]{2,0,1:T(2,128)(2,1)S(1)}, u32[]{:S(2)}, u32[]{:S(2)}) async-start(bf16[1,16,6]{2,0,1:T(2,128)(2,1)} %convert_element_type.121), calls=%async_computation.4 | async-start | bytes 16384 | tf_op jit(solution)/shard_map/all_to_all | solution.py:113
  133.4 7.0 %all-to-all-done.4 = bf16[1,16,6]{2,0,1:T(2,128)(2,1)S(1)} async-done(((bf16[1,16,6]{2,0,1:T(2,128)(2,1)}), bf16[1,16,6]{2,0,1:T(2,128)(2,1)S(1)}, u32[]{:S(2)}, u32[]{:S(2)}) %all-to-all-start.4) | async-done | bytes 224 | tf_op jit(solution)/shard_map/all_to_all | solution.py:113
  141.0 15.3 %fusion.18 = (f32[1024]{0:T(1024)S(1)}, f32[8192,1024]{1,0:T(8,128)}) fusion(s32[1024]{0:T(1024)S(1)} %copy-done.8, s32[1024]{0:T(1024)S(1)} %iota_add_fusion.2, s32[8192]{0:T(1024)S(1)} %all_gather.9, bf16[1024,128]{1,0:T(8,128)(2,1)S(1)} %copy-done.5, bf16[2,8192,128]{2,1,0:T(8,128)(2,1)} %all-gather.3.cloned.1.call-done), kind=kOutput, calls=%fused_computation.25 | convolution fusion | flops 2197814272 | bytes 35958784 | tf_op jit(solution)/shard_map/dot_general | solution.py:26
  156.3 15.7 %fusion.22 = f32[1024]{0:T(1024)S(1)} fusion(f32[8192,1024]{1,0:T(8,128)} %get-tuple-element.382, f32[1024]{0:T(1024)S(1)} %broadcast_maximum_fusion, s32[1024]{0:T(1024)S(1)} %copy-done.8, s32[1024]{0:T(1024)S(1)} %iota_add_fusion.2, s32[8192]{0:T(1024)S(1)} %all_gather.9), kind=kLoop, calls=%fused_computation.31 | loop fusion | flops 58719232 | bytes 33603584 | tf_op jit(solution)/shard_map/reduce_sum | solution.py:43
  172.1 4.3 convolution_convert_fusion
  176.4 17.2 %multiply_reduce_fusion = f32[1024]{0:T(1024)S(1)} fusion(f32[8192,1024]{1,0:T(8,128)} %get-tuple-element.382, bf16[1024,128]{1,0:T(8,128)(2,1)} %convolution_convert_fusion, f32[1024]{0:T(1024)S(1)} %broadcast_maximum_fusion, s32[1024]{0:T(1024)S(1)} %copy-done.8, s32[1024]{0:T(1024)S(1)} %iota_add_fusion.2, s32[8192]{0:T(1024)S(1)} %all_gather.9, ...), kind=kOutput, calls=%fused_computation.28 | convolution fusion | flops 2214591488 | bytes 35962880 | tf_op jit(solution)/shard_map/dot_general | solution.py:40
  193.7 254.3 %while.20 = (s32[]{:T(128)}, bf16[2,1024,128]{2,1,0:T(8,128)(2,1)S(1)}, f32[2,1024,128]{2,1,0:T(8,128)}, f32[1024,128]{1,0:T(8,128)}, s32[]{:T(128)}, /*index=5*...) while((s32[]{:T(128)}, ...), condition=%wide.region_4.6_spmd.clone, body=%wide.region_3.5_spmd.clone.sunk | while | flops 1360529408 | bytes 36499916 | solution.py:173
  207.3 10.7 %collective-permute-done.1 = bf16[2,1024,128]{2,1,0:T(8,128)(2,1)} collective-permute-done((bf16[2,1024,128]{2,1,0:T(8,128)(2,1)}, bf16[2,1024,128]{2,1,0:T(8,128)(2,1)}, u32[]{:S(2)}, u32[]{:S(2)}) %collective-permute-start.1) | collective-permute-done | bytes 524320 | tf_op jit(solution)/shard_map/while/body/eval_jaxpr/ppermute | solution.py:20
  220.1 9.0 %collective-permute-done = bf16[2,1024,128]{2,1,0:T(8,128)(2,1)S(1)} collective-permute-done((bf16[2,1024,128]{2,1,0:T(8,128)(2,1)S(1)}, bf16[2,1024,128]{2,1,0:T(8,128)(2,1)S(1)}, u32[]{:S(2)}, u32[]{:S(2)}) %collective-permute-start) | collective-permute-done | bytes 524320 | tf_op jit(solution)/shard_map/while/body/eval_jaxpr/ppermute | solution.py:14
  241.8 10.1 %collective-permute-done.1 = bf16[2,1024,128]{2,1,0:T(8,128)(2,1)} collective-permute-done((bf16[2,1024,128]{2,1,0:T(8,128)(2,1)}, bf16[2,1024,128]{2,1,0:T(8,128)(2,1)}, u32[]{:S(2)}, u32[]{:S(2)}) %collective-permute-start.1) | collective-permute-done | bytes 524320 | tf_op jit(solution)/shard_map/while/body/eval_jaxpr/ppermute | solution.py:20
  254.1 9.0 %collective-permute-done = bf16[2,1024,128]{2,1,0:T(8,128)(2,1)S(1)} collective-permute-done((bf16[2,1024,128]{2,1,0:T(8,128)(2,1)S(1)}, bf16[2,1024,128]{2,1,0:T(8,128)(2,1)S(1)}, u32[]{:S(2)}, u32[]{:S(2)}) %collective-permute-start) | collective-permute-done | bytes 524320 | tf_op jit(solution)/shard_map/while/body/eval_jaxpr/ppermute | solution.py:14
  275.8 9.2 %collective-permute-done.1 = bf16[2,1024,128]{2,1,0:T(8,128)(2,1)} collective-permute-done((bf16[2,1024,128]{2,1,0:T(8,128)(2,1)}, bf16[2,1024,128]{2,1,0:T(8,128)(2,1)}, u32[]{:S(2)}, u32[]{:S(2)}) %collective-permute-start.1) | collective-permute-done | bytes 524320 | tf_op jit(solution)/shard_map/while/body/eval_jaxpr/ppermute | solution.py:20
  287.2 9.0 %collective-permute-done = bf16[2,1024,128]{2,1,0:T(8,128)(2,1)S(1)} collective-permute-done((bf16[2,1024,128]{2,1,0:T(8,128)(2,1)S(1)}, bf16[2,1024,128]{2,1,0:T(8,128)(2,1)S(1)}, u32[]{:S(2)}, u32[]{:S(2)}) %collective-permute-start) | collective-permute-done | bytes 524320 | tf_op jit(solution)/shard_map/while/body/eval_jaxpr/ppermute | solution.py:14
  308.9 8.3 %collective-permute-done.1 = bf16[2,1024,128]{2,1,0:T(8,128)(2,1)} collective-permute-done((bf16[2,1024,128]{2,1,0:T(8,128)(2,1)}, bf16[2,1024,128]{2,1,0:T(8,128)(2,1)}, u32[]{:S(2)}, u32[]{:S(2)}) %collective-permute-start.1) | collective-permute-done | bytes 524320 | tf_op jit(solution)/shard_map/while/body/eval_jaxpr/ppermute | solution.py:20
  319.3 9.0 %collective-permute-done = bf16[2,1024,128]{2,1,0:T(8,128)(2,1)S(1)} collective-permute-done((bf16[2,1024,128]{2,1,0:T(8,128)(2,1)S(1)}, bf16[2,1024,128]{2,1,0:T(8,128)(2,1)S(1)}, u32[]{:S(2)}, u32[]{:S(2)}) %collective-permute-start) | collective-permute-done | bytes 524320 | tf_op jit(solution)/shard_map/while/body/eval_jaxpr/ppermute | solution.py:14
  341.1 7.4 %collective-permute-done.1 = bf16[2,1024,128]{2,1,0:T(8,128)(2,1)} collective-permute-done((bf16[2,1024,128]{2,1,0:T(8,128)(2,1)}, bf16[2,1024,128]{2,1,0:T(8,128)(2,1)}, u32[]{:S(2)}, u32[]{:S(2)}) %collective-permute-start.1) | collective-permute-done | bytes 524320 | tf_op jit(solution)/shard_map/while/body/eval_jaxpr/ppermute | solution.py:20
  350.5 9.0 %collective-permute-done = bf16[2,1024,128]{2,1,0:T(8,128)(2,1)S(1)} collective-permute-done((bf16[2,1024,128]{2,1,0:T(8,128)(2,1)S(1)}, bf16[2,1024,128]{2,1,0:T(8,128)(2,1)S(1)}, u32[]{:S(2)}, u32[]{:S(2)}) %collective-permute-start) | collective-permute-done | bytes 524320 | tf_op jit(solution)/shard_map/while/body/eval_jaxpr/ppermute | solution.py:14
  372.3 6.5 %collective-permute-done.1 = bf16[2,1024,128]{2,1,0:T(8,128)(2,1)} collective-permute-done((bf16[2,1024,128]{2,1,0:T(8,128)(2,1)}, bf16[2,1024,128]{2,1,0:T(8,128)(2,1)}, u32[]{:S(2)}, u32[]{:S(2)}) %collective-permute-start.1) | collective-permute-done | bytes 524320 | tf_op jit(solution)/shard_map/while/body/eval_jaxpr/ppermute | solution.py:20
  380.8 9.0 %collective-permute-done = bf16[2,1024,128]{2,1,0:T(8,128)(2,1)S(1)} collective-permute-done((bf16[2,1024,128]{2,1,0:T(8,128)(2,1)S(1)}, bf16[2,1024,128]{2,1,0:T(8,128)(2,1)S(1)}, u32[]{:S(2)}, u32[]{:S(2)}) %collective-permute-start) | collective-permute-done | bytes 524320 | tf_op jit(solution)/shard_map/while/body/eval_jaxpr/ppermute | solution.py:14
  402.6 6.0 %collective-permute-done.1 = bf16[2,1024,128]{2,1,0:T(8,128)(2,1)} collective-permute-done((bf16[2,1024,128]{2,1,0:T(8,128)(2,1)}, bf16[2,1024,128]{2,1,0:T(8,128)(2,1)}, u32[]{:S(2)}, u32[]{:S(2)}) %collective-permute-start.1) | collective-permute-done | bytes 524320 | tf_op jit(solution)/shard_map/while/body/eval_jaxpr/ppermute | solution.py:20
  410.7 8.7 %collective-permute-done = bf16[2,1024,128]{2,1,0:T(8,128)(2,1)S(1)} collective-permute-done((bf16[2,1024,128]{2,1,0:T(8,128)(2,1)S(1)}, bf16[2,1024,128]{2,1,0:T(8,128)(2,1)S(1)}, u32[]{:S(2)}, u32[]{:S(2)}) %collective-permute-start) | collective-permute-done | bytes 524320 | tf_op jit(solution)/shard_map/while/body/eval_jaxpr/ppermute | solution.py:14
  432.1 6.0 %collective-permute-done.1 = bf16[2,1024,128]{2,1,0:T(8,128)(2,1)} collective-permute-done((bf16[2,1024,128]{2,1,0:T(8,128)(2,1)}, bf16[2,1024,128]{2,1,0:T(8,128)(2,1)}, u32[]{:S(2)}, u32[]{:S(2)}) %collective-permute-start.1) | collective-permute-done | bytes 524320 | tf_op jit(solution)/shard_map/while/body/eval_jaxpr/ppermute | solution.py:20
  440.1 7.9 %collective-permute-done = bf16[2,1024,128]{2,1,0:T(8,128)(2,1)S(1)} collective-permute-done((bf16[2,1024,128]{2,1,0:T(8,128)(2,1)S(1)}, bf16[2,1024,128]{2,1,0:T(8,128)(2,1)S(1)}, u32[]{:S(2)}, u32[]{:S(2)}) %collective-permute-start) | collective-permute-done | bytes 524320 | tf_op jit(solution)/shard_map/while/body/eval_jaxpr/ppermute | solution.py:14
  (192 shorter events, 144.9 us)
Async XLA Ops:
  7.2 164.9 %copy-start = (bf16[128,2048]{1,0:T(8,128)(2,1)S(1)}, bf16[128,2048]{1,0:T(8,128)(2,1)}, u32[]{:S(2)}) copy-start(bf16[128,2048]{1,0:T(8,128)(2,1)} %param.20) | copy-start | bytes 1572868
  7.2 14.1 %copy-start.3 = (bf16[64,2048]{1,0:T(8,128)(2,1)S(1)}, bf16[64,2048]{1,0:T(8,128)(2,1)}, u32[]{:S(2)}) copy-start(bf16[64,2048]{1,0:T(8,128)(2,1)} %param.21) | copy-start | bytes 786436
  7.2 133.8 %all-gather.3.cloned.1.call-start = ((), (), s32[]{:S(2)}) async-start(), calls=%async_computation.5 | async-start | bytes 4718592 | tf_op jit(solution)/shard_map/all_gather | solution.py:139
  10.6 14.5 %all-to-all-start = ((bf16[16,1,6]{2,1,0:T(2,128)(2,1)}), bf16[16,1,6]{2,1,0:T(2,128)(2,1)S(1)}, u32[]{:S(2)}, u32[]{:S(2)}) async-start(bf16[16,1,6]{2,1,0:T(2,128)(2,1)} %copy.26), calls=%async_computation | async-start | bytes 16384 | tf_op jit(solution)/shard_map/all_to_all | solution.py:94
  25.1 22.7 %all-to-all-start.2 = ((bf16[16,1,6,2048]{3,2,1,0:T(8,128)(2,1)}), bf16[16,1,6,2048]{3,2,1,0:T(8,128)(2,1)S(1)}, u32[]{:S(2)}, u32[]{:S(2)}) async-start(bf16[16,1,6,2048]{3,2,1,0:T(8,128)(2,1)} %bitcast.7), calls=%async_computation.2 | async-start | bytes 1048576 | tf_op jit(solution)/shard_map/all_to_all | solution.py:92
  47.8 21.1 %all-to-all-start.1 = ((bf16[16,1,6,2048]{3,2,1,0:T(8,128)(2,1)}), bf16[16,1,6,2048]{3,2,1,0:T(8,128)(2,1)S(1)}, u32[]{:S(2)}, u32[]{:S(2)}) async-start(bf16[16,1,6,2048]{3,2,1,0:T(8,128)(2,1)} %bitcast.5), calls=%async_computation.1 | async-start | bytes 1048576 | tf_op jit(solution)/shard_map/all_to_all | solution.py:93
  51.8 120.3 %all-gather.5.cloned.1.call-start = ((), (), s32[]{:S(2)}) async-start(), calls=%async_computation.6 | async-start | bytes 4456448 | tf_op jit(solution)/shard_map/all_gather | solution.py:122
  68.9 8.6 %slice-start.4 = ((s8[5767168]{0:T(1024)(128)(4,1)}), s8[1572864]{0:T(1024)(128)(4,1)S(1)}, s32[]{:S(2)}) async-start(s8[5767168]{0:T(1024)(128)(4,1)} %bitcast.104), calls=%async_computation.11 | async-start | bytes 3145728
  69.8 7.7 %slice-start.5 = ((s8[5767168]{0:T(1024)(128)(4,1)}), s8[4194304]{0:T(1024)(128)(4,1)S(1)}, s32[]{:S(2)}) async-start(s8[5767168]{0:T(1024)(128)(4,1)} %bitcast.104), calls=%async_computation.12 | async-start | bytes 8388608
  69.8 7.7 %copy-start.7 = (bf16[96,2048]{1,0:T(8,128)(2,1)S(1)}, bf16[96,2048]{1,0:T(8,128)(2,1)}, u32[]{:S(2)}) copy-start(bf16[96,2048]{1,0:T(8,128)(2,1)} %reshape.157) | copy-start | bytes 1179652
  73.7 5.9 %slice-start = ((s8[5767168]{0:T(1024)(128)(4,1)}), s8[4194304]{0:T(1024)(128)(4,1)S(1)}, s32[]{:S(2)}) async-start(s8[5767168]{0:T(1024)(128)(4,1)} %bitcast.100), calls=%async_computation.7 | async-start | bytes 8388608
  81.5 17.0 %copy-start.2 = (bf16[64,2048]{1,0:T(8,128)(2,1)S(1)}, bf16[64,2048]{1,0:T(8,128)(2,1)}, u32[]{:S(2)}) copy-start(bf16[64,2048]{1,0:T(8,128)(2,1)} %param.22) | copy-start | bytes 786436
  81.5 18.1 %copy-start.8 = (s32[1024]{0:T(1024)S(1)}, s32[1024]{0:T(1024)}, u32[]{:S(2)}) copy-start(s32[1024]{0:T(1024)} %param.19) | copy-start | bytes 12292
  81.6 59.5 %copy-start.5 = (bf16[1024,128]{1,0:T(8,128)(2,1)S(1)}, bf16[1024,128]{1,0:T(8,128)(2,1)}, u32[]{:S(2)}) copy-start(bf16[1024,128]{1,0:T(8,128)(2,1)} %param.16) | copy-start | bytes 786436
  122.9 17.4 %all-to-all-start.4 = ((bf16[1,16,6]{2,0,1:T(2,128)(2,1)}), bf16[1,16,6]{2,0,1:T(2,128)(2,1)S(1)}, u32[]{:S(2)}, u32[]{:S(2)}) async-start(bf16[1,16,6]{2,0,1:T(2,128)(2,1)} %convert_element_type.121), calls=%async_computation.4 | async-start | bytes 16384 | tf_op jit(solution)/shard_map/all_to_all | solution.py:113
  176.4 17.2 %copy-start.6 = (bf16[2,1024,128]{2,1,0:T(8,128)(2,1)S(1)}, bf16[2,1024,128]{2,1,0:T(8,128)(2,1)}, u32[]{:S(2)}) copy-start(bf16[2,1024,128]{2,1,0:T(8,128)(2,1)} %pad_maximum_fusion) | copy-start | bytes 1572868
  202.2 15.8 %collective-permute-start.1 = (bf16[2,1024,128]{2,1,0:T(8,128)(2,1)}, bf16[2,1024,128]{2,1,0:T(8,128)(2,1)}, u32[]{:S(2)}, u32[]{:S(2)}) collective-permute-start(bf16[2,1024,128]{2,1,0:T(8,128)(2,1)} %fusion.91), channel_id=1, source_target_pairs={{112,0},{0,16},{16,32},{32,48},{48,64},{64,80},{80,96},{96,112},{1... | collective-permute-start | bytes 1572872 | tf_op jit(solution)/shard_map/while/body/eval_jaxpr/ppermute | solution.py:20
  203.9 25.2 %collective-permute-start = (bf16[2,1024,128]{2,1,0:T(8,128)(2,1)S(1)}, bf16[2,1024,128]{2,1,0:T(8,128)(2,1)S(1)}, u32[]{:S(2)}, u32[]{:S(2)}) collective-permute-start(bf16[2,1024,128]{2,1,0:T(8,128)(2,1)S(1)} %copy.39), channel_id=1, source_target_pairs={{0,16},{16,32},{32,48},{48,64},{64,80},{80,96},{96,112},{1,17},{17... | collective-permute-start | bytes 1572872 | tf_op jit(solution)/shard_map/while/body/eval_jaxpr/ppermute | solution.py:14
  237.4 14.6 %collective-permute-start.1 = (bf16[2,1024,128]{2,1,0:T(8,128)(2,1)}, bf16[2,1024,128]{2,1,0:T(8,128)(2,1)}, u32[]{:S(2)}, u32[]{:S(2)}) collective-permute-start(bf16[2,1024,128]{2,1,0:T(8,128)(2,1)} %fusion.91), channel_id=1, source_target_pairs={{112,0},{0,16},{16,32},{32,48},{48,64},{64,80},{80,96},{96,112},{1... | collective-permute-start | bytes 1572872 | tf_op jit(solution)/shard_map/while/body/eval_jaxpr/ppermute | solution.py:20
  237.4 25.8 %collective-permute-start = (bf16[2,1024,128]{2,1,0:T(8,128)(2,1)S(1)}, bf16[2,1024,128]{2,1,0:T(8,128)(2,1)S(1)}, u32[]{:S(2)}, u32[]{:S(2)}) collective-permute-start(bf16[2,1024,128]{2,1,0:T(8,128)(2,1)S(1)} %copy.39), channel_id=1, source_target_pairs={{0,16},{16,32},{32,48},{48,64},{64,80},{80,96},{96,112},{1,17},{17... | collective-permute-start | bytes 1572872 | tf_op jit(solution)/shard_map/while/body/eval_jaxpr/ppermute | solution.py:14
  271.4 13.7 %collective-permute-start.1 = (bf16[2,1024,128]{2,1,0:T(8,128)(2,1)}, bf16[2,1024,128]{2,1,0:T(8,128)(2,1)}, u32[]{:S(2)}, u32[]{:S(2)}) collective-permute-start(bf16[2,1024,128]{2,1,0:T(8,128)(2,1)} %fusion.91), channel_id=1, source_target_pairs={{112,0},{0,16},{16,32},{32,48},{48,64},{64,80},{80,96},{96,112},{1... | collective-permute-start | bytes 1572872 | tf_op jit(solution)/shard_map/while/body/eval_jaxpr/ppermute | solution.py:20
  271.4 24.8 %collective-permute-start = (bf16[2,1024,128]{2,1,0:T(8,128)(2,1)S(1)}, bf16[2,1024,128]{2,1,0:T(8,128)(2,1)S(1)}, u32[]{:S(2)}, u32[]{:S(2)}) collective-permute-start(bf16[2,1024,128]{2,1,0:T(8,128)(2,1)S(1)} %copy.39), channel_id=1, source_target_pairs={{0,16},{16,32},{32,48},{48,64},{64,80},{80,96},{96,112},{1,17},{17... | collective-permute-start | bytes 1572872 | tf_op jit(solution)/shard_map/while/body/eval_jaxpr/ppermute | solution.py:14
  304.4 12.8 %collective-permute-start.1 = (bf16[2,1024,128]{2,1,0:T(8,128)(2,1)}, bf16[2,1024,128]{2,1,0:T(8,128)(2,1)}, u32[]{:S(2)}, u32[]{:S(2)}) collective-permute-start(bf16[2,1024,128]{2,1,0:T(8,128)(2,1)} %fusion.91), channel_id=1, source_target_pairs={{112,0},{0,16},{16,32},{32,48},{48,64},{64,80},{80,96},{96,112},{1... | collective-permute-start | bytes 1572872 | tf_op jit(solution)/shard_map/while/body/eval_jaxpr/ppermute | solution.py:20
  304.4 23.9 %collective-permute-start = (bf16[2,1024,128]{2,1,0:T(8,128)(2,1)S(1)}, bf16[2,1024,128]{2,1,0:T(8,128)(2,1)S(1)}, u32[]{:S(2)}, u32[]{:S(2)}) collective-permute-start(bf16[2,1024,128]{2,1,0:T(8,128)(2,1)S(1)} %copy.39), channel_id=1, source_target_pairs={{0,16},{16,32},{32,48},{48,64},{64,80},{80,96},{96,112},{1,17},{17... | collective-permute-start | bytes 1572872 | tf_op jit(solution)/shard_map/while/body/eval_jaxpr/ppermute | solution.py:14
  336.6 11.9 %collective-permute-start.1 = (bf16[2,1024,128]{2,1,0:T(8,128)(2,1)}, bf16[2,1024,128]{2,1,0:T(8,128)(2,1)}, u32[]{:S(2)}, u32[]{:S(2)}) collective-permute-start(bf16[2,1024,128]{2,1,0:T(8,128)(2,1)} %fusion.91), channel_id=1, source_target_pairs={{112,0},{0,16},{16,32},{32,48},{48,64},{64,80},{80,96},{96,112},{1... | collective-permute-start | bytes 1572872 | tf_op jit(solution)/shard_map/while/body/eval_jaxpr/ppermute | solution.py:20
  336.6 23.0 %collective-permute-start = (bf16[2,1024,128]{2,1,0:T(8,128)(2,1)S(1)}, bf16[2,1024,128]{2,1,0:T(8,128)(2,1)S(1)}, u32[]{:S(2)}, u32[]{:S(2)}) collective-permute-start(bf16[2,1024,128]{2,1,0:T(8,128)(2,1)S(1)} %copy.39), channel_id=1, source_target_pairs={{0,16},{16,32},{32,48},{48,64},{64,80},{80,96},{96,112},{1,17},{17... | collective-permute-start | bytes 1572872 | tf_op jit(solution)/shard_map/while/body/eval_jaxpr/ppermute | solution.py:14
  367.8 10.9 %collective-permute-start.1 = (bf16[2,1024,128]{2,1,0:T(8,128)(2,1)}, bf16[2,1024,128]{2,1,0:T(8,128)(2,1)}, u32[]{:S(2)}, u32[]{:S(2)}) collective-permute-start(bf16[2,1024,128]{2,1,0:T(8,128)(2,1)} %fusion.91), channel_id=1, source_target_pairs={{112,0},{0,16},{16,32},{32,48},{48,64},{64,80},{80,96},{96,112},{1... | collective-permute-start | bytes 1572872 | tf_op jit(solution)/shard_map/while/body/eval_jaxpr/ppermute | solution.py:20
  367.8 22.1 %collective-permute-start = (bf16[2,1024,128]{2,1,0:T(8,128)(2,1)S(1)}, bf16[2,1024,128]{2,1,0:T(8,128)(2,1)S(1)}, u32[]{:S(2)}, u32[]{:S(2)}) collective-permute-start(bf16[2,1024,128]{2,1,0:T(8,128)(2,1)S(1)} %copy.39), channel_id=1, source_target_pairs={{0,16},{16,32},{32,48},{48,64},{64,80},{80,96},{96,112},{1,17},{17... | collective-permute-start | bytes 1572872 | tf_op jit(solution)/shard_map/while/body/eval_jaxpr/ppermute | solution.py:14
  398.1 10.5 %collective-permute-start.1 = (bf16[2,1024,128]{2,1,0:T(8,128)(2,1)}, bf16[2,1024,128]{2,1,0:T(8,128)(2,1)}, u32[]{:S(2)}, u32[]{:S(2)}) collective-permute-start(bf16[2,1024,128]{2,1,0:T(8,128)(2,1)} %fusion.91), channel_id=1, source_target_pairs={{112,0},{0,16},{16,32},{32,48},{48,64},{64,80},{80,96},{96,112},{1... | collective-permute-start | bytes 1572872 | tf_op jit(solution)/shard_map/while/body/eval_jaxpr/ppermute | solution.py:20
  398.1 21.2 %collective-permute-start = (bf16[2,1024,128]{2,1,0:T(8,128)(2,1)S(1)}, bf16[2,1024,128]{2,1,0:T(8,128)(2,1)S(1)}, u32[]{:S(2)}, u32[]{:S(2)}) collective-permute-start(bf16[2,1024,128]{2,1,0:T(8,128)(2,1)S(1)} %copy.39), channel_id=1, source_target_pairs={{0,16},{16,32},{32,48},{48,64},{64,80},{80,96},{96,112},{1,17},{17... | collective-permute-start | bytes 1572872 | tf_op jit(solution)/shard_map/while/body/eval_jaxpr/ppermute | solution.py:14
  427.6 10.5 %collective-permute-start.1 = (bf16[2,1024,128]{2,1,0:T(8,128)(2,1)}, bf16[2,1024,128]{2,1,0:T(8,128)(2,1)}, u32[]{:S(2)}, u32[]{:S(2)}) collective-permute-start(bf16[2,1024,128]{2,1,0:T(8,128)(2,1)} %fusion.91), channel_id=1, source_target_pairs={{112,0},{0,16},{16,32},{32,48},{48,64},{64,80},{80,96},{96,112},{1... | collective-permute-start | bytes 1572872 | tf_op jit(solution)/shard_map/while/body/eval_jaxpr/ppermute | solution.py:20
  427.6 20.4 %collective-permute-start = (bf16[2,1024,128]{2,1,0:T(8,128)(2,1)S(1)}, bf16[2,1024,128]{2,1,0:T(8,128)(2,1)S(1)}, u32[]{:S(2)}, u32[]{:S(2)}) collective-permute-start(bf16[2,1024,128]{2,1,0:T(8,128)(2,1)S(1)} %copy.39), channel_id=1, source_target_pairs={{0,16},{16,32},{32,48},{48,64},{64,80},{80,96},{96,112},{1,17},{17... | collective-permute-start | bytes 1572872 | tf_op jit(solution)/shard_map/while/body/eval_jaxpr/ppermute | solution.py:14
  (13 other events, 47.9 us)
Sparse Core Ops, SparseCore 0:
  9.7 65.2 all-gather.2
  99.7 54.2 all-gather.4
where the time goes:
time: 469 us; the launch traced here: 460 us
  waiting for transfers between devices  177 us (38%)
  matrix products  128 us (27%)
  other arithmetic  45.9 us (10%)
  starting transfers between devices  44.4 us (9%)
  blocking collectives  37.3 us (8%)
  between operations  14.4 us (3%)
  local copies, waits for them, and re-layouts  12.1 us (3%)
    ppermute x8, waiting for transfers between devices, from_behind(): return lax.ppermute(value, axis, pairs)  70.8 us
    ppermute x8, waiting for transfers between devices, passed_along(): return lax.ppermute(block, axis, route)  64.2 us
    dot_general x8, matrix products, grad_step(): lax.dot_general(d_out, piece[1], (((1,), (1,)), ((), ())), preferred_elem...  24.2 us
    all_gather x1, blocking collectives, per_device(): doc_all = lax.all_gather(doc_ids, 'ctx', axis=0, tiled=True)  22.6 us
    dot_general x8, matrix products, grad_step(): lax.dot_general(probs_low, d_out, (((0,), (0,)), ((), ())), preferred_ele...  21.6 us
    dot_general x9, matrix products, score_block(): lax.dot_general(queries, keys, (((1,), (1,)), ((), ())), preferred_elemen...  20.9 us
    dot_general x8, matrix products, grad_step(): jnp.dot(d_scores, piece[0], preferred_element_type=jnp.float32)  19.4 us
    dot_general x1, matrix products, stats_step(): lax.dot_general(d_out, piece[1], (((1,), (1,)), ((), ())), preferred_elem...  17.2 us
  transfers between devices with their start and end apart: 22, of which 20 were waited for; matrix products, arithmetic and copies ran while one was open for 20% of the time, Pallas kernels for 0%

commit v1 on v0

v1 whole, which is shorter than its diff:
```python
import math

import jax
import jax.numpy as jnp
from jax import lax
from jax.experimental import pallas as pl
from jax.experimental.pallas import tpu as pltpu
from jax.sharding import PartitionSpec as P

NEG = -1e30
SCALE = 1.0 / math.sqrt(128)
KT = 512
QT = 256


def doc_start(place, scal):
    start = jnp.zeros_like(place)
    for d in range(1, 4):
        start = jnp.maximum(start, jnp.where(scal[d] <= place, scal[d], 0))
    return start


def doc_end(place, scal, tokens):
    end = jnp.full_like(place, tokens)
    for d in range(1, 4):
        end = jnp.minimum(end, jnp.where(scal[d] > place, scal[d], tokens))
    return end


def nt(a, b):
    return lax.dot_general(a, b, (((1,), (1,)), ((), ())), preferred_element_type=jnp.float32)


def fold(x, op):
    parts = [x[:, i * 128:(i + 1) * 128] for i in range(x.shape[1] // 128)]
    while len(parts) > 1:
        parts = [op(parts[i], parts[i + 1]) for i in range(0, len(parts), 2)]
    return parts[0]


def query_kernel(scal, qkv, d_out, dq_out, stats, s_buf, dp_buf):
    tok = d_out.shape[0]
    per = tok // KT
    me = scal[0]

    def one(qi, _):
        rows = pl.ds(pl.multiple_of(qi * QT, QT), QT)
        row0 = me * tok + qi * QT
        first = doc_start(row0, scal) // KT
        last = (row0 + QT - 1) // KT
        count = last - first + 1
        q = qkv[me, 0, rows, :]
        do = d_out[rows, :]
        place = row0 + lax.broadcasted_iota(jnp.int32, (QT, KT), 0)
        start = doc_start(place, scal)
        lane = lax.broadcasted_iota(jnp.int32, (QT, KT), 1)

        def tile(t, which):
            at = first + t
            return qkv[at // per, which, pl.ds(pl.multiple_of((at % per) * KT, KT), KT), :]

        def scores(t, top):
            s = nt(q, tile(t, 1)) * SCALE
            key = (first + t) * KT + lane
            s = jnp.where((key >= start) & (key <= place), s, NEG)
            s_buf[t] = s
            return jnp.maximum(top, fold(s, jnp.maximum))

        top = lax.fori_loop(0, count, scores, jnp.full((QT, 128), NEG, jnp.float32))
        top = jnp.max(top, axis=1, keepdims=True)

        def probs(t, carry):
            total, weighted = carry
            p = jnp.exp(s_buf[t] - top)
            dp = nt(do, tile(t, 2))
            s_buf[t] = p
            dp_buf[t] = dp
            return total + fold(p, jnp.add), weighted + fold(p * dp, jnp.add)

        zero = jnp.zeros((QT, 128), jnp.float32)
        total, weighted = lax.fori_loop(0, count, probs, (zero, zero))
        total = jnp.sum(total, axis=1, keepdims=True)
        inv = 1.0 / total
        delta = jnp.sum(weighted, axis=1, keepdims=True) * inv
        lse = top + jnp.log(total)

        def grads(t, dq):
            ds = (s_buf[t] * inv) * (dp_buf[t] - delta)
            return dq + jnp.dot(ds.astype(jnp.bfloat16), tile(t, 1), preferred_element_type=jnp.float32)

        dq = lax.fori_loop(0, count, grads, zero)
        dq_out[rows, :] = (dq * SCALE).astype(jnp.bfloat16)
        stats[0:1, rows] = jnp.transpose(jnp.broadcast_to(lse, (QT, 128)))[0:1, :]
        stats[1:2, rows] = jnp.transpose(jnp.broadcast_to(delta, (QT, 128)))[0:1, :]
        return 0

    lax.fori_loop(0, tok // QT, one, 0)


def key_kernel(scal, qkv, d_out, stats, dk_out, dv_out):
    tok = dk_out.shape[0]
    per = tok // KT
    me = scal[0]
    tokens = tok * qkv.shape[0]

    def one(ki, _):
        rows = pl.ds(pl.multiple_of(ki * QT, QT), QT)
        row0 = me * tok + ki * QT
        first = row0 // KT
        last = (doc_end(row0 + QT - 1, scal, tokens) - 1) // KT
        k = qkv[me, 1, rows, :]
        v = qkv[me, 2, rows, :]
        key = row0 + lax.broadcasted_iota(jnp.int32, (QT, KT), 0)
        lane = lax.broadcasted_iota(jnp.int32, (1, KT), 1)

        def step(at, carry):
            dk, dv = carry
            block = at // per
            cols = pl.ds(pl.multiple_of((at % per) * KT, KT), KT)
            q = qkv[block, 0, cols, :]
            do = d_out[block, cols, :]
            place = at * KT + lane
            start = doc_start(place, scal)
            allowed = (key >= start) & (key <= place)
            s = nt(k, q) * SCALE
            p = jnp.where(allowed, jnp.exp(s - stats[block, 0:1, cols]), 0.0)
            dp = nt(v, do)
            dv = dv + jnp.dot(p.astype(jnp.bfloat16), do, preferred_element_type=jnp.float32)
            ds = (p * (dp - stats[block, 1:2, cols])).astype(jnp.bfloat16)
            dk = dk + jnp.dot(ds, q, preferred_element_type=jnp.float32)
            return dk, dv

        zero = jnp.zeros((QT, 128), jnp.float32)
        dk, dv = lax.fori_loop(first, last + 1, step, (zero, zero))
        dk_out[rows, :] = (dk * SCALE).astype(jnp.bfloat16)
        dv_out[rows, :] = dv.astype(jnp.bfloat16)
        return 0

    lax.fori_loop(0, tok // QT, one, 0)


def attention(q_heads, k_heads, v_heads, doc_ids, d_out):
    tok, width = q_heads.shape
    ncx = lax.axis_size("ctx")
    me = lax.axis_index("ctx")
    qkv = lax.all_gather(jnp.stack([q_heads, k_heads, v_heads]), "ctx", axis=0)
    doc_all = lax.all_gather(doc_ids, "ctx", axis=0, tiled=True)
    starts = jnp.sum((doc_all[None, :] < jnp.arange(1, 4)[:, None]).astype(jnp.int32), axis=1)
    scal = jnp.concatenate([me[None].astype(jnp.int32), starts])
    d_out_all = lax.all_gather(d_out, "ctx", axis=0)
    vmem = pl.BlockSpec(memory_space=pltpu.VMEM)
    smem = pl.BlockSpec(memory_space=pltpu.SMEM)
    params = pltpu.CompilerParams(vmem_limit_bytes=48 * 2**20)
    low = jax.ShapeDtypeStruct((tok, width), jnp.bfloat16)
    pairs = 3 * tok * tok * 2 * width
    cost = pl.CostEstimate(flops=4 * pairs, bytes_accessed=8 * 2**20, transcendentals=3 * tok * tok)
    d_queries, stats = pl.pallas_call(
        query_kernel,
        out_shape=(low, jax.ShapeDtypeStruct((2, tok), jnp.float32)),
        in_specs=[smem, vmem, vmem],
        out_specs=(vmem, vmem),
        scratch_shapes=[pltpu.VMEM((9, QT, KT), jnp.float32), pltpu.VMEM((9, QT, KT), jnp.float32)],
        compiler_params=params,
        cost_estimate=cost,
        name="query_grads",
    )(scal, qkv, d_out)
    stats_all = lax.all_gather(stats, "ctx", axis=0)
    d_keys, d_values = pl.pallas_call(
        key_kernel,
        out_shape=(low, low),
        in_specs=[smem, vmem, vmem, vmem],
        out_specs=(vmem, vmem),
        compiler_params=params,
        cost_estimate=cost,
        name="key_grads",
    )(scal, qkv, d_out_all, stats_all)
    return d_queries, d_keys, d_values


def per_device(
    q_heads,
    k_heads,
    v_heads,
    doc_ids,
    w_out,
    hidden_rows,
    out_grad,
    picks,
    gates,
    w_gate,
    w_up,
    w_down,
):
    rows = hidden_rows.shape[0]
    model = hidden_rows.shape[1]
    experts = picks.shape[1]
    slots = picks.shape[2]
    index = picks[0].reshape(-1)
    chosen_h = jnp.take(hidden_rows, index, axis=0).reshape(experts, 1, slots, model)
    chosen_g = jnp.take(out_grad, index, axis=0).reshape(experts, 1, slots, model)
    chosen_w = gates.reshape(experts, 1, slots)
    xs = lax.all_to_all(chosen_h, "exp", split_axis=0, concat_axis=1, tiled=True)
    gs = lax.all_to_all(chosen_g, "exp", split_axis=0, concat_axis=1, tiled=True)
    ws = lax.all_to_all(chosen_w, "exp", split_axis=0, concat_axis=1, tiled=True)
    local = xs.shape[0]
    x_rows = xs.reshape(local, -1, model)
    g_rows = gs.reshape(local, -1, model)
    weight = ws.reshape(local, -1).astype(jnp.float32)
    a = jnp.einsum("erd,edf->erf", x_rows, w_gate, preferred_element_type=jnp.float32)
    b = jnp.einsum("erd,edf->erf", x_rows, w_up, preferred_element_type=jnp.float32)
    u = jnp.einsum("erd,efd->erf", g_rows, w_down, preferred_element_type=jnp.float32)
    sig = jax.nn.sigmoid(a)
    act_gate = a * sig
    d_gate = jnp.sum(act_gate * b * u, axis=2).astype(jnp.bfloat16)
    d_act = weight[..., None] * u
    da = (d_act * b * sig * (1.0 + a * (1.0 - sig))).astype(jnp.bfloat16)
    db = (d_act * act_gate).astype(jnp.bfloat16)
    d_x = jnp.einsum("erf,edf->erd", da, w_gate, preferred_element_type=jnp.float32)
    d_x = d_x + jnp.einsum("erf,edf->erd", db, w_up, preferred_element_type=jnp.float32)
    d_x = d_x.astype(jnp.bfloat16).reshape(xs.shape)
    d_gate = d_gate.reshape(ws.shape)
    back_rows = lax.all_to_all(d_x, "exp", split_axis=1, concat_axis=0, tiled=True)
    back_gates = lax.all_to_all(d_gate, "exp", split_axis=1, concat_axis=0, tiled=True)
    flat_rows = back_rows.reshape(experts * slots, model)
    one_hot = (index[:, None] == jnp.arange(rows)[None, :]).astype(jnp.bfloat16)
    summed = lax.dot_general(
        one_hot, flat_rows, (((0,), (0,)), ((), ())), preferred_element_type=jnp.float32
    )
    d_hidden = (out_grad.astype(jnp.float32) + summed).astype(jnp.bfloat16)
    d_gates = back_gates.reshape(1, experts, slots)
    d_out = lax.dot_general(
        lax.all_gather(d_hidden, "exp", axis=0, tiled=True),
        w_out,
        (((1,), (1,)), ((), ())),
        preferred_element_type=jnp.float32,
    ).astype(jnp.bfloat16)
    d_queries, d_keys, d_values = attention(q_heads, k_heads, v_heads, doc_ids, d_out)
    return (d_queries, d_keys, d_values, d_hidden, d_gates)


def solution(mesh):
    return jax.shard_map(
        per_device,
        mesh=mesh,
        in_specs=(
            P("ctx", "exp"),
            P("ctx", "exp"),
            P("ctx", "exp"),
            P("ctx"),
            P("exp", None),
            P(("ctx", "exp"), None),
            P(("ctx", "exp"), None),
            P(("ctx", "exp"), None, None),
            P(("ctx", "exp"), None, None),
            P("exp", None, None),
            P("exp", None, None),
            P("exp", None, None),
        ),
        out_specs=(
            P("ctx", "exp"),
            P("ctx", "exp"),
            P("ctx", "exp"),
            P(("ctx", "exp"), None),
            P(("ctx", "exp"), None, None),
        ),
        check_vma=False,
    )
```

time: 469 us -> 292 us (0.62)
  the two profiles are of different devices: /device:TPU:3 before, /device:TPU:0 now
where the time goes in v1:
time: 292 us; the launch traced here: 291 us
  waiting for transfers between devices  102 us (35%)
  blocking collectives  83.6 us (29%)
  Pallas kernels  30.2 us (10%)
  starting transfers between devices  22.2 us (8%)
  matrix products  21.6 us (7%)
  local copies, waits for them, and re-layouts  15.7 us (5%)
  between operations  14 us (5%)
    all_gather x1, waiting for transfers between devices, per_device(): lax.all_gather(d_hidden, 'exp', axis=0, tiled=True)  51.7 us
    all_gather x1, blocking collectives, attention(): stats_all = lax.all_gather(stats, 'ctx', axis=0)  40 us
    all_gather x1, blocking collectives, attention(): doc_all = lax.all_gather(doc_ids, 'ctx', axis=0, tiled=True)  28.1 us
    all_gather x1, waiting for transfers between devices, attention(): qkv = lax.all_gather(jnp.stack([q_heads, k_heads, v_heads]), 'ctx', axis=0)  26.9 us
    pallas_call x1, Pallas kernels, attention(): pl.pallas_call(key_kernel, out_shape=(low, low), in_specs=[smem, vmem, vm...  20.4 us
    all_to_all x1, blocking collectives, per_device(): lax.all_to_all(d_x, 'exp', split_axis=1, concat_axis=0, tiled=True)  15.6 us
    all_to_all x1, waiting for transfers between devices, per_device(): lax.all_to_all(chosen_h, 'exp', split_axis=0, concat_axis=1, tiled=True)  11.3 us
    pallas_call x1, Pallas kernels, attention(): pl.pallas_call(query_kernel, out_shape=(low, jax.ShapeDtypeStruct((2, tok...  9.86 us
  transfers between devices with their start and end apart: 7, of which 6 were waited for; matrix products, arithmetic and copies ran while one was open for 8% of the time, Pallas kernels for 3%

profile of v1, /device:TPU:0, one launch (start us, length us, event | category | flops | bytes accessed | tf_op | source)
XLA Modules:
  0.0 291.1 jit_solution(2275661392082144268)
XLA Ops:
  7.2 1.4 copy.31
  8.6 8.0 %all-to-all-start = ((bf16[16,1,6]{2,1,0:T(2,128)(2,1)}), bf16[16,1,6]{2,1,0:T(2,128)(2,1)S(1)}, u32[]{:S(2)}, u32[]{:S(2)}) async-start(bf16[16,1,6]{2,1,0:T(2,128)(2,1)} %copy.31), calls=%async_computation | async-start | bytes 16384 | tf_op jit(solution)/shard_map/all_to_all | solution.py:204
  17.5 2.2 gather_fusion
  19.7 2.2 gather_fusion.1
  22.0 0.9 reshape.142
  23.0 1.1 all-to-all-done
  24.1 6.1 %all-to-all-start.2 = ((bf16[16,1,6,2048]{3,2,1,0:T(8,128)(2,1)}), bf16[16,1,6,2048]{3,2,1,0:T(8,128)(2,1)S(1)}, u32[]{:S(2)}, u32[]{:S(2)}) async-start(bf16[16,1,6,2048]{3,2,1,0:T(8,128)(2,1)} %bitcast.8), calls=%async_computation.2 | async-start | bytes 1048576 | tf_op jit(solution)/shard_map/all_to_all | solution.py:202
  30.2 0.9 reshape.139
  31.3 11.3 %all-to-all-done.2 = bf16[16,1,6,2048]{3,2,1,0:T(8,128)(2,1)S(1)} async-done(((bf16[16,1,6,2048]{3,2,1,0:T(8,128)(2,1)}), bf16[16,1,6,2048]{3,2,1,0:T(8,128)(2,1)S(1)}, u32[]{:S(2)}, u32[]{:S(2)}) %all-to-all-start.2) | async-done | bytes 393248 | tf_op jit(solution)/shard_map/all_to_all | solution.py:202
  42.6 4.2 %all-to-all-start.1 = ((bf16[16,1,6,2048]{3,2,1,0:T(8,128)(2,1)}), bf16[16,1,6,2048]{3,2,1,0:T(8,128)(2,1)}, u32[]{:S(2)}, u32[]{:S(2)}) async-start(bf16[16,1,6,2048]{3,2,1,0:T(8,128)(2,1)} %bitcast.6), calls=%async_computation.1 | async-start | bytes 1048576 | tf_op jit(solution)/shard_map/all_to_all | solution.py:203
  46.9 0.9 reshape.143
  47.7 3.8 %fusion.2 = f32[96,1408]{1,0:T(8,128)S(1)} fusion(bf16[96,2048]{1,0:T(8,128)(2,1)} %reshape.143, bf16[1,2048,1408]{2,1,0:T(8,128)(2,1)} %param.23), kind=kOutput, calls=%fused_computation.4 | convolution fusion | flops 553648128 | bytes 6701056 | tf_op jit(solution)/shard_map/erd,edf->erf/dot_general | solution.py:209
  51.6 3.9 %fusion.6 = f32[96,1408]{1,0:T(8,128)S(1)} fusion(bf16[96,2048]{1,0:T(8,128)(2,1)} %reshape.143, bf16[1,2048,1408]{2,1,0:T(8,128)(2,1)} %param.24), kind=kOutput, calls=%fused_computation.8 | convolution fusion | flops 553648128 | bytes 6701056 | tf_op jit(solution)/shard_map/erd,edf->erf/dot_general | solution.py:210
  55.5 3.7 %all-to-all-done.1 = bf16[16,1,6,2048]{3,2,1,0:T(8,128)(2,1)} async-done(((bf16[16,1,6,2048]{3,2,1,0:T(8,128)(2,1)}), bf16[16,1,6,2048]{3,2,1,0:T(8,128)(2,1)}, u32[]{:S(2)}, u32[]{:S(2)}) %all-to-all-start.1) | async-done | bytes 393248 | tf_op jit(solution)/shard_map/all_to_all | solution.py:203
  59.2 1.9 reshape.140
  61.1 4.9 %multiply_reduce_fusion = (bf16[96]{0:T(256)(128)(2,1)S(1)}, f32[96,1408]{1,0:T(8,128)S(1)}) fusion(f32[96,1408]{1,0:T(8,128)S(1)} %fusion.6, f32[96,1408]{1,0:T(8,128)S(1)} %fusion.2, bf16[96,2048]{1,0:T(8,128)(2,1)} %reshape.140, bf16[1,1408,2048]{2,1,0:T(8,128)(2,1)} %param.25), kind=kOutput, calls=%fused_computation.18 | convolution fusion | flops 554594176 | bytes 7782592 | tf_op jit(solution)/shard_map/erd,efd->erf/dot_general | solution.py:211
  66.1 1.9 fusion
  68.0 1.9 fusion.13
  70.1 15.6 %all_to_all.20 = bf16[1,16,6,2048]{3,2,0,1:T(8,128)(2,1)S(1)} all-to-all(bf16[1,16,6,2048]{3,2,0,1:T(8,128)(2,1)S(1)} %bitcast.44), channel_id=1, replica_groups=mesh['ctx'=8,'exp'=16] {'exp'}, dimensions={1} | all-to-all | bytes 786432 | tf_op jit(solution)/shard_map/all_to_all | solution.py:222
  85.8 1.1 fusion.16
  87.0 1.0 pad_maximum_fusion
  88.0 51.7 %all-gather.8.cloned.1.call-done = bf16[1024,2048]{1,0:T(8,128)(2,1)} async-done(((bf16[64,2048]{1,0:T(8,128)(2,1)}), bf16[1024,2048]{1,0:T(8,128)(2,1)}) %all-gather.8.cloned.1.call-update) | async-done | bytes 4194320 | tf_op jit(solution)/shard_map/all_gather | solution.py:232
  139.8 4.1 %convolution_convert_fusion.d_out = bf16[1024,128]{1,0:T(8,128)(2,1)} fusion(bf16[1024,2048]{1,0:T(8,128)(2,1)} %all-gather.8.cloned.1.call-done, bf16[128,2048]{1,0:T(8,128)(2,1)S(1)} %copy-done), kind=kOutput, calls=%fused_computation.16 | convolution fusion | flops 537001984 | bytes 4980736 | tf_op jit(solution)/shard_map/dot_general | solution.py:231
  144.0 28.1 %all_gather.24 = s32[8192]{0:T(1024)S(1)} all-gather(s32[1024]{0:T(1024)S(1)} %copy-done.7), channel_id=1, replica_groups=mesh['ctx'=8,'exp'=16] {'ctx'}, dimensions={0}, use_global_device_ids=true | all-gather | bytes 36864 | tf_op jit(solution)/shard_map/all_gather | solution.py:147
  173.0 3.8 %all-to-all-start.4 = ((bf16[1,16,6]{2,0,1:T(2,128)(2,1)}), bf16[1,16,6]{2,0,1:T(2,128)(2,1)S(1)}, u32[]{:S(2)}, u32[]{:S(2)}) async-start(bf16[1,16,6]{2,0,1:T(2,128)(2,1)} %convert_element_type.64), calls=%async_computation.4 | async-start | bytes 16384 | tf_op jit(solution)/shard_map/all_to_all | solution.py:223
  176.8 7.4 %all-to-all-done.4 = bf16[1,16,6]{2,0,1:T(2,128)(2,1)S(1)} async-done(((bf16[1,16,6]{2,0,1:T(2,128)(2,1)}), bf16[1,16,6]{2,0,1:T(2,128)(2,1)S(1)}, u32[]{:S(2)}, u32[]{:S(2)}) %all-to-all-start.4) | async-done | bytes 224 | tf_op jit(solution)/shard_map/all_to_all | solution.py:223
  184.9 26.9 %all-gather.10.cloned.1.call-done = bf16[24,1024,128]{2,1,0:T(8,128)(2,1)} async-done(((bf16[3,1024,128]{2,1,0:T(8,128)(2,1)}), bf16[24,1024,128]{2,1,0:T(8,128)(2,1)}) %all-gather.10.cloned.1.call-update) | async-done | bytes 6291472 | tf_op jit(solution)/shard_map/all_gather | solution.py:146
  211.8 0.9 copy-done.1
  212.7 9.9 %query_grads.1 = (bf16[1024,128]{1,0:T(8,128)(2,1)}, f32[2,1024]{1,0:T(2,128)S(1)}) custom-call(s32[4]{0:T(128)S(1)} %pad_add_fusion.scal, bf16[8,3,1024,128]{3,2,1,0:T(8,128)(2,1)} %bitcast.49, bf16[1024,128]{1,0:T(8,128)(2,1)S(1)} %copy-done.1), custom_call_target="tpu_custom_call" | custom-call | flops 3221225472 | bytes 8388608 | tf_op jit(solution)/shard_map/query_grads/pallas_call | solution.py:157
  222.6 40.0 %all-gather.3.stats = f32[8,2,1024]{2,1,0:T(2,128)S(1)} all-gather(f32[1,2,1024]{2,1,0:T(2,128)S(1)} %bitcast.38), channel_id=4, replica_groups=mesh['ctx'=8,'exp'=16] {'ctx'}, dimensions={0}, use_global_device_ids=true | all-gather | bytes 73728 | tf_op jit(solution)/shard_map/all_gather | solution.py:167
  262.6 1.6 copy-done.2
  264.2 20.4 %key_grads.1 = (bf16[1024,128]{1,0:T(8,128)(2,1)}, bf16[1024,128]{1,0:T(8,128)(2,1)}) custom-call(s32[4]{0:T(128)S(1)} %pad_add_fusion.scal, bf16[8,3,1024,128]{3,2,1,0:T(8,128)(2,1)} %bitcast.50, bf16[8,1024,128]{2,1,0:T(8,128)(2,1)S(1)} %bitcast.39, f32[8,2,1024]{2,1,0:T(2,128)S(1)} %all-gather.3.stats), custom_call_target="tpu_custom_call" | custom-call | flops 3221225472 | bytes 8388608 | tf_op jit(solution)/shard_map/key_grads/pallas_call | solution.py:168
  (46 shorter events, 3.3 us)
Async XLA Ops:
  7.2 132.6 %copy-start = (bf16[128,2048]{1,0:T(8,128)(2,1)S(1)}, bf16[128,2048]{1,0:T(8,128)(2,1)}, u32[]{:S(2)}) copy-start(bf16[128,2048]{1,0:T(8,128)(2,1)} %param.18) | copy-start | bytes 1572868
  8.6 15.4 %all-to-all-start = ((bf16[16,1,6]{2,1,0:T(2,128)(2,1)}), bf16[16,1,6]{2,1,0:T(2,128)(2,1)S(1)}, u32[]{:S(2)}, u32[]{:S(2)}) async-start(bf16[16,1,6]{2,1,0:T(2,128)(2,1)} %copy.31), calls=%async_computation | async-start | bytes 16384 | tf_op jit(solution)/shard_map/all_to_all | solution.py:204
  24.1 18.5 %all-to-all-start.2 = ((bf16[16,1,6,2048]{3,2,1,0:T(8,128)(2,1)}), bf16[16,1,6,2048]{3,2,1,0:T(8,128)(2,1)S(1)}, u32[]{:S(2)}, u32[]{:S(2)}) async-start(bf16[16,1,6,2048]{3,2,1,0:T(8,128)(2,1)} %bitcast.8), calls=%async_computation.2 | async-start | bytes 1048576 | tf_op jit(solution)/shard_map/all_to_all | solution.py:202
  42.6 16.6 %all-to-all-start.1 = ((bf16[16,1,6,2048]{3,2,1,0:T(8,128)(2,1)}), bf16[16,1,6,2048]{3,2,1,0:T(8,128)(2,1)}, u32[]{:S(2)}, u32[]{:S(2)}) async-start(bf16[16,1,6,2048]{3,2,1,0:T(8,128)(2,1)} %bitcast.6), calls=%async_computation.1 | async-start | bytes 1048576 | tf_op jit(solution)/shard_map/all_to_all | solution.py:203
  46.8 93.0 %all-gather.8.cloned.1.call-start = ((), (), s32[]{:S(2)}) async-start(), calls=%async_computation.5 | async-start | bytes 4456448 | tf_op jit(solution)/shard_map/all_gather | solution.py:232
  51.5 14.5 %slice-start = ((s8[5767168]{0:T(1024)(128)(4,1)}), s8[1572864]{0:T(1024)(128)(4,1)S(1)}, s32[]{:S(2)}) async-start(s8[5767168]{0:T(1024)(128)(4,1)} %bitcast.40), calls=%async_computation.8 | async-start | bytes 3145728
  61.1 4.9 %slice-start.1 = ((s8[5767168]{0:T(1024)(128)(4,1)}), s8[4194304]{0:T(1024)(128)(4,1)S(1)}, s32[]{:S(2)}) async-start(s8[5767168]{0:T(1024)(128)(4,1)} %bitcast.40), calls=%async_computation.9 | async-start | bytes 8388608
  61.1 6.9 %slice-start.2 = ((s8[5767168]{0:T(1024)(128)(4,1)}), s8[4194304]{0:T(1024)(128)(4,1)S(1)}, s32[]{:S(2)}) async-start(s8[5767168]{0:T(1024)(128)(4,1)} %bitcast.42), calls=%async_computation.10 | async-start | bytes 8388608
  66.0 1.9 slice-start.3
  68.0 17.8 %copy-start.3 = (bf16[64,2048]{1,0:T(8,128)(2,1)S(1)}, bf16[64,2048]{1,0:T(8,128)(2,1)}, u32[]{:S(2)}) copy-start(bf16[64,2048]{1,0:T(8,128)(2,1)} %param.20) | copy-start | bytes 786436
  68.0 18.9 %copy-start.4 = (bf16[1024,128]{1,0:T(8,128)(2,1)S(1)}, bf16[1024,128]{1,0:T(8,128)(2,1)}, u32[]{:S(2)}) copy-start(bf16[1024,128]{1,0:T(8,128)(2,1)} %param.16) | copy-start | bytes 786436
  68.0 18.9 %copy-start.5 = (bf16[1024,128]{1,0:T(8,128)(2,1)S(1)}, bf16[1024,128]{1,0:T(8,128)(2,1)}, u32[]{:S(2)}) copy-start(bf16[1024,128]{1,0:T(8,128)(2,1)} %param.15) | copy-start | bytes 786436
  68.0 18.9 %copy-start.6 = (bf16[1024,128]{1,0:T(8,128)(2,1)S(1)}, bf16[1024,128]{1,0:T(8,128)(2,1)}, u32[]{:S(2)}) copy-start(bf16[1024,128]{1,0:T(8,128)(2,1)} %param.14) | copy-start | bytes 786436
  85.7 58.3 %copy-start.7 = (s32[1024]{0:T(1024)S(1)}, s32[1024]{0:T(1024)}, u32[]{:S(2)}) copy-start(s32[1024]{0:T(1024)} %param.17) | copy-start | bytes 12292
  86.9 124.9 %all-gather.10.cloned.1.call-start = ((), (), s32[]{:S(2)}) async-start(), calls=%async_computation.6 | async-start | bytes 7077888 | tf_op jit(solution)/shard_map/all_gather | solution.py:146
  88.0 174.6 %all-gather.12.cloned.1.call-start = ((), (), s32[]{:S(2)}) async-start(), calls=%async_computation.7 | async-start | bytes 2359296 | tf_op jit(solution)/shard_map/all_gather | solution.py:150
  173.0 11.3 %all-to-all-start.4 = ((bf16[1,16,6]{2,0,1:T(2,128)(2,1)}), bf16[1,16,6]{2,0,1:T(2,128)(2,1)S(1)}, u32[]{:S(2)}, u32[]{:S(2)}) async-start(bf16[1,16,6]{2,0,1:T(2,128)(2,1)} %convert_element_type.64), calls=%async_computation.4 | async-start | bytes 16384 | tf_op jit(solution)/shard_map/all_to_all | solution.py:223
  211.8 0.9 copy-start.1
  262.6 1.6 copy-start.2
Sparse Core Ops, SparseCore 0:
  87.0 52.7 all-gather.7
  141.4 70.3 all-gather.9
  214.0 39.6 all-gather.11

commit v2 on v1

v2 whole, which is shorter than its diff:
```python
import math

import jax
import jax.numpy as jnp
from jax import lax
from jax.experimental import pallas as pl
from jax.experimental.pallas import tpu as pltpu
from jax.sharding import PartitionSpec as P

NEG = -1e30
SCALE = 1.0 / math.sqrt(128)
KT = 512
QT = 256


def doc_start(place, scal):
    start = jnp.zeros_like(place)
    for d in range(1, 4):
        start = jnp.maximum(start, jnp.where(scal[d] <= place, scal[d], 0))
    return start


def doc_end(place, scal, tokens):
    end = jnp.full_like(place, tokens)
    for d in range(1, 4):
        end = jnp.minimum(end, jnp.where(scal[d] > place, scal[d], tokens))
    return end


def nt(a, b):
    return lax.dot_general(a, b, (((1,), (1,)), ((), ())), preferred_element_type=jnp.float32)


def fold(x, op):
    parts = [x[:, i * 128:(i + 1) * 128] for i in range(x.shape[1] // 128)]
    while len(parts) > 1:
        parts = [op(parts[i], parts[i + 1]) for i in range(0, len(parts), 2)]
    return parts[0]


BF = jnp.bfloat16
F32 = jnp.float32
MESH = pl.DeviceIdType.MESH
FC = 256


def iota(shape, dim):
    return lax.broadcasted_iota(jnp.int32, shape, dim)


def mm(a, b):
    return jnp.dot(a, b, preferred_element_type=F32)


def place_in_message(r, j):
    tail = (r - 12, jnp.where(r < 14, r - 8, r - 14), r - 10)[j]
    slot = jnp.where(r < 6, r, jnp.where(r < 12, r - 6, tail))
    block = jnp.where(r < 6, 0, jnp.where(r < 12, 1, 2))
    if j == 1:
        block = jnp.where(r >= 14, 3, block)
    return slot, block


BLOCKS = ((0, 3, 6), (1, 4, 6, 7), (2, 5, 7))


def stacked(array, j, width=256):
    return jnp.concatenate([array[:, c * width:(c + 1) * width] for c in BLOCKS[j]], axis=0)


def pack_weights(j, rows_in_block):
    wide = len(BLOCKS[j]) * rows_in_block
    row = iota((256, wide), 0)
    slot, block = place_in_message(row % 16, j)
    return (iota((256, wide), 1) == block * rows_in_block + (row // 16) * 6 + slot).astype(BF)


def unpack(buf, c):
    lane, i = iota((96, 256), 1), iota((96, 256), 0)
    r, src = lane % 16, lane // 16
    out = None
    for j in range(3):
        if c not in BLOCKS[j]:
            continue
        slot, block = place_in_message(r, j)
        pick = ((i == src * 6 + slot) & (block == BLOCKS[j].index(c))).astype(BF)
        part = mm(pick, buf[:, j * 256:(j + 1) * 256])
        out = part if out is None else out + part
    return out.astype(BF)


def remote(src, dst, ss, rs, device):
    return pltpu.make_async_remote_copy(
        src_ref=src, dst_ref=dst, send_sem=ss, recv_sem=rs, device_id=device, device_id_type=MESH)


def start(copy):
    copy.start()


def sent(copy):
    copy.wait_send()


def received(copy):
    copy.wait_recv()


def q_own(src, win, ss, rs, slot, device):
    return remote(src, win.at[slot], ss.at[slot], rs.at[slot], device)


def backward(src, win, ss, rs, act):
    c, e = lax.axis_index("ctx"), lax.axis_index("exp")
    xl, y = c // 4, c % 4

    @pl.when(xl == 1)
    def _():
        act(q_own(src, win, ss, rs, 4, ((c + 4) % 8, e)))
    for o in range(1, 4):
        yo = (y + o) % 4

        @pl.when(yo < y)
        def _():
            act(q_own(src, win, ss, rs, y - yo, (xl * 4 + yo, e)))


def backward_first(src, win, ss, rs, act):
    c, e = lax.axis_index("ctx"), lax.axis_index("exp")

    @pl.when(c // 4 == 0)
    def _():
        act(q_own(src, win, ss, rs, 4, ((c + 4) % 8, e)))


def backward_relay(win, ss, rs, act):
    c, e = lax.axis_index("ctx"), lax.axis_index("exp")
    xl, y = c // 4, c % 4
    for o in range(1, 4):
        yo = (y + o) % 4

        @pl.when((xl == 0) & (yo > y))
        def _():
            act(q_own(win.at[4], win, ss, rs, 4 + y - yo, (xl * 4 + yo, e)))


def backward_rest(src, win, ss, rs, act):
    c, e = lax.axis_index("ctx"), lax.axis_index("exp")
    for slot in range(1, 5):
        @pl.when((c + slot <= 7) & ((c >= 4) | (slot < 4)))
        def _():
            act(q_own(src, win, ss, rs, slot, (c, e)))


def rows16(ref, i):
    return ref.at[pl.ds(pl.multiple_of(i * 16, 16), 16), :]


def moe_kernel(hidden, grad, picks, gates, docs, wg, wu, wd, wo, qh, kh, vh,
               d_hidden, d_gates, kv_win, q_win, do_win, counts,
               wg_v, wu_v, wd_v, w4, sx, sg, rx, rg, x_v, g_v, a_v, b_v, da_v, db_v, dx_v,
               px, rr, dgs, dgr, selw, ag, d4, d_out, cnt,
               local_sem, x_ss, x_rs, g_ss, g_rs, r_ss, r_rs, t_ss, t_rs, c_ss, c_rs,
               w_ss, w_rs, ag_ss, ag_rs, ex_ss, ex_rs, kv_ss, kv_rs, q_ss, q_rs, do_ss, do_rs):
    c = lax.axis_index("ctx")
    e = lax.axis_index("exp")
    xl, y = c // 4, c % 4
    xh, z, k = e // 8, (e // 2) % 4, e % 2
    across = (c + 4) % 8

    def exp_at(xh_, z_, k_):
        return (xh_ * 4 + z_) * 2 + k_

    def peer(d):
        p = (e + d) % 16
        return p, ((c + 4 * ((p // 8 + xh) % 2)) % 8, p)

    loads = [
        pltpu.make_async_copy(wg, wg_v, local_sem.at[0]),
        pltpu.make_async_copy(wu, wu_v, local_sem.at[1]),
        pltpu.make_async_copy(wd, wd_v, local_sem.at[2]),
        pltpu.make_async_copy(wo, w4.at[xh * 2 + k], local_sem.at[3]),
        pltpu.make_async_copy(qh, q_win.at[0], local_sem.at[4]),
        pltpu.make_async_copy(kh, kv_win.at[0, 0], local_sem.at[5]),
        pltpu.make_async_copy(vh, kv_win.at[0, 1], local_sem.at[6]),
    ]
    for load in loads:
        load.start()

    barrier = pltpu.get_barrier_semaphore()

    def greet(d, _):
        pl.semaphore_signal(barrier, inc=1, device_id=peer(d)[1], device_id_type=MESH)
        return 0

    lax.fori_loop(1, 16, greet, 0)
    for k_ in range(2):
        pl.semaphore_signal(barrier, inc=1, device_id=(c, exp_at(1 - xh, z, k_)), device_id_type=MESH)

    def greet_ctx(o, _):
        pl.semaphore_signal(barrier, inc=1, device_id=((c + o) % 8, e), device_id_type=MESH)
        return 0

    lax.fori_loop(1, 8, greet_ctx, 0)

    row = iota((256, 16), 0)
    spread = (row // 16 == iota((256, 16), 1)).astype(BF)
    pick_rows = mm(spread, picks[0].astype(F32).astype(BF))
    gate_rows = mm(spread, gates[0])
    r = iota((256, 6), 0) % 16
    lane6 = iota((256, 6), 1)
    hid, gra = hidden[...], grad[...]
    for j in range(3):
        slot, block = place_in_message(r, j)
        mine = lane6 == slot
        pick = jnp.sum(jnp.where(mine, pick_rows, 0.0), axis=1, keepdims=True)
        gate = jnp.sum(jnp.where(mine, gate_rows, 0.0), axis=1, keepdims=True)
        wide = 64 * len(BLOCKS[j])
        target = block[:, 0:1].astype(F32) * 64.0 + pick
        hit = iota((256, wide), 1).astype(F32) == target
        sel = hit.astype(BF)
        sx[:, j * 256:(j + 1) * 256] = mm(sel, stacked(hid, j)).astype(BF)
        sg[:, j * 256:(j + 1) * 256] = mm(sel, stacked(gra, j)).astype(BF)
        if wide == 256:
            hit_w = hit
        else:
            hit_w = iota((256, 256), 1).astype(F32) == target
        selw[j] = jnp.transpose(jnp.where(hit_w, gate, 0.0)).astype(BF)
    sizes = []
    for d in range(8):
        under_d = jnp.sum((docs[...] < d).astype(F32), axis=1, keepdims=True)
        sizes.append(jnp.broadcast_to(jnp.sum(under_d, axis=0, keepdims=True), (1, 128)))
    below = jnp.concatenate(sizes, axis=0).astype(jnp.int32)
    cnt[...] = below
    counts[c] = below

    pl.semaphore_wait(barrier, 15 + 2 + 7)

    def x_copy(d):
        p, device = peer(d)
        return remote(rows16(sx, p), rows16(rx, e), x_ss.at[p], x_rs.at[e], device)

    def g_copy(d):
        p, device = peer(d)
        return remote(rows16(sg, p), rows16(rg, e), g_ss.at[p], g_rs.at[e], device)

    def r_copy(d):
        p, device = peer(d)
        return remote(rows16(px, p), rows16(rr, e), r_ss.at[p], r_rs.at[e], device)

    def t_copy(d):
        p, device = peer(d)
        return remote(rows16(dgs, p), rows16(dgr, e), t_ss.at[p], t_rs.at[e], device)

    def c_copy(o):
        return remote(cnt, counts.at[c], c_ss.at[o], c_rs.at[c], ((c + o) % 8, e))

    def recv(buf, rs):
        def one(d, _):
            p, device = peer(d)
            remote(rows16(buf, p), rows16(buf, p), rs.at[p], rs.at[p], device).wait_recv()
            return 0
        lax.fori_loop(1, 16, one, 0)

    def each(n0, n1, act):
        def one(d, _):
            act(d)
            return 0
        lax.fori_loop(n0, n1, one, 0)

    each(1, 16, lambda d: x_copy(d).start())
    each(1, 16, lambda d: g_copy(d).start())
    own16 = pl.ds(pl.multiple_of(e * 16, 16), 16)
    rx[own16, :] = sx[own16, :]
    rg[own16, :] = sg[own16, :]

    mate = (c, exp_at(xh, z, 1 - k))
    facing = (across, exp_at(1 - xh, z, k))
    own_q, mate_q = xh * 2 + k, xh * 2 + 1 - k
    far_q, far_mate_q = (1 - xh) * 2 + k, (1 - xh) * 2 + 1 - k
    w_mate = remote(wo, w4.at[own_q], w_ss.at[0], w_rs.at[0], mate)
    w_facing = remote(wo, w4.at[own_q], w_ss.at[1], w_rs.at[1], facing)
    w_relay = remote(w4.at[far_q], w4.at[far_q], w_ss.at[2], w_rs.at[2], mate)
    w_mate.start()
    w_facing.start()
    each(1, 8, lambda o: c_copy(o).start())

    def kv_own(slot, device):
        return [remote(src, kv_win.at[slot, i], kv_ss.at[slot, i], kv_rs.at[slot, i], device)
                for i, src in enumerate((kh, vh))]

    def forward(act):
        @pl.when(xl == 0)
        def _():
            for copy in kv_own(4, (across, e)):
                act(copy)
        for o in range(1, 4):
            yo = (y + o) % 4

            @pl.when(yo > y)
            def _():
                for copy in kv_own(yo - y, (xl * 4 + yo, e)):
                    act(copy)

    def forward_relay(act):
        for o in range(1, 4):
            yo = (y + o) % 4

            @pl.when((xl == 1) & (yo < y))
            def _():
                slot = 4 + yo - y
                act(remote(kv_win.at[4], kv_win.at[slot], kv_ss.at[slot, 0], kv_rs.at[slot, 0], (xl * 4 + yo, e)))

    forward(start)
    backward(qh, q_win, q_ss, q_rs, start)

    recv(rx, x_rs)
    for col in range(8):
        x_v[:, col * 256:(col + 1) * 256] = unpack(rx[...], col)
    loads[0].wait()
    loads[1].wait()

    def up(f0, n):
        cols = pl.ds(f0, n)
        a_v[:, cols] = mm(x_v[...], wg_v[:, cols])
        b_v[:, cols] = mm(x_v[...], wu_v[:, cols])

    def up_step(i, _):
        up(pl.multiple_of(i * FC, FC), FC)
        return 0

    ff = wg.shape[1]
    whole = ff // FC
    lax.fori_loop(0, whole, up_step, 0)
    if ff % FC:
        up(whole * FC, ff % FC)
    recv(rg, g_rs)
    for col in range(8):
        g_v[:, col * 256:(col + 1) * 256] = unpack(rg[...], col)
    loads[2].wait()

    def down(f0, n, acc):
        cols = pl.ds(f0, n)
        u = nt(g_v[...], wd_v[cols, :])
        a, b = a_v[:, cols], b_v[:, cols]
        sig = 1.0 / (1.0 + jnp.exp(-a))
        act = a * sig
        da_v[:, cols] = (u * b * sig * (1.0 + a * (1.0 - sig))).astype(BF)
        db_v[:, cols] = (u * act).astype(BF)
        return acc + fold(act * b * u, jnp.add)

    def down_step(i, acc):
        return down(pl.multiple_of(i * FC, FC), FC, acc)

    acc = lax.fori_loop(0, whole, down_step, jnp.zeros((96, 128), F32))
    if ff % FC:
        acc = down(whole * FC, ff % FC, acc)

    def back_step(i, _):
        cols = pl.ds(pl.multiple_of(i * FC, FC), FC)
        dx_v[:, cols] = (nt(da_v[...], wg_v[cols, :]) + nt(db_v[...], wu_v[cols, :])).astype(BF)
        return 0

    lax.fori_loop(0, wg.shape[0] // FC, back_step, 0)
    for j in range(3):
        px[:, j * 256:(j + 1) * 256] = mm(pack_weights(j, 96), stacked(dx_v[...], j)).astype(BF)
    each(1, 16, lambda d: r_copy(d).start())
    rr[own16, :] = px[own16, :]
    d_gate = jnp.broadcast_to(jnp.sum(acc, axis=1, keepdims=True), (96, 128)).astype(BF)
    row = iota((256, 96), 0)
    pack6 = ((iota((256, 96), 1) == (row // 16) * 6 + row % 16) & (row % 16 < 6)).astype(BF)
    dgs[...] = mm(pack6, d_gate).astype(BF)
    each(1, 16, lambda d: t_copy(d).start())
    dgr[own16, :] = dgs[own16, :]

    w_facing.wait_recv()
    w_relay.start()

    @pl.when(xl == 1)
    def _():
        for copy in kv_own(4, (across, e)):
            copy.wait_recv()
    forward_relay(start)

    backward_first(qh, q_win, q_ss, q_rs, received)
    backward_relay(q_win, q_ss, q_rs, start)

    recv(rr, r_rs)
    sums = [mm(selw[j], rr[:, j * 256:(j + 1) * 256]) for j in range(3)]
    parts = [sums[c_ % 3][(c_ // 3) * 64:(c_ // 3) * 64 + 64] for c_ in range(6)]
    parts.append(sums[0][128:192] + sums[1][128:192])
    parts.append(sums[1][192:256] + sums[2][128:192])
    for col in range(8):
        cols = slice(col * 256, (col + 1) * 256)
        low = (grad[:, cols].astype(F32) + parts[col]).astype(BF)
        ag[z, :, cols] = low
        d_hidden[:, cols] = low

    above, under = (c, exp_at(xh, (z + 1) % 4, k)), (c, exp_at(xh, (z + 3) % 4, k))
    z_up, z_down = (z + 1) % 4, (z + 3) % 4
    first, second = pl.ds(0, 32), pl.ds(32, 32)
    g_up = remote(ag.at[z], ag.at[z], ag_ss.at[0], ag_rs.at[0], above)
    g_down = remote(ag.at[z], ag.at[z], ag_ss.at[1], ag_rs.at[1], under)
    g_up2 = remote(ag.at[z_down, first], ag.at[z_down, first], ag_ss.at[2], ag_rs.at[2], above)
    g_down2 = remote(ag.at[z_up, second], ag.at[z_up, second], ag_ss.at[3], ag_rs.at[3], under)
    g_up.start()
    g_down.start()
    g_up.wait_recv()
    g_up2.start()
    g_down.wait_recv()
    g_down2.start()
    loads[3].wait()
    w_mate.wait_recv()
    w_relay.wait_recv()
    g_up2.wait_recv()
    g_down2.wait_recv()

    tokens = ag[...].reshape(256, ag.shape[2])
    for q_ in range(4):
        d4[q_] = nt(tokens, w4[q_]).astype(BF).reshape(4, 64, 128)
    others = [(mate_q, mate), (far_q, (c, exp_at(1 - xh, z, k))), (far_mate_q, (c, exp_at(1 - xh, z, 1 - k)))]
    sends = [remote(d4.at[q_], d_out.at[xh, :, k], ex_ss.at[i], ex_rs.at[i], device)
             for i, (q_, device) in enumerate(others)]
    for copy in sends:
        copy.start()
    d_out[xh, :, k] = d4[own_q]
    for copy in sends:
        copy.wait_recv()

    flat = d_out
    keep = pltpu.make_async_copy(flat, do_win.at[0], local_sem.at[7])
    keep.start()
    backward(flat, do_win, do_ss, do_rs, start)

    backward_first(flat, do_win, do_ss, do_rs, received)
    backward_relay(do_win, do_ss, do_rs, start)

    recv(dgr, t_rs)
    row, lane = iota((256, 128), 0), iota((256, 128), 1)
    diag = jnp.where(row % 16 == lane, dgr[...].astype(F32), 0.0).astype(BF)
    gather = (iota((16, 256), 1) // 16 == iota((16, 256), 0)).astype(BF)
    d_gates[...] = mm(gather, diag)[:, 0:6].astype(BF)

    def c_recv(o):
        src = (c + o) % 8
        remote(cnt, counts.at[src], c_ss.at[o], c_rs.at[src], (src, e)).wait_recv()

    each(1, 8, c_recv)
    for slot in range(1, 5):
        @pl.when((c >= slot) & (slot < 4))
        def _():
            @pl.when(c - slot >= xl * 4)
            def _():
                for copy in kv_own(slot, (c, e)):
                    copy.wait_recv()

            @pl.when(c - slot < xl * 4)
            def _():
                remote(kv_win.at[slot], kv_win.at[slot], kv_ss.at[slot, 0], kv_rs.at[slot, 0], (c, e)).wait_recv()

    backward_rest(qh, q_win, q_ss, q_rs, received)
    backward_rest(flat, do_win, do_ss, do_rs, received)
    each(1, 16, lambda d: x_copy(d).wait_send())
    each(1, 16, lambda d: g_copy(d).wait_send())
    each(1, 16, lambda d: r_copy(d).wait_send())
    each(1, 16, lambda d: t_copy(d).wait_send())
    each(1, 8, lambda o: c_copy(o).wait_send())
    for copy in [w_mate, w_facing, w_relay, g_up, g_down, g_up2, g_down2] + sends:
        copy.wait_send()
    forward(sent)
    forward_relay(sent)
    backward(qh, q_win, q_ss, q_rs, sent)
    backward_relay(q_win, q_ss, q_rs, sent)
    backward(flat, do_win, do_ss, do_rs, sent)
    backward_relay(do_win, do_ss, do_rs, sent)
    for load in loads[4:] + [keep]:
        load.wait()


def moe(q_heads, k_heads, v_heads, doc_ids, w_out, hidden_rows, out_grad, picks, gates, w_gate, w_up, w_down):
    vm, hbm = pl.BlockSpec(memory_space=pltpu.VMEM), pl.BlockSpec(memory_space=pl.ANY)
    tok, width = q_heads.shape
    rows, model = hidden_rows.shape
    ff = w_gate.shape[2]
    dma = pltpu.SemaphoreType.DMA

    def low(*shape):
        return pltpu.VMEM(shape, BF)

    def out(*shape, dtype=BF):
        return jax.ShapeDtypeStruct(shape, dtype)

    return pl.pallas_call(
        moe_kernel,
        out_shape=(out(rows, model), out(16, 6), out(5, 2, tok, width), out(5, tok, width),
                   out(5, 2, 4, 2, rows, width), out(8, 8, 128, dtype=jnp.int32)),
        in_specs=[vm] * 5 + [hbm] * 7,
        out_specs=(vm, vm, hbm, hbm, hbm, vm),
        scratch_shapes=[
            low(model, ff), low(model, ff), low(ff, model), low(4, 128, model),
            low(256, 768), low(256, 768), low(256, 768), low(256, 768),
            low(96, model), low(96, model), pltpu.VMEM((96, ff), F32), pltpu.VMEM((96, ff), F32),
            low(96, ff), low(96, ff), low(96, model),
            low(256, 768), low(256, 768), low(256, 128), low(256, 128),
            low(3, 256, 256), low(4, rows, model), low(4, 4, rows, width), low(2, 4, 2, rows, width),
            pltpu.VMEM((8, 128), jnp.int32),
            dma((8,)), dma((16,)), dma((16,)), dma((16,)), dma((16,)), dma((16,)), dma((16,)), dma((16,)), dma((16,)),
            dma((8,)), dma((8,)), dma((3,)), dma((3,)), dma((4,)), dma((4,)), dma((3,)), dma((3,)),
            dma((5, 2)), dma((5, 2)), dma((5,)), dma((5,)), dma((5,)), dma((5,)),
        ],
        compiler_params=pltpu.CompilerParams(
            collective_id=0, has_side_effects=True, vmem_limit_bytes=48 * 2**20),
        name="experts",
    )(hidden_rows, out_grad, picks, gates, doc_ids.reshape(8, 128), w_gate[0], w_up[0], w_down[0], w_out,
      q_heads, k_heads, v_heads)


def query_kernel(scal, q_ref, kv_win, d_out, dq_out, stats, s_buf, dp_buf):
    tok = q_ref.shape[0]
    per = tok // KT
    me = scal[0]

    def one(qi, _):
        rows = pl.ds(pl.multiple_of(qi * QT, QT), QT)
        row0 = me * tok + qi * QT
        first = doc_start(row0, scal) // KT
        last = (row0 + QT - 1) // KT
        count = last - first + 1
        q = q_ref[rows, :]
        do = d_out[0, rows, :]
        place = row0 + lax.broadcasted_iota(jnp.int32, (QT, KT), 0)
        start = doc_start(place, scal)
        lane = lax.broadcasted_iota(jnp.int32, (QT, KT), 1)

        def tile(t, which):
            at = first + t
            return kv_win[me - at // per, which, pl.ds(pl.multiple_of((at % per) * KT, KT), KT), :]

        def scores(t, top):
            s = nt(q, tile(t, 0)) * SCALE
            key = (first + t) * KT + lane
            s = jnp.where((key >= start) & (key <= place), s, NEG)
            s_buf[t] = s
            return jnp.maximum(top, fold(s, jnp.maximum))

        top = lax.fori_loop(0, count, scores, jnp.full((QT, 128), NEG, jnp.float32))
        top = jnp.max(top, axis=1, keepdims=True)

        def probs(t, carry):
            total, weighted = carry
            p = jnp.exp(s_buf[t] - top)
            dp = nt(do, tile(t, 1))
            s_buf[t] = p
            dp_buf[t] = dp
            return total + fold(p, jnp.add), weighted + fold(p * dp, jnp.add)

        zero = jnp.zeros((QT, 128), jnp.float32)
        total, weighted = lax.fori_loop(0, count, probs, (zero, zero))
        total = jnp.sum(total, axis=1, keepdims=True)
        inv = 1.0 / total
        delta = jnp.sum(weighted, axis=1, keepdims=True) * inv
        lse = top + jnp.log(total)

        def grads(t, dq):
            ds = (s_buf[t] * inv) * (dp_buf[t] - delta)
            return dq + jnp.dot(ds.astype(jnp.bfloat16), tile(t, 0), preferred_element_type=jnp.float32)

        dq = lax.fori_loop(0, count, grads, zero)
        dq_out[rows, :] = (dq * SCALE).astype(jnp.bfloat16)
        stats[0:1, rows] = jnp.transpose(jnp.broadcast_to(lse, (QT, 128)))[0:1, :]
        stats[1:2, rows] = jnp.transpose(jnp.broadcast_to(delta, (QT, 128)))[0:1, :]
        return 0

    lax.fori_loop(0, tok // QT, one, 0)


def key_kernel(scal, k_ref, v_ref, q_win, do_win, stats, dk_out, dv_out):
    tok = dk_out.shape[0]
    per = tok // KT
    me = scal[0]
    tokens = tok * 8

    def one(ki, _):
        rows = pl.ds(pl.multiple_of(ki * QT, QT), QT)
        row0 = me * tok + ki * QT
        first = row0 // KT
        last = (doc_end(row0 + QT - 1, scal, tokens) - 1) // KT
        k = k_ref[rows, :]
        v = v_ref[rows, :]
        key = row0 + lax.broadcasted_iota(jnp.int32, (QT, KT), 0)
        lane = lax.broadcasted_iota(jnp.int32, (1, KT), 1)

        def step(at, carry):
            dk, dv = carry
            block = at // per - me
            cols = pl.ds(pl.multiple_of((at % per) * KT, KT), KT)
            q = q_win[block, cols, :]
            do = do_win[block, cols, :]
            place = at * KT + lane
            start = doc_start(place, scal)
            allowed = (key >= start) & (key <= place)
            s = nt(k, q) * SCALE
            p = jnp.where(allowed, jnp.exp(s - stats[block, 0:1, cols]), 0.0)
            dp = nt(v, do)
            dv = dv + jnp.dot(p.astype(jnp.bfloat16), do, preferred_element_type=jnp.float32)
            ds = (p * (dp - stats[block, 1:2, cols])).astype(jnp.bfloat16)
            dk = dk + jnp.dot(ds, q, preferred_element_type=jnp.float32)
            return dk, dv

        zero = jnp.zeros((QT, 128), jnp.float32)
        dk, dv = lax.fori_loop(first, last + 1, step, (zero, zero))
        dk_out[rows, :] = (dk * SCALE).astype(jnp.bfloat16)
        dv_out[rows, :] = dv.astype(jnp.bfloat16)
        return 0

    lax.fori_loop(0, tok // QT, one, 0)


def stats_kernel(stats, win, local_sem, ss, rs):
    c, e = lax.axis_index("ctx"), lax.axis_index("exp")
    barrier = pltpu.get_barrier_semaphore()
    peers = [((c + 4) % 8, e)] + [((c // 4) * 4 + (c + o) % 4, e) for o in range(1, 4)]
    for device in peers:
        pl.semaphore_signal(barrier, inc=1, device_id=device, device_id_type=MESH)
    win[0] = stats[...]
    pl.semaphore_wait(barrier, 4)
    backward(stats, win, ss, rs, start)
    backward_first(stats, win, ss, rs, received)
    backward_relay(win, ss, rs, start)
    backward_rest(stats, win, ss, rs, received)
    backward(stats, win, ss, rs, sent)
    backward_relay(win, ss, rs, sent)


def attention(q_heads, k_heads, v_heads, kv_win, q_win, do_win, counts):
    tok, width = q_heads.shape
    me = lax.axis_index("ctx")
    starts = jnp.sum(counts[:, 1:4, 0], axis=0)
    scal = jnp.concatenate([me[None].astype(jnp.int32), starts])
    vmem = pl.BlockSpec(memory_space=pltpu.VMEM)
    smem = pl.BlockSpec(memory_space=pltpu.SMEM)
    params = pltpu.CompilerParams(vmem_limit_bytes=48 * 2**20)
    low = jax.ShapeDtypeStruct((tok, width), jnp.bfloat16)
    d_queries, stats = pl.pallas_call(
        query_kernel,
        grid=(1,),
        out_shape=(low, jax.ShapeDtypeStruct((8, tok), jnp.float32)),
        in_specs=[smem, vmem, vmem, pl.BlockSpec((1, tok, width), lambda *_: (0, 0, 0))],
        out_specs=(vmem, vmem),
        scratch_shapes=[pltpu.VMEM((9, QT, KT), jnp.float32), pltpu.VMEM((9, QT, KT), jnp.float32)],
        compiler_params=params,
        name="query_grads",
    )(scal, q_heads, kv_win, do_win)
    dma = pltpu.SemaphoreType.DMA
    stats_win = pl.pallas_call(
        stats_kernel,
        out_shape=jax.ShapeDtypeStruct((5, 8, tok), jnp.float32),
        in_specs=[vmem],
        out_specs=vmem,
        scratch_shapes=[dma((1,)), dma((5,)), dma((5,))],
        compiler_params=pltpu.CompilerParams(collective_id=1, has_side_effects=True),
        name="row_stats",
    )(stats)
    d_keys, d_values = pl.pallas_call(
        key_kernel,
        out_shape=(low, low),
        in_specs=[smem] + [vmem] * 5,
        out_specs=(vmem, vmem),
        compiler_params=params,
        name="key_grads",
    )(scal, k_heads, v_heads, q_win, do_win, stats_win)
    return d_queries, d_keys, d_values


def per_device(q_heads, k_heads, v_heads, doc_ids, w_out, hidden_rows, out_grad, picks, gates, w_gate, w_up, w_down):
    tok, width = q_heads.shape
    d_hidden, d_gates, kv_win, q_win, do_win, counts = moe(
        q_heads, k_heads, v_heads, doc_ids, w_out, hidden_rows, out_grad, picks, gates, w_gate, w_up, w_down)
    do_win = do_win.reshape(5, tok, width)
    d_queries, d_keys, d_values = attention(q_heads, k_heads, v_heads, kv_win, q_win, do_win, counts)
    return (d_queries, d_keys, d_values, d_hidden, d_gates[None])


def solution(mesh):
    return jax.shard_map(
        per_device,
        mesh=mesh,
        in_specs=(
            P("ctx", "exp"),
            P("ctx", "exp"),
            P("ctx", "exp"),
            P("ctx"),
            P("exp", None),
            P(("ctx", "exp"), None),
            P(("ctx", "exp"), None),
            P(("ctx", "exp"), None, None),
            P(("ctx", "exp"), None, None),
            P("exp", None, None),
            P("exp", None, None),
            P("exp", None, None),
        ),
        out_specs=(
            P("ctx", "exp"),
            P("ctx", "exp"),
            P("ctx", "exp"),
            P(("ctx", "exp"), None),
            P(("ctx", "exp"), None, None),
        ),
        check_vma=False,
    )
```

time: 292 us -> 142 us (0.49)
  waiting for transfers between devices: 102 us -> 0 us
  Pallas kernels: 30.2 us -> 128 us
  blocking collectives: 83.6 us -> 0 us
  starting transfers between devices: 22.2 us -> 0 us
  matrix products: 21.6 us -> 0 us
  between operations: 14 us -> 0.69 us
  local copies, waits for them, and re-layouts: 15.7 us -> 12.7 us
    pallas_call x2 -> x4, Pallas kernels: 30.2 us -> 128 us  [the longest x1 74.6 us: moe(): pl.pallas_call(moe_kernel, out_shape=(out(rows, model), out(16, 6), out(5...]
    all_gather x3 -> x0, waiting for transfers between devices: 78.6 us -> none  [the longest x1 51.7 us: per_device(): lax.all_gather(d_hidden, 'exp', axis=0, tiled=True)]
    all_gather x2 -> x0, blocking collectives: 68.1 us -> none  [the longest x1 40 us: attention(): stats_all = lax.all_gather(stats, 'ctx', axis=0)]
    all_to_all x4 -> x0, waiting for transfers between devices: 23.5 us -> none  [the longest x1 11.3 us: per_device(): lax.all_to_all(chosen_h, 'exp', split_axis=0, concat_axis=1, tiled=True)]
    all_to_all x4 -> x0, starting transfers between devices: 22.1 us -> none  [the longest x1 7.96 us: per_device(): lax.all_to_all(chosen_w, 'exp', split_axis=0, concat_axis=1, tiled=True)]
    dot_general x7 -> x0, matrix products: 21.6 us -> none  [the longest x1 4.9 us: per_device(): jnp.einsum('erd,efd->erf', g_rows, w_down, preferred_element_type=jnp.flo...]
    all_to_all x1 -> x0, blocking collectives: 15.6 us -> none  [per_device(): lax.all_to_all(d_x, 'exp', split_axis=1, concat_axis=0, tiled=True)]
    unnamed x26 -> x29, local copies, waits for them, and re-layouts: 4.03 us -> 12 us
  transfers between devices with their start and end apart: 7 -> 0, of which waited for: 6 -> 0; matrix products, arithmetic and copies ran while one was open for 8% -> 0% of each run, Pallas kernels for 3% -> 0%
where the time goes in v2:
time: 142 us; the launch traced here: 141 us
  Pallas kernels  128 us (90%)
  local copies, waits for them, and re-layouts  12.7 us (9%)
    pallas_call x1, Pallas kernels, moe(): pl.pallas_call(moe_kernel, out_shape=(out(rows, model), out(16, 6), out(5...  74.6 us
    pallas_call x1, Pallas kernels, attention(): pl.pallas_call(stats_kernel, out_shape=jax.ShapeDtypeStruct((5, 8, tok),...  27.6 us
    pallas_call x1, Pallas kernels, attention(): pl.pallas_call(key_kernel, out_shape=(low, low), in_specs=[smem] + [vmem]...  18 us
    unnamed x29, local copies, waits for them, and re-layouts  12 us
    pallas_call x1, Pallas kernels, attention(): pl.pallas_call(query_kernel, grid=(1,), out_shape=(low, jax.ShapeDtypeStr...  7.57 us

profile of v2, /device:TPU:0, one launch (start us, length us, event | category | flops | bytes accessed | tf_op | source)
XLA Modules:
  0.0 141.3 jit_solution(11147566010042417917)
XLA Ops:
  0.6 0.8 copy.18.gates
  1.4 0.8 copy.17.picks
  2.2 0.0 copy-start.1
  2.2 0.9 copy-done.1
  3.1 0.0 copy-start.3
  3.1 0.9 copy-done.3
  4.1 0.0 copy-start.5
  4.1 0.9 copy-done.5
  5.0 0.0 copy-start.8
  5.0 1.0 copy-done.8
  6.1 0.0 copy-start.9
  6.1 0.9 copy-done.9
  7.0 0.0 copy-start.10
  7.0 0.9 copy-done.10
  8.0 0.0 copy-start.12
  8.0 0.7 copy-done.12
  8.7 0.0 copy-start.2
  8.7 74.6 %experts.1 = (bf16[64,2048]{1,0:T(8,128)(2,1)S(1)}, bf16[16,6]{1,0:T(8,128)(2,1)S(1)}, bf16[5,2,1024,128]{3,2,1,0:T(8,128)(2,1)}, bf16[5,1024,128]{2,1,0:T(8,128...) custom-call(bf16[64,2048]{1,0:T(8,128)(2,1)S(1)} %copy-done.9, ...), custom_call_target="tpu_custom_call" | custom-call | tf_op jit(solution)/shard_map/experts/pallas_call | solution.py:493
  83.2 0.1 slice_reduce_fusion
  83.3 0.1 pad_add_fusion.scal
  83.4 0.0 copy-done.2
  83.4 1.7 %copy-done = bf16[5,2,1024,128]{3,2,1,0:T(8,128)(2,1)S(1)} copy-done((bf16[5,2,1024,128]{3,2,1,0:T(8,128)(2,1)S(1)}, bf16[5,2,1024,128]{3,2,1,0:T(8,128)(2,1)}, u32[]{:S(2)}) %copy-start) | copy-done | bytes 2621464
  85.2 7.6 %query_grads.1 = (bf16[1024,128]{1,0:T(8,128)(2,1)}, f32[8,1024]{1,0:T(8,128)S(1)}) custom-call(s32[4]{0:T(128)S(1)} %pad_add_fusion.scal, bf16[1024,128]{1,0:T(8,128)(2,1)S(1)} %copy-done.2, bf16[5,2,1024,128]{3,2,1,0:T(8,128)(2,1)S(1)} %copy-done, bf16[5,1024,128]{2,1,0:T(8,128)(2,1)S(1)} %bitcast.7), custom_call_target="tpu_custom_call" | custom-call | tf_op jit(solution)/shard_map/query_grads/pallas_call | solution.py:644
  92.7 0.6 copy-done.11
  93.4 0.7 copy.19
  94.0 27.6 %row_stats.1.stats = f32[5,8,1024]{2,1,0:T(8,128)} custom-call(f32[8,1024]{1,0:T(8,128)} %copy-done.11), custom_call_target="tpu_custom_call" | custom-call | tf_op jit(solution)/shard_map/row_stats/pallas_call | solution.py:655
  121.7 0.0 copy-done.4
  121.7 0.0 copy-done.6
  121.7 0.0 copy-start.7
  121.7 0.9 copy-done.7
  122.6 18.0 %key_grads.1 = (bf16[1024,128]{1,0:T(8,128)(2,1)}, bf16[1024,128]{1,0:T(8,128)(2,1)}) custom-call(s32[4]{0:T(128)S(1)} %pad_add_fusion.scal, bf16[1024,128]{1,0:T(8,128)(2,1)S(1)} %copy-done.4, bf16[1024,128]{1,0:T(8,128)(2,1)S(1)} %copy-done.6, bf16[5,1024,128]{2,1,0:T(8,128)(2,1)S(1)} %get-tuple-element.19.q_win, bf16[5,1024,128]{2,1,0:T(8,128)(2,1)S(1)} %bitcast.8, ...), custom_call_target="tpu_custom_call" | custom-call | tf_op jit(solution)/shard_map/key_grads/pallas_call | solution.py:664
  140.6 0.7 copy.21
  (4 shorter events, 0.0 us)
Async XLA Ops:
  2.2 0.9 copy-start.1
  3.1 0.9 copy-start.3
  4.1 0.9 copy-start.5
  5.0 1.0 copy-start.8
  6.1 0.9 copy-start.9
  7.0 0.9 copy-start.10
  8.0 0.7 copy-start.12
  8.7 74.8 %copy-start.2 = (bf16[1024,128]{1,0:T(8,128)(2,1)S(1)}, bf16[1024,128]{1,0:T(8,128)(2,1)}, u32[]{:S(2)}) copy-start(bf16[1024,128]{1,0:T(8,128)(2,1)} %q_ref.1) | copy-start | bytes 786436
  8.7 113.0 %copy-start.4 = (bf16[1024,128]{1,0:T(8,128)(2,1)S(1)}, bf16[1024,128]{1,0:T(8,128)(2,1)}, u32[]{:S(2)}) copy-start(bf16[1024,128]{1,0:T(8,128)(2,1)} %k_ref.1) | copy-start | bytes 786436
  8.7 113.0 %copy-start.6 = (bf16[1024,128]{1,0:T(8,128)(2,1)S(1)}, bf16[1024,128]{1,0:T(8,128)(2,1)}, u32[]{:S(2)}) copy-start(bf16[1024,128]{1,0:T(8,128)(2,1)} %v_ref.1) | copy-start | bytes 786436
  83.4 1.7 %copy-start = (bf16[5,2,1024,128]{3,2,1,0:T(8,128)(2,1)S(1)}, bf16[5,2,1024,128]{3,2,1,0:T(8,128)(2,1)}, u32[]{:S(2)}) copy-start(bf16[5,2,1024,128]{3,2,1,0:T(8,128)(2,1)} %get-tuple-element.16.kv_win) | copy-start | bytes 7864324
  92.7 0.6 copy-start.11
  121.7 0.9 copy-start.7

commit v3 on v2

v3 whole, which is shorter than its diff:
```python
import math

import jax
import jax.numpy as jnp
from jax import lax
from jax.experimental import pallas as pl
from jax.experimental.pallas import tpu as pltpu
from jax.sharding import PartitionSpec as P

NEG = -1e30
SCALE = 1.0 / math.sqrt(128)


def nt(a, b):
    return lax.dot_general(a, b, (((1,), (1,)), ((), ())), preferred_element_type=jnp.float32)


def fold(x, op):
    parts = [x[:, i * 128:(i + 1) * 128] for i in range(x.shape[1] // 128)]
    while len(parts) > 1:
        parts = [op(parts[i], parts[i + 1]) for i in range(0, len(parts), 2)]
    return parts[0]


BF = jnp.bfloat16
F32 = jnp.float32
MESH = pl.DeviceIdType.MESH
FC = 256


def iota(shape, dim):
    return lax.broadcasted_iota(jnp.int32, shape, dim)


def mm(a, b):
    return jnp.dot(a, b, preferred_element_type=F32)


def place_in_message(r, j):
    tail = (r - 12, jnp.where(r < 14, r - 8, r - 14), r - 10)[j]
    slot = jnp.where(r < 6, r, jnp.where(r < 12, r - 6, tail))
    block = jnp.where(r < 6, 0, jnp.where(r < 12, 1, 2))
    if j == 1:
        block = jnp.where(r >= 14, 3, block)
    return slot, block


BLOCKS = ((0, 3, 6), (1, 4, 6, 7), (2, 5, 7))


def stacked(array, j, width=256):
    return jnp.concatenate([array[:, c * width:(c + 1) * width] for c in BLOCKS[j]], axis=0)


def pack_weights(j, rows_in_block):
    wide = len(BLOCKS[j]) * rows_in_block
    row = iota((256, wide), 0)
    slot, block = place_in_message(row % 16, j)
    return (iota((256, wide), 1) == block * rows_in_block + (row // 16) * 6 + slot).astype(BF)


def unpack(buf, c):
    lane, i = iota((96, 256), 1), iota((96, 256), 0)
    r, src = lane % 16, lane // 16
    out = None
    for j in range(3):
        if c not in BLOCKS[j]:
            continue
        slot, block = place_in_message(r, j)
        pick = ((i == src * 6 + slot) & (block == BLOCKS[j].index(c))).astype(BF)
        part = mm(pick, buf[:, j * 256:(j + 1) * 256])
        out = part if out is None else out + part
    return out.astype(BF)


def remote(src, dst, ss, rs, device):
    return pltpu.make_async_remote_copy(
        src_ref=src, dst_ref=dst, send_sem=ss, recv_sem=rs, device_id=device, device_id_type=MESH)


def rows16(ref, i):
    return ref.at[pl.ds(pl.multiple_of(i * 16, 16), 16), :]


def kernel(hidden, grad, picks, gates, docs, wg, wu, wd, wo, qh, kh, vh,
           d_hidden, d_gates, dq_out, dk_out, dv_out,
           wg_v, wu_v, wd_v, w4, sx, sg, rx, rg, x_v, g_v, a_v, b_v, da_v, db_v, dx_v,
           px, rr, dgs, dgr, selw, ag, d4, cnt, counts,
           q_win, k_win, v_win, do_win, lse_win, delta_win, top_v, sum_v, o_v, lse_v, delta_v, start_v,
           pt_v, dq_v, dk_v, dv_v,
           local_sem, x_ss, x_rs, g_ss, g_rs, r_ss, r_rs, t_ss, t_rs, c_ss, c_rs,
           w_ss, w_rs, ag_ss, ag_rs, ex_ss, ex_rs, xs_ss, kv_ss, kv_rs, q_ss, q_rs, do_ss, do_rs,
           lse_ss, lse_rs, dl_ss, dl_rs):
    c = lax.axis_index("ctx")
    e = lax.axis_index("exp")
    xl, y = c // 4, c % 4
    xh, z, k = e // 8, (e // 2) % 4, e % 2
    across = (c + 4) % 8

    def exp_at(xh_, z_, k_):
        return (xh_ * 4 + z_) * 2 + k_

    def peer(d):
        p = (e + d) % 16
        return p, ((c + 4 * ((p // 8 + xh) % 2)) % 8, p)

    loads = [
        pltpu.make_async_copy(wg, wg_v, local_sem.at[0]),
        pltpu.make_async_copy(wu, wu_v, local_sem.at[1]),
        pltpu.make_async_copy(wd, wd_v, local_sem.at[2]),
        pltpu.make_async_copy(wo, w4.at[xh * 2 + k], local_sem.at[3]),
        pltpu.make_async_copy(qh, q_win.at[0], local_sem.at[4]),
        pltpu.make_async_copy(kh, k_win.at[0], local_sem.at[5]),
        pltpu.make_async_copy(vh, v_win.at[0], local_sem.at[6]),
    ]
    for load in loads:
        load.start()

    barrier = pltpu.get_barrier_semaphore()

    def greet(d, _):
        pl.semaphore_signal(barrier, inc=1, device_id=peer(d)[1], device_id_type=MESH)
        return 0

    lax.fori_loop(1, 16, greet, 0)
    for k_ in range(2):
        pl.semaphore_signal(barrier, inc=1, device_id=(c, exp_at(1 - xh, z, k_)), device_id_type=MESH)

    pl.semaphore_signal(barrier, inc=1, device_id=(across, exp_at(xh, z, 1 - k)), device_id_type=MESH)

    def greet_ctx(o, _):
        pl.semaphore_signal(barrier, inc=1, device_id=((c + o) % 8, e), device_id_type=MESH)
        return 0

    lax.fori_loop(1, 8, greet_ctx, 0)

    row = iota((256, 16), 0)
    spread = (row // 16 == iota((256, 16), 1)).astype(BF)
    pick_rows = nt(spread, jnp.concatenate([picks[i] for i in range(6)], axis=0).astype(F32).astype(BF))
    gate_rows = nt(spread, gates[0])
    r = iota((256, 6), 0) % 16
    lane6 = iota((256, 6), 1)
    hid, gra = hidden[...], grad[...]
    for j in range(3):
        slot, block = place_in_message(r, j)
        mine = lane6 == slot
        pick = jnp.sum(jnp.where(mine, pick_rows, 0.0), axis=1, keepdims=True)
        gate = jnp.sum(jnp.where(mine, gate_rows, 0.0), axis=1, keepdims=True)
        wide = 64 * len(BLOCKS[j])
        target = block[:, 0:1].astype(F32) * 64.0 + pick
        hit = iota((256, wide), 1).astype(F32) == target
        sel = hit.astype(BF)
        sx[:, j * 256:(j + 1) * 256] = mm(sel, stacked(hid, j)).astype(BF)
        sg[:, j * 256:(j + 1) * 256] = mm(sel, stacked(gra, j)).astype(BF)
        if wide == 256:
            hit_w = hit
        else:
            hit_w = iota((256, 256), 1).astype(F32) == target
        selw[j] = jnp.transpose(jnp.where(hit_w, gate, 0.0)).astype(BF)
    sizes = []
    for d in range(8):
        under_d = jnp.sum((docs[...] < d).astype(F32), axis=1, keepdims=True)
        sizes.append(jnp.broadcast_to(jnp.sum(under_d, axis=0, keepdims=True), (1, 128)))
    below = jnp.concatenate(sizes, axis=0).astype(jnp.int32)
    cnt[...] = below
    counts[c] = below

    pl.semaphore_wait(barrier, 15 + 3 + 7)

    def x_copy(d):
        p, device = peer(d)
        return remote(rows16(sx, p), rows16(rx, e), x_ss.at[p], x_rs.at[e], device)

    def g_copy(d):
        p, device = peer(d)
        return remote(rows16(sg, p), rows16(rg, e), g_ss.at[p], g_rs.at[e], device)

    def r_copy(d):
        p, device = peer(d)
        return remote(rows16(px, p), rows16(rr, e), r_ss.at[p], r_rs.at[e], device)

    def t_copy(d):
        p, device = peer(d)
        return remote(rows16(dgs, p), rows16(dgr, e), t_ss.at[p], t_rs.at[e], device)

    def c_copy(o):
        return remote(cnt, counts.at[c], c_ss.at[o], c_rs.at[c], ((c + o) % 8, e))

    def c_recv(o):
        src = (c + o) % 8
        remote(cnt, counts.at[src], c_ss.at[o], c_rs.at[src], (src, e)).wait_recv()

    def recv(buf, rs):
        def one(d, _):
            p, device = peer(d)
            remote(rows16(buf, p), rows16(buf, p), rs.at[p], rs.at[p], device).wait_recv()
            return 0
        lax.fori_loop(1, 16, one, 0)

    def each(n0, n1, act):
        def one(d, _):
            act(d)
            return 0
        lax.fori_loop(n0, n1, one, 0)

    each(1, 16, lambda d: x_copy(d).start())
    each(1, 16, lambda d: g_copy(d).start())
    own16 = pl.ds(pl.multiple_of(e * 16, 16), 16)
    rx[own16, :] = sx[own16, :]
    rg[own16, :] = sg[own16, :]

    mate = (c, exp_at(xh, z, 1 - k))
    facing = (across, exp_at(1 - xh, z, k))
    own_q, mate_q = xh * 2 + k, xh * 2 + 1 - k
    far_q, far_mate_q = (1 - xh) * 2 + k, (1 - xh) * 2 + 1 - k
    w_mate = remote(wo, w4.at[own_q], w_ss.at[0], w_rs.at[0], mate)
    w_facing = remote(wo, w4.at[own_q], w_ss.at[1], w_rs.at[1], facing)
    w_relay = remote(w4.at[far_q], w4.at[far_q], w_ss.at[2], w_rs.at[2], mate)
    w_mate.start()
    w_facing.start()
    each(1, 8, lambda o: c_copy(o).start())

    def kv_copy(slot, device, relay=False):
        return [remote(win.at[4] if relay else src, win.at[slot], kv_ss.at[slot, i], kv_rs.at[slot, i], device)
                for i, (src, win) in enumerate(((kh, k_win), (vh, v_win)))]

    def q_copy(slot, device, relay=False):
        return [remote(q_win.at[4] if relay else qh, q_win.at[slot], q_ss.at[slot], q_rs.at[slot], device)]

    def to_row(act):
        @pl.when(xl == 0)
        def _():
            act(kv_copy(4, (across, e)))

        @pl.when(xl == 1)
        def _():
            act(q_copy(4, (across, e)))
        for o in range(1, 4):
            yo = (y + o) % 4

            @pl.when(yo > y)
            def _():
                act(kv_copy(yo - y, (xl * 4 + yo, e)))

            @pl.when(yo < y)
            def _():
                act(q_copy(y - yo, (xl * 4 + yo, e)))

    def relay_row(act):
        for o in range(1, 4):
            yo = (y + o) % 4

            @pl.when((xl == 1) & (yo < y))
            def _():
                act(kv_copy(4 + yo - y, (xl * 4 + yo, e), True))

            @pl.when((xl == 0) & (yo > y))
            def _():
                act(q_copy(4 + y - yo, (xl * 4 + yo, e), True))

    def start(copies):
        for copy in copies:
            copy.start()

    def sent(copies):
        for copy in copies:
            copy.wait_send()

    def received(copies):
        for copy in copies:
            copy.wait_recv()

    to_row(start)

    recv(rx, x_rs)
    for col in range(8):
        x_v[:, col * 256:(col + 1) * 256] = unpack(rx[...], col)
    loads[0].wait()
    loads[1].wait()

    def up(f0, n):
        cols = pl.ds(f0, n)
        a_v[:, cols] = mm(x_v[...], wg_v[:, cols])
        b_v[:, cols] = mm(x_v[...], wu_v[:, cols])

    def up_step(i, _):
        up(pl.multiple_of(i * FC, FC), FC)
        return 0

    ff = wg.shape[1]
    whole = ff // FC
    lax.fori_loop(0, whole, up_step, 0)
    if ff % FC:
        up(whole * FC, ff % FC)
    recv(rg, g_rs)
    for col in range(8):
        g_v[:, col * 256:(col + 1) * 256] = unpack(rg[...], col)
    loads[2].wait()

    def down(f0, n, acc):
        cols = pl.ds(f0, n)
        u = nt(g_v[...], wd_v[cols, :])
        a, b = a_v[:, cols], b_v[:, cols]
        sig = 1.0 / (1.0 + jnp.exp(-a))
        act = a * sig
        da_v[:, cols] = (u * b * sig * (1.0 + a * (1.0 - sig))).astype(BF)
        db_v[:, cols] = (u * act).astype(BF)
        return acc + fold(act * b * u, jnp.add)

    def down_step(i, acc):
        return down(pl.multiple_of(i * FC, FC), FC, acc)

    acc = lax.fori_loop(0, whole, down_step, jnp.zeros((96, 128), F32))
    if ff % FC:
        acc = down(whole * FC, ff % FC, acc)

    def back_step(i, _):
        cols = pl.ds(pl.multiple_of(i * FC, FC), FC)
        dx_v[:, cols] = (nt(da_v[...], wg_v[cols, :]) + nt(db_v[...], wu_v[cols, :])).astype(BF)
        return 0

    lax.fori_loop(0, wg.shape[0] // FC, back_step, 0)
    for j in range(3):
        px[:, j * 256:(j + 1) * 256] = mm(pack_weights(j, 96), stacked(dx_v[...], j)).astype(BF)
    each(1, 16, lambda d: r_copy(d).start())
    rr[own16, :] = px[own16, :]
    d_gate = jnp.broadcast_to(jnp.sum(acc, axis=1, keepdims=True), (96, 128)).astype(BF)
    row = iota((256, 96), 0)
    pack6 = ((iota((256, 96), 1) == (row // 16) * 6 + row % 16) & (row % 16 < 6)).astype(BF)
    dgs[...] = mm(pack6, d_gate).astype(BF)
    each(1, 16, lambda d: t_copy(d).start())
    dgr[own16, :] = dgs[own16, :]

    w_facing.wait_recv()
    w_relay.start()

    @pl.when(xl == 1)
    def _():
        received(kv_copy(4, (across, e)))

    @pl.when(xl == 0)
    def _():
        received(q_copy(4, (across, e)))
    relay_row(start)

    recv(rr, r_rs)
    sums = [mm(selw[j], rr[:, j * 256:(j + 1) * 256]) for j in range(3)]
    parts = [sums[c_ % 3][(c_ // 3) * 64:(c_ // 3) * 64 + 64] for c_ in range(6)]
    parts.append(sums[0][128:192] + sums[1][128:192])
    parts.append(sums[1][192:256] + sums[2][128:192])
    for col in range(8):
        cols = slice(col * 256, (col + 1) * 256)
        low = (grad[:, cols].astype(F32) + parts[col]).astype(BF)
        ag[z, :, cols] = low
        d_hidden[:, cols] = low

    above, under = (c, exp_at(xh, (z + 1) % 4, k)), (c, exp_at(xh, (z + 3) % 4, k))
    z_up, z_down = (z + 1) % 4, (z + 3) % 4
    first, second = pl.ds(0, 32), pl.ds(32, 32)
    g_up = remote(ag.at[z], ag.at[z], ag_ss.at[0], ag_rs.at[0], above)
    g_down = remote(ag.at[z], ag.at[z], ag_ss.at[1], ag_rs.at[1], under)
    g_up2 = remote(ag.at[z_down, first], ag.at[z_down, first], ag_ss.at[2], ag_rs.at[2], above)
    g_down2 = remote(ag.at[z_up, second], ag.at[z_up, second], ag_ss.at[3], ag_rs.at[3], under)
    g_up.start()
    g_down.start()

    each(1, 8, lambda o: c_recv(o))
    total = counts[0]
    for src in range(1, 8):
        total = total + counts[src]

    def doc_start(place):
        start_at = jnp.zeros_like(place)
        for d in range(1, 4):
            first_of = jnp.concatenate([total[d:d + 1]] * (place.shape[1] // 128), axis=1)
            start_at = jnp.maximum(start_at, jnp.where(first_of <= place, first_of, 0))
        return start_at

    for i in (4, 5, 6):
        loads[i].wait()

    def half(i):
        return slice(i * 512, (i + 1) * 512)

    def row_mask(t, d, h):
        key = (c - d) * 1024 + h * 512 + iota((512, 512), 1)
        allowed = key >= start_v[half(t), 0:1]
        if isinstance(d, int) and d == 0:
            allowed = allowed & (key <= c * 1024 + t * 512 + iota((512, 512), 0))
        return allowed

    def key_tiles(t, act):
        act(0, range(t + 1))

        def step(d, _):
            act(d, range(2))
            return 0

        lax.fori_loop(1, jnp.minimum(c, 3) + 1, step, 0)

        @pl.when(xl == 1)
        def _():
            act(4, range(t, 2))

    def statistics(t):
        rows = half(t)
        start_v[rows, :] = doc_start(c * 1024 + t * 512 + iota((512, 128), 0))
        top_v[...] = jnp.full((512, 128), NEG, F32)
        sum_v[...] = jnp.zeros((512, 128), F32)
        o_v[rows, :] = jnp.zeros((512, 128), F32)
        q = q_win[0, rows, :]

        def act(d, halves):
            for h in halves:
                keys = half(h)
                s = jnp.where(row_mask(t, d, h), nt(q, k_win[d, keys, :]) * SCALE, NEG)
                old = top_v[...]
                new = jnp.maximum(old, jnp.max(fold(s, jnp.maximum), axis=1, keepdims=True))
                p = jnp.exp(s - new[:, 0:1])
                fade = jnp.exp(old - new)
                top_v[...] = new
                sum_v[...] = sum_v[...] * fade + fold(p, jnp.add)
                o_v[rows, :] = o_v[rows, :] * fade + mm(p.astype(BF), v_win[d, keys, :])

        key_tiles(t, act)
        norm = jnp.broadcast_to(jnp.sum(sum_v[...], axis=1, keepdims=True), (512, 128))
        o_v[rows, :] = o_v[rows, :] / norm
        lse = top_v[...] + jnp.log(norm)
        lse_v[rows, :] = lse
        lse_win[0, :, rows] = jnp.transpose(lse)[0:8, :]

    def row_copy(win, ss, rs, d):
        return remote(win.at[0], win.at[d], ss.at[d], rs.at[d], ((c + 8 - d) % 8, e))

    def before(act):
        for d in range(1, 5):
            @pl.when(c >= d)
            def _():
                act(d)

    def later(act):
        for d in range(1, 5):
            @pl.when(c + d <= 7)
            def _():
                act(d)

    for slot in range(1, 4):
        @pl.when(c >= slot)
        def _():
            received(kv_copy(slot, (c, e)))
    statistics(0)
    g_up.wait_recv()
    g_up2.start()
    g_down.wait_recv()
    g_down2.start()
    statistics(1)
    before(lambda d: row_copy(lse_win, lse_ss, lse_rs, d).start())
    loads[3].wait()
    w_mate.wait_recv()
    w_relay.wait_recv()
    g_up2.wait_recv()
    g_down2.wait_recv()

    tokens = ag[...].reshape(256, ag.shape[2])
    for q_ in range(4):
        d4[q_] = nt(tokens, w4[q_]).astype(BF).reshape(4, 64, 128)
    pieces = [
        (own_q, e, (xh, k)),
        (mate_q, exp_at(xh, z, 1 - k), (xh, 1 - k)),
        (far_q, exp_at(1 - xh, z, k), (1 - xh, k)),
        (far_mate_q, exp_at(1 - xh, z, 1 - k), (1 - xh, 1 - k)),
    ]

    def piece_copy(i):
        q_, head, _ = pieces[i]
        return remote(d4.at[q_], do_win.at[0, xh, :, k], ex_ss.at[i], ex_rs.at[i], (c, head))

    def piece_across(i):
        q_, head, _ = pieces[i]
        return remote(d4.at[q_], do_win.at[4, xh, :, k], xs_ss.at[i], do_rs.at[4, i], (across, head))

    def piece_along(i, slot, yo, src):
        _, _, (xs, ks) = pieces[i]
        return remote(do_win.at[src, xs, :, ks], do_win.at[slot, xs, :, ks], do_ss.at[slot, i], do_rs.at[slot, i],
                      (xl * 4 + yo, e))

    def along(i, act):
        for o in range(1, 4):
            yo = (y + o) % 4

            @pl.when(yo < y)
            def _():
                act(piece_along(i, y - yo, yo, 0))

    def along_relay(i, act):
        for o in range(1, 4):
            yo = (y + o) % 4

            @pl.when((xl == 0) & (yo > y))
            def _():
                act(piece_along(i, 4 + y - yo, yo, 4))

    for i in (2, 3, 1):
        piece_copy(i).start()

    @pl.when(xl == 1)
    def _():
        for i in (2, 3, 1, 0):
            piece_across(i).start()
    do_win[0, xh, :, k] = d4[own_q]
    along(0, lambda copy: copy.start())

    later(lambda d: received(q_copy(d, (c, e))) if d < 4 else None)

    def key_probs(t, d, halves, masked):
        key = c * 1024 + t * 512 + iota((512, 512), 0)
        for h in halves:
            cols = half(h)
            place = (c + d) * 1024 + h * 512 + iota((1, 512), 1)
            allowed = key >= doc_start(place)
            if masked:
                allowed = allowed & (key <= place)
            s = nt(k_win[0, half(t), :], q_win[d, cols, :]) * SCALE
            p = jnp.where(allowed, jnp.exp(s - lse_win[d, 0:1, cols]), 0.0)
            pt_v[t, d, :, cols] = p.astype(BF)

    def query_tiles(d, act):
        if d == 0:
            act(0, 0, range(2))
            act(1, 0, range(1, 2))
        elif d == 4:
            act(0, 4, range(1))
            act(1, 4, range(2))
        else:
            act(0, d, range(2))
            act(1, d, range(2))

    query_tiles(0, lambda t, d, halves: key_probs(t, d, halves, True))
    for i in (1, 2, 3):
        piece_copy(i).wait_recv()
        along(i, lambda copy: copy.start())

    @pl.when(xl == 0)
    def _():
        for i in range(4):
            piece_across(i).wait_recv()
    for i in range(4):
        along_relay(i, lambda copy: copy.start())

    d_own = do_win[0].reshape(1024, 128)
    prod = d_own.astype(F32) * o_v[...]
    delta_v[...] = jnp.broadcast_to(jnp.sum(prod, axis=1, keepdims=True), (1024, 128))
    high = prod.astype(BF)
    low_part = (prod - high.astype(F32)).astype(BF)
    ones = jnp.ones((8, 128), BF)
    delta_win[0] = nt(ones, high) + nt(ones, low_part)
    before(lambda d: row_copy(delta_win, dl_ss, dl_rs, d).start())
    later(lambda d: row_copy(lse_win, lse_ss, lse_rs, d).wait_recv())

    def probs_step(d, _):
        query_tiles(1, lambda t, _, halves: key_probs(t, d, halves, False))
        return 0

    lax.fori_loop(1, jnp.minimum(7 - c, 3) + 1, probs_step, 0)

    @pl.when(xl == 0)
    def _():
        query_tiles(4, lambda t, d, halves: key_probs(t, d, halves, False))

    for t in range(2):
        rows = half(t)
        dq_v[...] = jnp.zeros((512, 128), F32)
        q = q_win[0, rows, :]
        do = d_own[rows, :]

        def act(d, halves, t=t, rows=rows, q=q, do=do):
            for h in halves:
                keys = half(h)
                k_ = k_win[d, keys, :]
                p = jnp.where(row_mask(t, d, h), jnp.exp(nt(q, k_) * SCALE - lse_v[rows, 0:1]), 0.0)
                ds = p * (nt(do, v_win[d, keys, :]) - delta_v[rows, 0:1])
                dq_v[...] += mm(ds.astype(BF), k_)

        key_tiles(t, act)
        dq_out[rows, :] = (dq_v[...] * SCALE).astype(BF)

    dk_v[...] = jnp.zeros((1024, 128), F32)
    dv_v[...] = jnp.zeros((1024, 128), F32)

    def key_grads(t, d, halves):
        rows = half(t)
        do_all = do_win[d].reshape(1024, 128)
        for h in halves:
            cols = half(h)
            do = do_all[cols, :]
            p = pt_v[t, d, :, cols]
            dv_v[rows, :] += mm(p, do)
            ds = p.astype(F32) * (nt(v_win[0, rows, :], do) - delta_win[d, 0:1, cols])
            dk_v[rows, :] += mm(ds.astype(BF), q_win[d, cols, :])

    query_tiles(0, key_grads)
    later(lambda d: row_copy(delta_win, dl_ss, dl_rs, d).wait_recv())

    def grads_step(d, _):
        for i in range(4):
            piece_along(i, d, y, 0).wait_recv()
        query_tiles(1, lambda t, _, halves: key_grads(t, d, halves))
        return 0

    lax.fori_loop(1, jnp.minimum(7 - c, 3) + 1, grads_step, 0)

    @pl.when(xl == 0)
    def _():
        query_tiles(4, key_grads)
    dk_out[...] = (dk_v[...] * SCALE).astype(BF)
    dv_out[...] = dv_v[...].astype(BF)

    recv(dgr, t_rs)
    row, lane = iota((256, 128), 0), iota((256, 128), 1)
    diag = jnp.where(row % 16 == lane, dgr[...].astype(F32), 0.0).astype(BF)
    gather = (iota((16, 256), 1) // 16 == iota((16, 256), 0)).astype(BF)
    d_gates[...] = mm(gather, diag)[:, 0:6].astype(BF)

    each(1, 16, lambda d: x_copy(d).wait_send())
    each(1, 16, lambda d: g_copy(d).wait_send())
    each(1, 16, lambda d: r_copy(d).wait_send())
    each(1, 16, lambda d: t_copy(d).wait_send())
    each(1, 8, lambda o: c_copy(o).wait_send())
    for copy in [w_mate, w_facing, w_relay, g_up, g_down, g_up2, g_down2]:
        copy.wait_send()
    to_row(sent)
    relay_row(sent)
    before(lambda d: row_copy(lse_win, lse_ss, lse_rs, d).wait_send())
    before(lambda d: row_copy(delta_win, dl_ss, dl_rs, d).wait_send())
    for i in range(1, 4):
        piece_copy(i).wait_send()

    @pl.when(xl == 1)
    def _():
        for i in range(4):
            piece_across(i).wait_send()
    for i in range(4):
        along(i, lambda copy: copy.wait_send())
        along_relay(i, lambda copy: copy.wait_send())


def per_device(q_heads, k_heads, v_heads, doc_ids, w_out, hidden_rows, out_grad, picks, gates, w_gate, w_up, w_down):
    vm, hbm = pl.BlockSpec(memory_space=pltpu.VMEM), pl.BlockSpec(memory_space=pl.ANY)
    tok, width = q_heads.shape
    rows, model = hidden_rows.shape
    ff = w_gate.shape[2]
    dma = pltpu.SemaphoreType.DMA

    def low(*shape):
        return pltpu.VMEM(shape, BF)

    def full(*shape):
        return pltpu.VMEM(shape, F32)

    def out(*shape):
        return jax.ShapeDtypeStruct(shape, BF)

    d_hidden, d_gates, d_queries, d_keys, d_values = pl.pallas_call(
        kernel,
        out_shape=(out(rows, model), out(16, 6), out(tok, width), out(tok, width), out(tok, width)),
        in_specs=[vm] * 5 + [hbm] * 7,
        out_specs=[vm] * 5,
        scratch_shapes=[
            low(model, ff), low(model, ff), low(ff, model), low(4, 128, model),
            low(256, 768), low(256, 768), low(256, 768), low(256, 768),
            low(96, model), low(96, model), full(96, ff), full(96, ff),
            low(96, ff), low(96, ff), low(96, model),
            low(256, 768), low(256, 768), low(256, 128), low(256, 128),
            low(3, 256, 256), low(4, rows, model), low(4, 4, rows, width),
            pltpu.VMEM((8, 128), jnp.int32), pltpu.VMEM((8, 8, 128), jnp.int32),
            low(5, tok, width), low(5, tok, width), low(5, tok, width), low(5, 2, 4, 2, rows, width),
            full(5, 8, tok), full(5, 8, tok), full(512, 128), full(512, 128), full(tok, 128), full(tok, 128),
            full(tok, 128), pltpu.VMEM((tok, 128), jnp.int32),
            low(2, 5, 512, tok), full(512, 128), full(tok, 128), full(tok, 128),
            dma((8,)), dma((16,)), dma((16,)), dma((16,)), dma((16,)), dma((16,)), dma((16,)), dma((16,)), dma((16,)),
            dma((8,)), dma((8,)), dma((3,)), dma((3,)), dma((4,)), dma((4,)), dma((4,)), dma((4,)), dma((4,)),
            dma((5, 2)), dma((5, 2)), dma((5,)), dma((5,)), dma((5, 4)), dma((5, 4)),
            dma((5,)), dma((5,)), dma((5,)), dma((5,)),
        ],
        compiler_params=pltpu.CompilerParams(
            collective_id=0, has_side_effects=True, vmem_limit_bytes=60 * 2**20),
        name="backward",
    )(hidden_rows, out_grad, jnp.transpose(picks, (2, 0, 1)), jnp.transpose(gates, (0, 2, 1)), doc_ids.reshape(8, 128),
      w_gate[0], w_up[0], w_down[0], w_out, q_heads, k_heads, v_heads)
    return (d_queries, d_keys, d_values, d_hidden, d_gates[None])


def solution(mesh):
    return jax.shard_map(
        per_device,
        mesh=mesh,
        in_specs=(
            P("ctx", "exp"),
            P("ctx", "exp"),
            P("ctx", "exp"),
            P("ctx"),
            P("exp", None),
            P(("ctx", "exp"), None),
            P(("ctx", "exp"), None),
            P(("ctx", "exp"), None, None),
            P(("ctx", "exp"), None, None),
            P("exp", None, None),
            P("exp", None, None),
            P("exp", None, None),
        ),
        out_specs=(
            P("ctx", "exp"),
            P("ctx", "exp"),
            P("ctx", "exp"),
            P(("ctx", "exp"), None),
            P(("ctx", "exp"), None, None),
        ),
        check_vma=False,
    )
```

time: 142 us -> 116 us (0.82)
  the two profiles are of different devices: /device:TPU:0 before, /device:TPU:3 now
where the time goes in v3:
time: 116 us
  Pallas kernels  107 us (92%)
  local copies, waits for them, and re-layouts  8.01 us (7%)
    pallas_call x1, Pallas kernels, per_device(): pl.pallas_call(kernel, out_shape=(out(rows, model), out(16, 6), out(tok,...  107 us
    unnamed x4, local copies, waits for them, and re-layouts  6.67 us

profile of v3, /device:TPU:3, one launch (start us, length us, event | category | flops | bytes accessed | tf_op | source)
XLA Modules:
  0.0 115.9 jit_solution(14550485502973098656)
XLA Ops:
  0.6 107.3 %backward.1 = (bf16[64,2048]{1,0:T(8,128)(2,1)}, bf16[16,6]{1,0:T(8,128)(2,1)}, bf16[1024,128]{1,0:T(8,128)(2,1)}, bf16[1024,128]{1,0:T(8,128)(2,1)}, bf16[1024,128]{1,0:T(8,128)(2,1)}) custom-call(bf16[64,2048]{1,0:T(8,128)(2,1)} %hidden.1, bf16[64,2048]{1,0:T(8,128)(2,1)} %grad.1, s32[6,1,16]{2,1,0:T(1,128)} %bitcast.11, bf16[1,6,16]{2,1,0:T(8,128)(2,1)} %bitcast.12, ...), custom_call_target="tpu_custom_call" | custom-call | tf_op jit(solution)/shard_map/backward/pallas_call | solution.py:663
  107.9 1.3 %copy.17 = bf16[16,6]{0,1:T(8,128)(2,1)} copy(bf16[16,6]{1,0:T(8,128)(2,1)} %get-tuple-element.14) | data formatting | bytes 384 | tf_op jit(solution)/shard_map/backward/pallas_call | solution.py:663
  109.3 1.7 %copy.22 = bf16[1024,128]{1,0:T(8,128)(2,1)} copy(bf16[1024,128]{1,0:T(8,128)(2,1)} %get-tuple-element.20) | data formatting | bytes 524288
  110.9 1.7 %copy.23 = bf16[1024,128]{1,0:T(8,128)(2,1)} copy(bf16[1024,128]{1,0:T(8,128)(2,1)} %get-tuple-element.21) | data formatting | bytes 524288
  112.6 1.7 %copy.24 = bf16[1024,128]{1,0:T(8,128)(2,1)} copy(bf16[1024,128]{1,0:T(8,128)(2,1)} %get-tuple-element.22) | data formatting | bytes 524288
  114.3 1.7 %copy.25 = bf16[64,2048]{1,0:T(8,128)(2,1)} copy(bf16[64,2048]{1,0:T(8,128)(2,1)} %get-tuple-element.23) | data formatting | bytes 524288

commit v4 on v3

--- a/solution.py
+++ b/solution.py
@@ -1,3 +1,4 @@
+import functools
 import math
 
 import jax
@@ -9,6 +10,7 @@
 
 NEG = -1e30
 SCALE = 1.0 / math.sqrt(128)
+SCALE2 = SCALE * math.log2(math.e)
 
 
 def nt(a, b):
@@ -78,6 +80,13 @@
         src_ref=src, dst_ref=dst, send_sem=ss, recv_sem=rs, device_id=device, device_id_type=MESH)
 
 
+def over_rows(x, op):
+    parts = [x[i * 8:(i + 1) * 8] for i in range(x.shape[0] // 8)]
+    while len(parts) > 1:
+        parts = [op(parts[i], parts[i + 1]) for i in range(0, len(parts), 2)]
+    return parts[0]
+
+
 def rows16(ref, i):
     return ref.at[pl.ds(pl.multiple_of(i * 16, 16), 16), :]
 
@@ -86,7 +95,7 @@
            d_hidden, d_gates, dq_out, dk_out, dv_out,
            wg_v, wu_v, wd_v, w4, sx, sg, rx, rg, x_v, g_v, a_v, b_v, da_v, db_v, dx_v,
            px, rr, dgs, dgr, selw, ag, d4, cnt, counts,
-           q_win, k_win, v_win, do_win, lse_win, delta_win, top_v, sum_v, o_v, lse_v, delta_v, start_v,
+           q_win, k_win, v_win, do_win, lse_win, delta_win, top_v, sum_v, o_v,
            pt_v, dq_v, dk_v, dv_v,
            local_sem, x_ss, x_rs, g_ss, g_rs, r_ss, r_rs, t_ss, t_rs, c_ss, c_rs,
            w_ss, w_rs, ag_ss, ag_rs, ex_ss, ex_rs, xs_ss, kv_ss, kv_rs, q_ss, q_rs, do_ss, do_rs,
@@ -209,6 +218,58 @@
     rx[own16, :] = sx[own16, :]
     rg[own16, :] = sg[own16, :]
 
+    def kv_copy(slot, device, relay=False):
+        return [remote(win.at[4] if relay else src, win.at[slot], kv_ss.at[slot, i], kv_rs.at[slot, i], device)
+                for i, (src, win) in enumerate(((kh, k_win), (vh, v_win)))]
+
+    def q_copy(slot, device, relay=False):
+        return [remote(q_win.at[4] if relay else qh, q_win.at[slot], q_ss.at[slot], q_rs.at[slot], device)]
+
+    def to_row(act):
+        @pl.when(xl == 0)
+        def _():
+            act(kv_copy(4, (across, e)))
+
+        @pl.when(xl == 1)
+        def _():
+            act(q_copy(4, (across, e)))
+        for o in range(1, 4):
+            yo = (y + o) % 4
+
+            @pl.when(yo > y)
+            def _():
+                act(kv_copy(yo - y, (xl * 4 + yo, e)))
+
+            @pl.when(yo < y)
+            def _():
+                act(q_copy(y - yo, (xl * 4 + yo, e)))
+
+    def relay_row(act):
+        for o in range(1, 4):
+            yo = (y + o) % 4
+
+            @pl.when((xl == 1) & (yo < y))
+            def _():
+                act(kv_copy(4 + yo - y, (xl * 4 + yo, e), True))
+
+            @pl.when((xl == 0) & (yo > y))
+            def _():
+                act(q_copy(4 + y - yo, (xl * 4 + yo, e), True))
+
+    def start(copies):
+        for copy in copies:
+            copy.start()
+
+    def sent(copies):
+        for copy in copies:
+            copy.wait_send()
+
+    def received(copies):
+        for copy in copies:
+            copy.wait_recv()
+
+    to_row(start)
+
     mate = (c, exp_at(xh, z, 1 - k))
     facing = (across, exp_at(1 - xh, z, k))
     own_q, mate_q = xh * 2 + k, xh * 2 + 1 - k
@@ -220,58 +281,6 @@
     w_facing.start()
     each(1, 8, lambda o: c_copy(o).start())
 
-    def kv_copy(slot, device, relay=False):
-        return [remote(win.at[4] if relay else src, win.at[slot], kv_ss.at[slot, i], kv_rs.at[slot, i], device)
-                for i, (src, win) in enumerate(((kh, k_win), (vh, v_win)))]
-
-    def q_copy(slot, device, relay=False):
-        return [remote(q_win.at[4] if relay else qh, q_win.at[slot], q_ss.at[slot], q_rs.at[slot], device)]
-
-    def to_row(act):
-        @pl.when(xl == 0)
-        def _():
-            act(kv_copy(4, (across, e)))
-
-        @pl.when(xl == 1)
-        def _():
-            act(q_copy(4, (across, e)))
-        for o in range(1, 4):
-            yo = (y + o) % 4
-
-            @pl.when(yo > y)
-            def _():
-                act(kv_copy(yo - y, (xl * 4 + yo, e)))
-
-            @pl.when(yo < y)
-            def _():
-                act(q_copy(y - yo, (xl * 4 + yo, e)))
-
-    def relay_row(act):
-        for o in range(1, 4):
-            yo = (y + o) % 4
-
-            @pl.when((xl == 1) & (yo < y))
-            def _():
-                act(kv_copy(4 + yo - y, (xl * 4 + yo, e), True))
-
-            @pl.when((xl == 0) & (yo > y))
-            def _():
-                act(q_copy(4 + y - yo, (xl * 4 + yo, e), True))
-
-    def start(copies):
-        for copy in copies:
-            copy.start()
-
-    def sent(copies):
-        for copy in copies:
-            copy.wait_send()
-
-    def received(copies):
-        for copy in copies:
-            copy.wait_recv()
-
-    to_row(start)
-
     recv(rx, x_rs)
     for col in range(8):
         x_v[:, col * 256:(col + 1) * 256] = unpack(rx[...], col)
@@ -313,6 +322,15 @@
     acc = lax.fori_loop(0, whole, down_step, jnp.zeros((96, 128), F32))
     if ff % FC:
         acc = down(whole * FC, ff % FC, acc)
+
+    @pl.when(xl == 1)
+    def _():
+        received(kv_copy(4, (across, e)))
+
+    @pl.when(xl == 0)
+    def _():
+        received(q_copy(4, (across, e)))
+    relay_row(start)
 
     def back_step(i, _):
         cols = pl.ds(pl.multiple_of(i * FC, FC), FC)
@@ -334,14 +352,71 @@
     w_facing.wait_recv()
     w_relay.start()
 
+    each(1, 8, lambda o: c_recv(o))
+    total = counts[0]
+    for src in range(1, 8):
+        total = total + counts[src]
+
+    def doc_start(place):
+        start_at = jnp.zeros_like(place)
+        for d in range(1, 4):
+            first_of = jnp.concatenate([total[d:d + 1]] * (place.shape[1] // 128), axis=1)
+            start_at = jnp.maximum(start_at, jnp.where(first_of <= place, first_of, 0))
+        return start_at
+
+    for i in (4, 5, 6):
+        loads[i].wait()
+
+    def half(i):
+        return slice(i * 512, (i + 1) * 512)
+
+    starts = [doc_start(c * 1024 + t * 512 + iota((1, 512), 1)) for t in range(2)]
+
+    def seen(t, d, h):
+        key = (c - d) * 1024 + h * 512 + iota((512, 512), 0)
+        allowed = key >= starts[t]
+        if isinstance(d, int) and d == 0:
+            allowed = allowed & (key <= c * 1024 + t * 512 + iota((512, 512), 1))
+        return allowed
+
+    def key_halves(t, d):
+        if isinstance(d, int):
+            return range(t + 1) if d == 0 else range(t, 2)
+        return range(2)
+
+    top_v[...] = jnp.full((8, 1024), NEG, F32)
+    sum_v[...] = jnp.zeros((8, 1024), F32)
+    o_v[...] = jnp.zeros((128, 1024), F32)
+
+    def statistics(d):
+        for t in range(2):
+            cols = half(t)
+            halves = key_halves(t, d)
+            q = q_win[0, cols, :]
+            scores = [jnp.where(seen(t, d, h), nt(k_win[d, half(h), :], q) * SCALE2, NEG) for h in halves]
+            most = functools.reduce(jnp.maximum, [over_rows(s, jnp.maximum) for s in scores])
+            old = top_v[:, cols]
+            new = jnp.maximum(old, jnp.max(most, axis=0, keepdims=True))
+            fade = jnp.exp2(old - new)
+            probs = [jnp.exp2(s - new[0:1]) for s in scores]
+            top_v[:, cols] = new
+            sum_v[:, cols] = sum_v[:, cols] * fade + sum(over_rows(p, jnp.add) for p in probs)
+            o_v[:, cols] = o_v[:, cols] * fade[0:1] + sum(
+                mm(jnp.transpose(v_win[d, half(h), :]), p.astype(BF)) for h, p in zip(halves, probs))
+
+    def statistics_step(d, _):
+        received(kv_copy(d, (c, e)))
+        statistics(d)
+        return 0
+
+    last_before = jnp.minimum(c, 3)
+    direct = jnp.minimum(y, 1)
+    statistics(0)
+
     @pl.when(xl == 1)
     def _():
-        received(kv_copy(4, (across, e)))
-
-    @pl.when(xl == 0)
-    def _():
-        received(q_copy(4, (across, e)))
-    relay_row(start)
+        statistics(4)
+    lax.fori_loop(1, direct + 1, statistics_step, 0)
 
     recv(rr, r_rs)
     sums = [mm(selw[j], rr[:, j * 256:(j + 1) * 256]) for j in range(3)]
@@ -364,70 +439,15 @@
     g_up.start()
     g_down.start()
 
-    each(1, 8, lambda o: c_recv(o))
-    total = counts[0]
-    for src in range(1, 8):
-        total = total + counts[src]
-
-    def doc_start(place):
-        start_at = jnp.zeros_like(place)
-        for d in range(1, 4):
-            first_of = jnp.concatenate([total[d:d + 1]] * (place.shape[1] // 128), axis=1)
-            start_at = jnp.maximum(start_at, jnp.where(first_of <= place, first_of, 0))
-        return start_at
-
-    for i in (4, 5, 6):
-        loads[i].wait()
-
-    def half(i):
-        return slice(i * 512, (i + 1) * 512)
-
-    def row_mask(t, d, h):
-        key = (c - d) * 1024 + h * 512 + iota((512, 512), 1)
-        allowed = key >= start_v[half(t), 0:1]
-        if isinstance(d, int) and d == 0:
-            allowed = allowed & (key <= c * 1024 + t * 512 + iota((512, 512), 0))
-        return allowed
-
-    def key_tiles(t, act):
-        act(0, range(t + 1))
-
-        def step(d, _):
-            act(d, range(2))
-            return 0
-
-        lax.fori_loop(1, jnp.minimum(c, 3) + 1, step, 0)
-
-        @pl.when(xl == 1)
-        def _():
-            act(4, range(t, 2))
-
-    def statistics(t):
-        rows = half(t)
-        start_v[rows, :] = doc_start(c * 1024 + t * 512 + iota((512, 128), 0))
-        top_v[...] = jnp.full((512, 128), NEG, F32)
-        sum_v[...] = jnp.zeros((512, 128), F32)
-        o_v[rows, :] = jnp.zeros((512, 128), F32)
-        q = q_win[0, rows, :]
-
-        def act(d, halves):
-            for h in halves:
-                keys = half(h)
-                s = jnp.where(row_mask(t, d, h), nt(q, k_win[d, keys, :]) * SCALE, NEG)
-                old = top_v[...]
-                new = jnp.maximum(old, jnp.max(fold(s, jnp.maximum), axis=1, keepdims=True))
-                p = jnp.exp(s - new[:, 0:1])
-                fade = jnp.exp(old - new)
-                top_v[...] = new
-                sum_v[...] = sum_v[...] * fade + fold(p, jnp.add)
-                o_v[rows, :] = o_v[rows, :] * fade + mm(p.astype(BF), v_win[d, keys, :])
-
-        key_tiles(t, act)
-        norm = jnp.broadcast_to(jnp.sum(sum_v[...], axis=1, keepdims=True), (512, 128))
-        o_v[rows, :] = o_v[rows, :] / norm
-        lse = top_v[...] + jnp.log(norm)
-        lse_v[rows, :] = lse
-        lse_win[0, :, rows] = jnp.transpose(lse)[0:8, :]
+    middle = jnp.minimum(direct + 3, last_before + 1)
+    lax.fori_loop(direct + 1, middle, statistics_step, 0)
+    g_up.wait_recv()
+    g_up2.start()
+    g_down.wait_recv()
+    g_down2.start()
+    lax.fori_loop(middle, last_before + 1, statistics_step, 0)
+    norm = jnp.sum(sum_v[...], axis=0, keepdims=True)
+    lse_win[0] = top_v[...] + jnp.log(norm) * math.log2(math.e)
 
     def row_copy(win, ss, rs, d):
         return remote(win.at[0], win.at[d], ss.at[d], rs.at[d], ((c + 8 - d) % 8, e))
@@ -444,16 +464,6 @@
             def _():
                 act(d)
 
-    for slot in range(1, 4):
-        @pl.when(c >= slot)
-        def _():
-            received(kv_copy(slot, (c, e)))
-    statistics(0)
-    g_up.wait_recv()
-    g_up2.start()
-    g_down.wait_recv()
-    g_down2.start()
-    statistics(1)
     before(lambda d: row_copy(lse_win, lse_ss, lse_rs, d).start())
     loads[3].wait()
     w_mate.wait_recv()
@@ -510,8 +520,6 @@
     do_win[0, xh, :, k] = d4[own_q]
     along(0, lambda copy: copy.start())
 
-    later(lambda d: received(q_copy(d, (c, e))) if d < 4 else None)
-
     def key_probs(t, d, halves, masked):
         key = c * 1024 + t * 512 + iota((512, 512), 0)
         for h in halves:
@@ -520,8 +528,8 @@
             allowed = key >= doc_start(place)
             if masked:
                 allowed = allowed & (key <= place)
-            s = nt(k_win[0, half(t), :], q_win[d, cols, :]) * SCALE
-            p = jnp.where(allowed, jnp.exp(s - lse_win[d, 0:1, cols]), 0.0)
+            s = nt(k_win[0, half(t), :], q_win[d, cols, :]) * SCALE2
+            p = jnp.where(allowed, jnp.exp2(s - lse_win[d, 0:1, cols]), 0.0)
             pt_v[t, d, :, cols] = p.astype(BF)
 
     def query_tiles(d, act):
@@ -535,8 +543,18 @@
             act(0, d, range(2))
             act(1, d, range(2))
 
+    def probs_step(d, _):
+        received(q_copy(d, (c, e)))
+        row_copy(lse_win, lse_ss, lse_rs, d).wait_recv()
+        query_tiles(1, lambda t, _, halves: key_probs(t, d, halves, False))
+        return 0
+
+    last_after = jnp.minimum(7 - c, 3)
     query_tiles(0, lambda t, d, halves: key_probs(t, d, halves, True))
-    for i in (1, 2, 3):
+    piece_copy(1).wait_recv()
+    along(1, lambda copy: copy.start())
+    lax.fori_loop(1, jnp.minimum(last_after, 1) + 1, probs_step, 0)
+    for i in (2, 3):
         piece_copy(i).wait_recv()
         along(i, lambda copy: copy.start())
 
@@ -548,41 +566,46 @@
         along_relay(i, lambda copy: copy.start())
 
     d_own = do_win[0].reshape(1024, 128)
-    prod = d_own.astype(F32) * o_v[...]
-    delta_v[...] = jnp.broadcast_to(jnp.sum(prod, axis=1, keepdims=True), (1024, 128))
+    prod = d_own.astype(F32) * jnp.transpose(o_v[...] / norm)
     high = prod.astype(BF)
     low_part = (prod - high.astype(F32)).astype(BF)
     ones = jnp.ones((8, 128), BF)
     delta_win[0] = nt(ones, high) + nt(ones, low_part)
     before(lambda d: row_copy(delta_win, dl_ss, dl_rs, d).start())
-    later(lambda d: row_copy(lse_win, lse_ss, lse_rs, d).wait_recv())
-
-    def probs_step(d, _):
-        query_tiles(1, lambda t, _, halves: key_probs(t, d, halves, False))
+    lax.fori_loop(2, last_after + 1, probs_step, 0)
+
+    @pl.when(xl == 0)
+    def _():
+        row_copy(lse_win, lse_ss, lse_rs, 4).wait_recv()
+        query_tiles(4, lambda t, d, halves: key_probs(t, d, halves, False))
+
+    dq_v[...] = jnp.zeros((128, 1024), F32)
+
+    def query_grads(d):
+        for t in range(2):
+            cols = half(t)
+            q = q_win[0, cols, :]
+            do = d_own[cols, :]
+            acc = dq_v[:, cols]
+            for h in key_halves(t, d):
+                keys = k_win[d, half(h), :]
+                p = jnp.exp2(nt(keys, q) * SCALE2 - lse_win[0, 0:1, cols])
+                p = jnp.where(seen(t, d, h), p, 0.0)
+                ds = p * (nt(v_win[d, half(h), :], do) - delta_win[0, 0:1, cols])
+                acc = acc + mm(jnp.transpose(keys), ds.astype(BF))
+            dq_v[:, cols] = acc
+
+    def query_step(d, _):
+        query_grads(d)
         return 0
 
-    lax.fori_loop(1, jnp.minimum(7 - c, 3) + 1, probs_step, 0)
-
-    @pl.when(xl == 0)
-    def _():
-        query_tiles(4, lambda t, d, halves: key_probs(t, d, halves, False))
-
-    for t in range(2):
-        rows = half(t)
-        dq_v[...] = jnp.zeros((512, 128), F32)
-        q = q_win[0, rows, :]
-        do = d_own[rows, :]
-
-        def act(d, halves, t=t, rows=rows, q=q, do=do):
-            for h in halves:
-                keys = half(h)
-                k_ = k_win[d, keys, :]
-                p = jnp.where(row_mask(t, d, h), jnp.exp(nt(q, k_) * SCALE - lse_v[rows, 0:1]), 0.0)
-                ds = p * (nt(do, v_win[d, keys, :]) - delta_v[rows, 0:1])
-                dq_v[...] += mm(ds.astype(BF), k_)
-
-        key_tiles(t, act)
-        dq_out[rows, :] = (dq_v[...] * SCALE).astype(BF)
+    query_grads(0)
+    lax.fori_loop(1, last_before + 1, query_step, 0)
+
+    @pl.when(xl == 1)
+    def _():
+        query_grads(4)
+    dq_out[...] = (jnp.transpose(dq_v[...]) * SCALE).astype(BF)
 
     dk_v[...] = jnp.zeros((1024, 128), F32)
     dv_v[...] = jnp.zeros((1024, 128), F32)
@@ -590,27 +613,27 @@
     def key_grads(t, d, halves):
         rows = half(t)
         do_all = do_win[d].reshape(1024, 128)
-        for h in halves:
-            cols = half(h)
-            do = do_all[cols, :]
-            p = pt_v[t, d, :, cols]
-            dv_v[rows, :] += mm(p, do)
-            ds = p.astype(F32) * (nt(v_win[0, rows, :], do) - delta_win[d, 0:1, cols])
-            dk_v[rows, :] += mm(ds.astype(BF), q_win[d, cols, :])
+        cols = slice(halves[0] * 512, halves[-1] * 512 + 512)
+        do = do_all[cols, :]
+        p = pt_v[t, d, :, cols]
+        dv_v[rows, :] += mm(p, do)
+        ds = p.astype(F32) * (nt(v_win[0, rows, :], do) - delta_win[d, 0:1, cols])
+        dk_v[rows, :] += mm(ds.astype(BF), q_win[d, cols, :])
 
     query_tiles(0, key_grads)
-    later(lambda d: row_copy(delta_win, dl_ss, dl_rs, d).wait_recv())
 
     def grads_step(d, _):
         for i in range(4):
             piece_along(i, d, y, 0).wait_recv()
+        row_copy(delta_win, dl_ss, dl_rs, d).wait_recv()
         query_tiles(1, lambda t, _, halves: key_grads(t, d, halves))
         return 0
 
-    lax.fori_loop(1, jnp.minimum(7 - c, 3) + 1, grads_step, 0)
+    lax.fori_loop(1, last_after + 1, grads_step, 0)
 
     @pl.when(xl == 0)
     def _():
+        row_copy(delta_win, dl_ss, dl_rs, 4).wait_recv()
         query_tiles(4, key_grads)
     dk_out[...] = (dk_v[...] * SCALE).astype(BF)
     dv_out[...] = dv_v[...].astype(BF)
@@ -619,7 +642,7 @@
     row, lane = iota((256, 128), 0), iota((256, 128), 1)
     diag = jnp.where(row % 16 == lane, dgr[...].astype(F32), 0.0).astype(BF)
     gather = (iota((16, 256), 1) // 16 == iota((16, 256), 0)).astype(BF)
-    d_gates[...] = mm(gather, diag)[:, 0:6].astype(BF)
+    d_gates[0] = jnp.transpose(mm(gather, diag))[0:6].astype(BF)
 
     each(1, 16, lambda d: x_copy(d).wait_send())
     each(1, 16, lambda d: g_copy(d).wait_send())
@@ -644,6 +667,20 @@
         along_relay(i, lambda copy: copy.wait_send())
 
 
+def hand_over(*refs):
+    n = len(refs) // 3
+    held, sems = refs[2 * n:3 * n], refs[-1]
+    reads = [pltpu.make_async_copy(refs[i], held[i], sems.at[i]) for i in range(n)]
+    writes = [pltpu.make_async_copy(held[i], refs[n + i], sems.at[n + i]) for i in range(n)]
+    for read in reads:
+        read.start()
+    for read, write in zip(reads, writes):
+        read.wait()
+        write.start()
+    for write in writes:
+        write.wait()
+
+
 def per_device(q_heads, k_heads, v_heads, doc_ids, w_out, hidden_rows, out_grad, picks, gates, w_gate, w_up, w_down):
     vm, hbm = pl.BlockSpec(memory_space=pltpu.VMEM), pl.BlockSpec(memory_space=pl.ANY)
     tok, width = q_heads.shape
@@ -660,9 +697,10 @@
     def out(*shape):
         return jax.ShapeDtypeStruct(shape, BF)
 
-    d_hidden, d_gates, d_queries, d_keys, d_values = pl.pallas_call(
+    shapes = (out(rows, model), out(1, 6, 16), out(tok, width), out(tok, width), out(tok, width))
+    results = pl.pallas_call(
         kernel,
-        out_shape=(out(rows, model), out(16, 6), out(tok, width), out(tok, width), out(tok, width)),
+        out_shape=shapes,
         in_specs=[vm] * 5 + [hbm] * 7,
         out_specs=[vm] * 5,
         scratch_shapes=[
@@ -674,9 +712,8 @@
             low(3, 256, 256), low(4, rows, model), low(4, 4, rows, width),
             pltpu.VMEM((8, 128), jnp.int32), pltpu.VMEM((8, 8, 128), jnp.int32),
             low(5, tok, width), low(5, tok, width), low(5, tok, width), low(5, 2, 4, 2, rows, width),
-            full(5, 8, tok), full(5, 8, tok), full(512, 128), full(512, 128), full(tok, 128), full(tok, 128),
-            full(tok, 128), pltpu.VMEM((tok, 128), jnp.int32),
-            low(2, 5, 512, tok), full(512, 128), full(tok, 128), full(tok, 128),
+            full(5, 8, tok), full(5, 8, tok), full(8, tok), full(8, tok), full(128, tok),
+            low(2, 5, 512, tok), full(128, tok), full(tok, 128), full(tok, 128),
             dma((8,)), dma((16,)), dma((16,)), dma((16,)), dma((16,)), dma((16,)), dma((16,)), dma((16,)), dma((16,)),
             dma((8,)), dma((8,)), dma((3,)), dma((3,)), dma((4,)), dma((4,)), dma((4,)), dma((4,)), dma((4,)),
             dma((5, 2)), dma((5, 2)), dma((5,)), dma((5,)), dma((5, 4)), dma((5, 4)),
@@ -687,7 +724,16 @@
         name="backward",
     )(hidden_rows, out_grad, jnp.transpose(picks, (2, 0, 1)), jnp.transpose(gates, (0, 2, 1)), doc_ids.reshape(8, 128),
       w_gate[0], w_up[0], w_down[0], w_out, q_heads, k_heads, v_heads)
-    return (d_queries, d_keys, d_values, d_hidden, d_gates[None])
+    d_hidden, d_gates, d_queries, d_keys, d_values = pl.pallas_call(
+        hand_over,
+        out_shape=shapes,
+        in_specs=[hbm] * 5,
+        out_specs=[hbm] * 5,
+        scratch_shapes=[pltpu.VMEM(shape.shape, BF) for shape in shapes] + [dma((10,))],
+        compiler_params=pltpu.CompilerParams(vmem_limit_bytes=60 * 2**20),
+        name="results",
+    )(*results)
+    return (d_queries, d_keys, d_values, d_hidden, jnp.transpose(d_gates, (0, 2, 1)))
 
 
 def solution(mesh):

time: 116 us -> 94.5 us (0.81)
  Pallas kernels: 107 us -> 93.4 us
  local copies, waits for them, and re-layouts: 8.01 us -> 0 us
    pallas_call x1 -> x2, Pallas kernels: 107 us -> 93.4 us  [the longest x1 91.4 us: per_device(): pl.pallas_call(kernel, out_shape=shapes, in_specs=[vm] * 5 + [hbm] * 7, o...]
    unnamed x4 -> x0, local copies, waits for them, and re-layouts: 6.67 us -> none
    pallas_call x1 -> x0, local copies, waits for them, and re-layouts: 1.34 us -> none  [per_device(): pl.pallas_call(kernel, out_shape=(out(rows, model), out(16, 6), out(tok,...]
where the time goes in v4:
time: 94.5 us; the launch traced here: 94.2 us
  Pallas kernels  93.4 us (99%)
    pallas_call x1, Pallas kernels, per_device(): pl.pallas_call(kernel, out_shape=shapes, in_specs=[vm] * 5 + [hbm] * 7, o...  91.4 us
    pallas_call x1, Pallas kernels, per_device(): pl.pallas_call(hand_over, out_shape=shapes, in_specs=[hbm] * 5, out_specs...  2 us

profile of v4, /device:TPU:3, one launch (start us, length us, event | category | flops | bytes accessed | tf_op | source)
XLA Modules:
  0.0 94.2 jit_solution(3038090763209174526)
XLA Ops:
  0.6 91.4 %backward.1 = (bf16[64,2048]{1,0:T(8,128)(2,1)}, bf16[1,6,16]{2,1,0:T(8,128)(2,1)}, bf16[1024,128]{1,0:T(8,128)(2,1)}, bf16[1024,128]{1,0:T(8,128)(2,1)}, bf16[1024,128]{1,0:T(8,128)(2,1)}) custom-call(bf16[64,2048]{1,0:T(8,128)(2,1)} %hidden.1, bf16[64,2048]{1,0:T(8,128)(2,1)} %grad.1, s32[6,1,16]{2,1,0:T(1,128)} %bitcast.11, bf16[1,6,16]{2,1,0:T(8,128)(2,1)} %bitcast.12, ...), custom_call_target="tpu_custom_call" | custom-call | tf_op jit(solution)/shard_map/backward/pallas_call | solution.py:701
  92.0 2.0 %results.1 = (bf16[64,2048]{1,0:T(8,128)(2,1)}, bf16[1,6,16]{2,1,0:T(8,128)(2,1)}, bf16[1024,128]{1,0:T(8,128)(2,1)}, bf16[1024,128]{1,0:T(8,128)(2,1)}, bf16[1024,128]{1,0:T(8,128)(2,1)}) custom-call(bf16[64,2048]{1,0:T(8,128)(2,1)} %get-tuple-element.15.refs_0_, bf16[1,6,16]{2,1,0:T(8,128)(2,1)} %get-tuple-element.16.refs_1_, ...), custom_call_target="tpu_custom_call" | custom-call | tf_op jit(solution)/shard_map/results/pallas_call | solution.py:727

commit v5 on v4

--- a/solution.py
+++ b/solution.py
@@ -93,10 +93,10 @@
 
 def kernel(hidden, grad, picks, gates, docs, wg, wu, wd, wo, qh, kh, vh,
            d_hidden, d_gates, dq_out, dk_out, dv_out,
-           wg_v, wu_v, wd_v, w4, sx, sg, rx, rg, x_v, g_v, a_v, b_v, da_v, db_v, dx_v,
+           wgu_v, wd_v, w4, sx, sg, rx, rg, x_v, g_v, a_v, b_v, da_v, db_v, dx_v,
            px, rr, dgs, dgr, selw, ag, d4, cnt, counts,
            q_win, k_win, v_win, do_win, lse_win, delta_win, top_v, sum_v, o_v,
-           pt_v, dq_v, dk_v, dv_v,
+           pt_v, tops_v, dq_v, dk_v, dv_v,
            local_sem, x_ss, x_rs, g_ss, g_rs, r_ss, r_rs, t_ss, t_rs, c_ss, c_rs,
            w_ss, w_rs, ag_ss, ag_rs, ex_ss, ex_rs, xs_ss, kv_ss, kv_rs, q_ss, q_rs, do_ss, do_rs,
            lse_ss, lse_rs, dl_ss, dl_rs):
@@ -112,6 +112,8 @@
     def peer(d):
         p = (e + d) % 16
         return p, ((c + 4 * ((p // 8 + xh) % 2)) % 8, p)
+
+    wg_v, wu_v = wgu_v.at[0], wgu_v.at[1]
 
     loads = [
         pltpu.make_async_copy(wg, wg_v, local_sem.at[0]),
@@ -150,6 +152,7 @@
     r = iota((256, 6), 0) % 16
     lane6 = iota((256, 6), 1)
     hid, gra = hidden[...], grad[...]
+    sels = []
     for j in range(3):
         slot, block = place_in_message(r, j)
         mine = lane6 == slot
@@ -159,21 +162,8 @@
         target = block[:, 0:1].astype(F32) * 64.0 + pick
         hit = iota((256, wide), 1).astype(F32) == target
         sel = hit.astype(BF)
+        sels.append((sel, target, gate, hit))
         sx[:, j * 256:(j + 1) * 256] = mm(sel, stacked(hid, j)).astype(BF)
-        sg[:, j * 256:(j + 1) * 256] = mm(sel, stacked(gra, j)).astype(BF)
-        if wide == 256:
-            hit_w = hit
-        else:
-            hit_w = iota((256, 256), 1).astype(F32) == target
-        selw[j] = jnp.transpose(jnp.where(hit_w, gate, 0.0)).astype(BF)
-    sizes = []
-    for d in range(8):
-        under_d = jnp.sum((docs[...] < d).astype(F32), axis=1, keepdims=True)
-        sizes.append(jnp.broadcast_to(jnp.sum(under_d, axis=0, keepdims=True), (1, 128)))
-    below = jnp.concatenate(sizes, axis=0).astype(jnp.int32)
-    cnt[...] = below
-    counts[c] = below
-
     pl.semaphore_wait(barrier, 15 + 3 + 7)
 
     def x_copy(d):
@@ -212,63 +202,69 @@
             return 0
         lax.fori_loop(n0, n1, one, 0)
 
+    def kv_copy(slot, device, relay=False, which=(0, 1)):
+        pairs = ((kh, k_win), (vh, v_win))
+        return [remote(pairs[i][1].at[4] if relay else pairs[i][0], pairs[i][1].at[slot], kv_ss.at[slot, i],
+                       kv_rs.at[slot, i], device) for i in which]
+
+    def q_copy(slot, device, relay=False):
+        return [remote(q_win.at[4] if relay else qh, q_win.at[slot], q_ss.at[slot], q_rs.at[slot], device)]
+
+    def to_half(act):
+        @pl.when(xl == 0)
+        def _():
+            act(kv_copy(4, (across, e)))
+
+        @pl.when(xl == 1)
+        def _():
+            act(q_copy(4, (across, e)))
+
+    def to_row(act):
+        for o in range(1, 4):
+            yo = (y + o) % 4
+
+            @pl.when(yo > y)
+            def _():
+                act(kv_copy(yo - y, (xl * 4 + yo, e)))
+
+            @pl.when(yo < y)
+            def _():
+                act(q_copy(y - yo, (xl * 4 + yo, e)))
+
+    def relay_row(act, which):
+        for o in range(1, 4):
+            yo = (y + o) % 4
+
+            @pl.when((xl == 1) & (yo < y))
+            def _():
+                act(kv_copy(4 + yo - y, (xl * 4 + yo, e), True, (which,)))
+
+            if which == 0:
+                @pl.when((xl == 0) & (yo > y))
+                def _():
+                    act(q_copy(4 + y - yo, (xl * 4 + yo, e), True))
+
+    def start(copies):
+        for copy in copies:
+            copy.start()
+
+    def sent(copies):
+        for copy in copies:
+            copy.wait_send()
+
+    def received(copies):
+        for copy in copies:
+            copy.wait_recv()
+
     each(1, 16, lambda d: x_copy(d).start())
+    to_half(start)
+    for j in range(3):
+        sg[:, j * 256:(j + 1) * 256] = mm(sels[j][0], stacked(gra, j)).astype(BF)
     each(1, 16, lambda d: g_copy(d).start())
+    to_row(start)
     own16 = pl.ds(pl.multiple_of(e * 16, 16), 16)
     rx[own16, :] = sx[own16, :]
     rg[own16, :] = sg[own16, :]
-
-    def kv_copy(slot, device, relay=False):
-        return [remote(win.at[4] if relay else src, win.at[slot], kv_ss.at[slot, i], kv_rs.at[slot, i], device)
-                for i, (src, win) in enumerate(((kh, k_win), (vh, v_win)))]
-
-    def q_copy(slot, device, relay=False):
-        return [remote(q_win.at[4] if relay else qh, q_win.at[slot], q_ss.at[slot], q_rs.at[slot], device)]
-
-    def to_row(act):
-        @pl.when(xl == 0)
-        def _():
-            act(kv_copy(4, (across, e)))
-
-        @pl.when(xl == 1)
-        def _():
-            act(q_copy(4, (across, e)))
-        for o in range(1, 4):
-            yo = (y + o) % 4
-
-            @pl.when(yo > y)
-            def _():
-                act(kv_copy(yo - y, (xl * 4 + yo, e)))
-
-            @pl.when(yo < y)
-            def _():
-                act(q_copy(y - yo, (xl * 4 + yo, e)))
-
-    def relay_row(act):
-        for o in range(1, 4):
-            yo = (y + o) % 4
-
-            @pl.when((xl == 1) & (yo < y))
-            def _():
-                act(kv_copy(4 + yo - y, (xl * 4 + yo, e), True))
-
-            @pl.when((xl == 0) & (yo > y))
-            def _():
-                act(q_copy(4 + y - yo, (xl * 4 + yo, e), True))
-
-    def start(copies):
-        for copy in copies:
-            copy.start()
-
-    def sent(copies):
-        for copy in copies:
-            copy.wait_send()
-
-    def received(copies):
-        for copy in copies:
-            copy.wait_recv()
-
-    to_row(start)
 
     mate = (c, exp_at(xh, z, 1 - k))
     facing = (across, exp_at(1 - xh, z, k))
@@ -278,8 +274,29 @@
     w_facing = remote(wo, w4.at[own_q], w_ss.at[1], w_rs.at[1], facing)
     w_relay = remote(w4.at[far_q], w4.at[far_q], w_ss.at[2], w_rs.at[2], mate)
     w_mate.start()
-    w_facing.start()
+
+    sizes = []
+    for d in range(8):
+        under_d = jnp.sum((docs[...] < d).astype(F32), axis=1, keepdims=True)
+        sizes.append(jnp.broadcast_to(jnp.sum(under_d, axis=0, keepdims=True), (1, 128)))
+    below = jnp.concatenate(sizes, axis=0).astype(jnp.int32)
+    cnt[...] = below
+    counts[c] = below
     each(1, 8, lambda o: c_copy(o).start())
+    for j in range(3):
+        _, target, gate, hit = sels[j]
+        if hit.shape[1] < 256:
+            hit = iota((256, 256), 1).astype(F32) == target
+        selw[j] = jnp.transpose(jnp.where(hit, gate, 0.0)).astype(BF)
+
+    @pl.when(xl == 1)
+    def _():
+        received(kv_copy(4, (across, e), which=(0,)))
+
+    @pl.when(xl == 0)
+    def _():
+        received(q_copy(4, (across, e)))
+    relay_row(start, 0)
 
     recv(rx, x_rs)
     for col in range(8):
@@ -301,7 +318,13 @@
     lax.fori_loop(0, whole, up_step, 0)
     if ff % FC:
         up(whole * FC, ff % FC)
+
+    @pl.when(xl == 1)
+    def _():
+        received(kv_copy(4, (across, e), which=(1,)))
+    relay_row(start, 1)
     recv(rg, g_rs)
+    w_facing.start()
     for col in range(8):
         g_v[:, col * 256:(col + 1) * 256] = unpack(rg[...], col)
     loads[2].wait()
@@ -322,15 +345,6 @@
     acc = lax.fori_loop(0, whole, down_step, jnp.zeros((96, 128), F32))
     if ff % FC:
         acc = down(whole * FC, ff % FC, acc)
-
-    @pl.when(xl == 1)
-    def _():
-        received(kv_copy(4, (across, e)))
-
-    @pl.when(xl == 0)
-    def _():
-        received(q_copy(4, (across, e)))
-    relay_row(start)
 
     def back_step(i, _):
         cols = pl.ds(pl.multiple_of(i * FC, FC), FC)
@@ -383,6 +397,11 @@
         if isinstance(d, int):
             return range(t + 1) if d == 0 else range(t, 2)
         return range(2)
+
+    def kept_probs(d, first, n, cols):
+        if isinstance(d, int) and d == 0:
+            return wd_v.at[first:first + n, cols]
+        return wgu_v.at[(d - 1) // 2, pl.ds(pl.multiple_of((d - 1) % 2 * 1024 + first, 512), n), cols]
 
     top_v[...] = jnp.full((8, 1024), NEG, F32)
     sum_v[...] = jnp.zeros((8, 1024), F32)
@@ -400,6 +419,9 @@
             fade = jnp.exp2(old - new)
             probs = [jnp.exp2(s - new[0:1]) for s in scores]
             top_v[:, cols] = new
+            tops_v[d, :, cols] = new
+            for h, p in zip(halves, probs):
+                kept_probs(d, h * 512, 512, cols)[...] = p.astype(BF)
             sum_v[:, cols] = sum_v[:, cols] * fade + sum(over_rows(p, jnp.add) for p in probs)
             o_v[:, cols] = o_v[:, cols] * fade[0:1] + sum(
                 mm(jnp.transpose(v_win[d, half(h), :]), p.astype(BF)) for h, p in zip(halves, probs))
@@ -558,11 +580,10 @@
         piece_copy(i).wait_recv()
         along(i, lambda copy: copy.start())
 
-    @pl.when(xl == 0)
-    def _():
-        for i in range(4):
+    for i in range(4):
+        @pl.when(xl == 0)
+        def _():
             piece_across(i).wait_recv()
-    for i in range(4):
         along_relay(i, lambda copy: copy.start())
 
     d_own = do_win[0].reshape(1024, 128)
@@ -584,15 +605,16 @@
     def query_grads(d):
         for t in range(2):
             cols = half(t)
-            q = q_win[0, cols, :]
             do = d_own[cols, :]
             acc = dq_v[:, cols]
-            for h in key_halves(t, d):
-                keys = k_win[d, half(h), :]
-                p = jnp.exp2(nt(keys, q) * SCALE2 - lse_win[0, 0:1, cols])
-                p = jnp.where(seen(t, d, h), p, 0.0)
-                ds = p * (nt(v_win[d, half(h), :], do) - delta_win[0, 0:1, cols])
-                acc = acc + mm(jnp.transpose(keys), ds.astype(BF))
+            fade = jnp.exp2(tops_v[d, 0:1, cols] - lse_win[0, 0:1, cols])
+            faded_delta = delta_win[0, 0:1, cols] * fade
+            halves = key_halves(t, d)
+            rows = slice(halves[0] * 512, halves[-1] * 512 + 512)
+            dp = nt(v_win[d, rows, :], do)
+            kept = kept_probs(d, rows.start, rows.stop - rows.start, cols)[...]
+            ds = kept.astype(F32) * (dp * fade - faded_delta)
+            acc = acc + mm(jnp.transpose(k_win[d, rows, :]), ds.astype(BF))
             dq_v[:, cols] = acc
 
     def query_step(d, _):
@@ -651,8 +673,10 @@
     each(1, 8, lambda o: c_copy(o).wait_send())
     for copy in [w_mate, w_facing, w_relay, g_up, g_down, g_up2, g_down2]:
         copy.wait_send()
+    to_half(sent)
     to_row(sent)
-    relay_row(sent)
+    relay_row(sent, 0)
+    relay_row(sent, 1)
     before(lambda d: row_copy(lse_win, lse_ss, lse_rs, d).wait_send())
     before(lambda d: row_copy(delta_win, dl_ss, dl_rs, d).wait_send())
     for i in range(1, 4):
@@ -704,7 +728,7 @@
         in_specs=[vm] * 5 + [hbm] * 7,
         out_specs=[vm] * 5,
         scratch_shapes=[
-            low(model, ff), low(model, ff), low(ff, model), low(4, 128, model),
+            low(2, model, ff), low(ff, model), low(4, 128, model),
             low(256, 768), low(256, 768), low(256, 768), low(256, 768),
             low(96, model), low(96, model), full(96, ff), full(96, ff),
             low(96, ff), low(96, ff), low(96, model),
@@ -713,7 +737,7 @@
             pltpu.VMEM((8, 128), jnp.int32), pltpu.VMEM((8, 8, 128), jnp.int32),
             low(5, tok, width), low(5, tok, width), low(5, tok, width), low(5, 2, 4, 2, rows, width),
             full(5, 8, tok), full(5, 8, tok), full(8, tok), full(8, tok), full(128, tok),
-            low(2, 5, 512, tok), full(128, tok), full(tok, 128), full(tok, 128),
+            low(2, 5, 512, tok), full(5, 8, tok), full(128, tok), full(tok, 128), full(tok, 128),
             dma((8,)), dma((16,)), dma((16,)), dma((16,)), dma((16,)), dma((16,)), dma((16,)), dma((16,)), dma((16,)),
             dma((8,)), dma((8,)), dma((3,)), dma((3,)), dma((4,)), dma((4,)), dma((4,)), dma((4,)), dma((4,)),
             dma((5, 2)), dma((5, 2)), dma((5,)), dma((5,)), dma((5, 4)), dma((5, 4)),

time: 94.5 us -> 89.3 us (0.945)
  the two profiles are of different devices: /device:TPU:3 before, /device:TPU:25 now
where the time goes in v5:
time: 89.3 us; the launch traced here: 89.2 us
  Pallas kernels  88.3 us (99%)
    pallas_call x1, Pallas kernels, per_device(): pl.pallas_call(kernel, out_shape=shapes, in_specs=[vm] * 5 + [hbm] * 7, o...  86.3 us
    pallas_call x1, Pallas kernels, per_device(): pl.pallas_call(hand_over, out_shape=shapes, in_specs=[hbm] * 5, out_specs...  2 us

profile of v5, /device:TPU:25, one launch (start us, length us, event | category | flops | bytes accessed | tf_op | source)
XLA Modules:
  0.0 89.2 jit_solution(10107178906871085615)
XLA Ops:
  0.6 86.3 %backward.1 = (bf16[64,2048]{1,0:T(8,128)(2,1)}, bf16[1,6,16]{2,1,0:T(8,128)(2,1)}, bf16[1024,128]{1,0:T(8,128)(2,1)}, bf16[1024,128]{1,0:T(8,128)(2,1)}, bf16[1024,128]{1,0:T(8,128)(2,1)}) custom-call(bf16[64,2048]{1,0:T(8,128)(2,1)} %hidden.1, bf16[64,2048]{1,0:T(8,128)(2,1)} %grad.1, s32[6,1,16]{2,1,0:T(1,128)} %bitcast.11, bf16[1,6,16]{2,1,0:T(8,128)(2,1)} %bitcast.12, ...), custom_call_target="tpu_custom_call" | custom-call | tf_op jit(solution)/shard_map/backward/pallas_call | solution.py:725
  87.0 2.0 %results.1 = (bf16[64,2048]{1,0:T(8,128)(2,1)}, bf16[1,6,16]{2,1,0:T(8,128)(2,1)}, bf16[1024,128]{1,0:T(8,128)(2,1)}, bf16[1024,128]{1,0:T(8,128)(2,1)}, bf16[1024,128]{1,0:T(8,128)(2,1)}) custom-call(bf16[64,2048]{1,0:T(8,128)(2,1)} %get-tuple-element.15.refs_0_, bf16[1,6,16]{2,1,0:T(8,128)(2,1)} %get-tuple-element.16.refs_1_, ...), custom_call_target="tpu_custom_call" | custom-call | tf_op jit(solution)/shard_map/results/pallas_call | solution.py:751

commit v6 on v5

--- a/solution.py
+++ b/solution.py
@@ -309,15 +309,10 @@
         a_v[:, cols] = mm(x_v[...], wg_v[:, cols])
         b_v[:, cols] = mm(x_v[...], wu_v[:, cols])
 
-    def up_step(i, _):
-        up(pl.multiple_of(i * FC, FC), FC)
-        return 0
-
     ff = wg.shape[1]
-    whole = ff // FC
-    lax.fori_loop(0, whole, up_step, 0)
-    if ff % FC:
-        up(whole * FC, ff % FC)
+    chunks = [(f0, min(FC, ff - f0)) for f0 in range(0, ff, FC)]
+    for f0, n in chunks:
+        up(f0, n)
 
     @pl.when(xl == 1)
     def _():
@@ -339,19 +334,13 @@
         db_v[:, cols] = (u * act).astype(BF)
         return acc + fold(act * b * u, jnp.add)
 
-    def down_step(i, acc):
-        return down(pl.multiple_of(i * FC, FC), FC, acc)
-
-    acc = lax.fori_loop(0, whole, down_step, jnp.zeros((96, 128), F32))
-    if ff % FC:
-        acc = down(whole * FC, ff % FC, acc)
-
-    def back_step(i, _):
-        cols = pl.ds(pl.multiple_of(i * FC, FC), FC)
+    acc = jnp.zeros((96, 128), F32)
+    for f0, n in chunks:
+        acc = down(f0, n, acc)
+
+    for d0 in range(0, wg.shape[0], FC):
+        cols = pl.ds(d0, FC)
         dx_v[:, cols] = (nt(da_v[...], wg_v[cols, :]) + nt(db_v[...], wu_v[cols, :])).astype(BF)
-        return 0
-
-    lax.fori_loop(0, wg.shape[0] // FC, back_step, 0)
     for j in range(3):
         px[:, j * 256:(j + 1) * 256] = mm(pack_weights(j, 96), stacked(dx_v[...], j)).astype(BF)
     each(1, 16, lambda d: r_copy(d).start())
@@ -461,41 +450,11 @@
     g_up.start()
     g_down.start()
 
-    middle = jnp.minimum(direct + 3, last_before + 1)
-    lax.fori_loop(direct + 1, middle, statistics_step, 0)
-    g_up.wait_recv()
-    g_up2.start()
-    g_down.wait_recv()
-    g_down2.start()
-    lax.fori_loop(middle, last_before + 1, statistics_step, 0)
-    norm = jnp.sum(sum_v[...], axis=0, keepdims=True)
-    lse_win[0] = top_v[...] + jnp.log(norm) * math.log2(math.e)
-
-    def row_copy(win, ss, rs, d):
-        return remote(win.at[0], win.at[d], ss.at[d], rs.at[d], ((c + 8 - d) % 8, e))
-
-    def before(act):
-        for d in range(1, 5):
-            @pl.when(c >= d)
-            def _():
-                act(d)
-
-    def later(act):
-        for d in range(1, 5):
-            @pl.when(c + d <= 7)
-            def _():
-                act(d)
-
-    before(lambda d: row_copy(lse_win, lse_ss, lse_rs, d).start())
     loads[3].wait()
     w_mate.wait_recv()
     w_relay.wait_recv()
-    g_up2.wait_recv()
-    g_down2.wait_recv()
-
-    tokens = ag[...].reshape(256, ag.shape[2])
-    for q_ in range(4):
-        d4[q_] = nt(tokens, w4[q_]).astype(BF).reshape(4, 64, 128)
+    sets = ((0, 1), (1, 2), (3, 1))
+    order = (z, z_up, z_down, (z + 2) % 4)
     pieces = [
         (own_q, e, (xh, k)),
         (mate_q, exp_at(xh, z, 1 - k), (xh, 1 - k)),
@@ -503,44 +462,107 @@
         (far_mate_q, exp_at(1 - xh, z, 1 - k), (1 - xh, 1 - k)),
     ]
 
-    def piece_copy(i):
+    def piece_copy(g, i):
         q_, head, _ = pieces[i]
-        return remote(d4.at[q_], do_win.at[0, xh, :, k], ex_ss.at[i], ex_rs.at[i], (c, head))
-
-    def piece_across(i):
+        part = pl.ds(*sets[g])
+        return remote(d4.at[q_, part], do_win.at[0, xh, part, k], ex_ss.at[g, i], ex_rs.at[g, i], (c, head))
+
+    def piece_across(g, i):
         q_, head, _ = pieces[i]
-        return remote(d4.at[q_], do_win.at[4, xh, :, k], xs_ss.at[i], do_rs.at[4, i], (across, head))
-
-    def piece_along(i, slot, yo, src):
+        part = pl.ds(*sets[g])
+        return remote(d4.at[q_, part], do_win.at[4, xh, part, k], xs_ss.at[g, i], do_rs.at[g, 4, i], (across, head))
+
+    def piece_along(g, i, slot, yo, src):
         _, _, (xs, ks) = pieces[i]
-        return remote(do_win.at[src, xs, :, ks], do_win.at[slot, xs, :, ks], do_ss.at[slot, i], do_rs.at[slot, i],
-                      (xl * 4 + yo, e))
-
-    def along(i, act):
-        for o in range(1, 4):
+        part = pl.ds(*sets[g])
+        return remote(do_win.at[src, xs, part, ks], do_win.at[slot, xs, part, ks], do_ss.at[g, slot, i],
+                      do_rs.at[g, slot, i], (xl * 4 + yo, e))
+
+    def along(g, i, act):
+        for o in (1, 3, 2):
             yo = (y + o) % 4
 
             @pl.when(yo < y)
             def _():
-                act(piece_along(i, y - yo, yo, 0))
-
-    def along_relay(i, act):
-        for o in range(1, 4):
+                act(piece_along(g, i, y - yo, yo, 0))
+
+    def along_relay(g, i, act):
+        for o in (1, 3, 2):
             yo = (y + o) % 4
 
             @pl.when((xl == 0) & (yo > y))
             def _():
-                act(piece_along(i, 4 + y - yo, yo, 4))
-
-    for i in (2, 3, 1):
-        piece_copy(i).start()
-
-    @pl.when(xl == 1)
-    def _():
-        for i in (2, 3, 1, 0):
-            piece_across(i).start()
-    do_win[0, xh, :, k] = d4[own_q]
-    along(0, lambda copy: copy.start())
+                act(piece_along(g, i, 4 + y - yo, yo, 4))
+
+    def begin(copy):
+        copy.start()
+
+    def project(g):
+        first_of, n = sets[g]
+        tokens = jnp.concatenate([ag[order[first_of + i]] for i in range(n)], axis=0)
+        flat = nt(tokens, w4[...].reshape(512, ag.shape[2])).astype(BF)
+        part = slice(first_of, first_of + n)
+        for q_ in range(4):
+            d4[q_, part] = flat[:, q_ * 128:(q_ + 1) * 128].reshape(n, 64, 128)
+        for i in (2, 3, 1):
+            piece_copy(g, i).start()
+
+        @pl.when(xl == 1)
+        def _():
+            for i in (2, 3, 1, 0):
+                piece_across(g, i).start()
+        do_win[0, xh, part, k] = d4[own_q, part]
+        along(g, 0, begin)
+
+    def pass_on(g):
+        for i in (1, 2, 3):
+            piece_copy(g, i).wait_recv()
+            along(g, i, begin)
+
+    def pass_across(g):
+        for i in range(4):
+            @pl.when(xl == 0)
+            def _():
+                piece_across(g, i).wait_recv()
+            along_relay(g, i, begin)
+
+    def gradient_rows(d):
+        halves = []
+        for xs in range(2):
+            for z_ in range(4):
+                away = (z_ + 4 - z) % 4
+                halves.append(do_win[d, xs, away + away // 2 - 2 * (away // 3)].reshape(128, 128))
+        return jnp.concatenate(halves, axis=0)
+
+    def row_copy(win, ss, rs, d):
+        return remote(win.at[0], win.at[d], ss.at[d], rs.at[d], ((c + 8 - d) % 8, e))
+
+    def before(act):
+        for d in range(1, 5):
+            @pl.when(c >= d)
+            def _():
+                act(d)
+
+    def later(act):
+        for d in range(1, 5):
+            @pl.when(c + d <= 7)
+            def _():
+                act(d)
+
+    project(0)
+    middle = jnp.minimum(direct + 3, last_before + 1)
+    lax.fori_loop(direct + 1, middle, statistics_step, 0)
+    pass_on(0)
+    g_up.wait_recv()
+    g_up2.start()
+    g_down.wait_recv()
+    g_down2.start()
+    project(1)
+    pass_across(0)
+    lax.fori_loop(middle, last_before + 1, statistics_step, 0)
+    norm = jnp.sum(sum_v[...], axis=0, keepdims=True)
+    lse_win[0] = top_v[...] + jnp.log(norm) * math.log2(math.e)
+    before(lambda d: row_copy(lse_win, lse_ss, lse_rs, d).start())
 
     def key_probs(t, d, halves, masked):
         key = c * 1024 + t * 512 + iota((512, 512), 0)
@@ -573,20 +595,16 @@
 
     last_after = jnp.minimum(7 - c, 3)
     query_tiles(0, lambda t, d, halves: key_probs(t, d, halves, True))
-    piece_copy(1).wait_recv()
-    along(1, lambda copy: copy.start())
+    pass_on(1)
+    g_up2.wait_recv()
+    g_down2.wait_recv()
+    project(2)
+    pass_across(1)
     lax.fori_loop(1, jnp.minimum(last_after, 1) + 1, probs_step, 0)
-    for i in (2, 3):
-        piece_copy(i).wait_recv()
-        along(i, lambda copy: copy.start())
-
-    for i in range(4):
-        @pl.when(xl == 0)
-        def _():
-            piece_across(i).wait_recv()
-        along_relay(i, lambda copy: copy.start())
-
-    d_own = do_win[0].reshape(1024, 128)
+    pass_on(2)
+    pass_across(2)
+
+    d_own = gradient_rows(0)
     prod = d_own.astype(F32) * jnp.transpose(o_v[...] / norm)
     high = prod.astype(BF)
     low_part = (prod - high.astype(F32)).astype(BF)
@@ -634,7 +652,7 @@
 
     def key_grads(t, d, halves):
         rows = half(t)
-        do_all = do_win[d].reshape(1024, 128)
+        do_all = gradient_rows(d)
         cols = slice(halves[0] * 512, halves[-1] * 512 + 512)
         do = do_all[cols, :]
         p = pt_v[t, d, :, cols]
@@ -644,19 +662,25 @@
 
     query_tiles(0, key_grads)
 
-    def grads_step(d, _):
-        for i in range(4):
-            piece_along(i, d, y, 0).wait_recv()
-        row_copy(delta_win, dl_ss, dl_rs, d).wait_recv()
-        query_tiles(1, lambda t, _, halves: key_grads(t, d, halves))
+    def grads_step(n, _):
+        d = 1 + 2 * n - 3 * (n // 2)
+
+        @pl.when(d <= last_after)
+        def _():
+            for g in range(3):
+                for i in range(4):
+                    piece_along(g, i, d, y, 0).wait_recv()
+            row_copy(delta_win, dl_ss, dl_rs, d).wait_recv()
+            query_tiles(1, lambda t, _, halves: key_grads(t, d, halves))
         return 0
-
-    lax.fori_loop(1, last_after + 1, grads_step, 0)
 
     @pl.when(xl == 0)
     def _():
         row_copy(delta_win, dl_ss, dl_rs, 4).wait_recv()
         query_tiles(4, key_grads)
+
+    lax.fori_loop(0, 3, grads_step, 0)
+
     dk_out[...] = (dk_v[...] * SCALE).astype(BF)
     dv_out[...] = dv_v[...].astype(BF)
 
@@ -679,16 +703,17 @@
     relay_row(sent, 1)
     before(lambda d: row_copy(lse_win, lse_ss, lse_rs, d).wait_send())
     before(lambda d: row_copy(delta_win, dl_ss, dl_rs, d).wait_send())
-    for i in range(1, 4):
-        piece_copy(i).wait_send()
-
-    @pl.when(xl == 1)
-    def _():
+    for g in range(3):
+        for i in range(1, 4):
+            piece_copy(g, i).wait_send()
+
+        @pl.when(xl == 1)
+        def _():
+            for i in range(4):
+                piece_across(g, i).wait_send()
         for i in range(4):
-            piece_across(i).wait_send()
-    for i in range(4):
-        along(i, lambda copy: copy.wait_send())
-        along_relay(i, lambda copy: copy.wait_send())
+            along(g, i, lambda copy: copy.wait_send())
+            along_relay(g, i, lambda copy: copy.wait_send())
 
 
 def hand_over(*refs):
@@ -739,8 +764,8 @@
             full(5, 8, tok), full(5, 8, tok), full(8, tok), full(8, tok), full(128, tok),
             low(2, 5, 512, tok), full(5, 8, tok), full(128, tok), full(tok, 128), full(tok, 128),
             dma((8,)), dma((16,)), dma((16,)), dma((16,)), dma((16,)), dma((16,)), dma((16,)), dma((16,)), dma((16,)),
-            dma((8,)), dma((8,)), dma((3,)), dma((3,)), dma((4,)), dma((4,)), dma((4,)), dma((4,)), dma((4,)),
-            dma((5, 2)), dma((5, 2)), dma((5,)), dma((5,)), dma((5, 4)), dma((5, 4)),
+            dma((8,)), dma((8,)), dma((3,)), dma((3,)), dma((4,)), dma((4,)), dma((3, 4)), dma((3, 4)), dma((3, 4)),
+            dma((5, 2)), dma((5, 2)), dma((5,)), dma((5,)), dma((3, 5, 4)), dma((3, 5, 4)),
             dma((5,)), dma((5,)), dma((5,)), dma((5,)),
         ],
         compiler_params=pltpu.CompilerParams(

time: 89.3 us -> 85 us (0.952)
  the two profiles are of different devices: /device:TPU:25 before, /device:TPU:3 now
where the time goes in v6:
time: 85 us; the launch traced here: 84.7 us
  Pallas kernels  83.9 us (99%)
    pallas_call x1, Pallas kernels, per_device(): pl.pallas_call(kernel, out_shape=shapes, in_specs=[vm] * 5 + [hbm] * 7, o...  81.9 us
    pallas_call x1, Pallas kernels, per_device(): pl.pallas_call(hand_over, out_shape=shapes, in_specs=[hbm] * 5, out_specs...  2 us

profile of v6, /device:TPU:3, one launch (start us, length us, event | category | flops | bytes accessed | tf_op | source)
XLA Modules:
  0.0 84.7 jit_solution(14850415446673596140)
XLA Ops:
  0.6 81.9 %backward.1 = (bf16[64,2048]{1,0:T(8,128)(2,1)}, bf16[1,6,16]{2,1,0:T(8,128)(2,1)}, bf16[1024,128]{1,0:T(8,128)(2,1)}, bf16[1024,128]{1,0:T(8,128)(2,1)}, bf16[1024,128]{1,0:T(8,128)(2,1)}) custom-call(bf16[64,2048]{1,0:T(8,128)(2,1)} %hidden.1, bf16[64,2048]{1,0:T(8,128)(2,1)} %grad.1, s32[6,1,16]{2,1,0:T(1,128)} %bitcast.11, bf16[1,6,16]{2,1,0:T(8,128)(2,1)} %bitcast.12, ...), custom_call_target="tpu_custom_call" | custom-call | tf_op jit(solution)/shard_map/backward/pallas_call | solution.py:750
  82.5 2.0 %results.1 = (bf16[64,2048]{1,0:T(8,128)(2,1)}, bf16[1,6,16]{2,1,0:T(8,128)(2,1)}, bf16[1024,128]{1,0:T(8,128)(2,1)}, bf16[1024,128]{1,0:T(8,128)(2,1)}, bf16[1024,128]{1,0:T(8,128)(2,1)}) custom-call(bf16[64,2048]{1,0:T(8,128)(2,1)} %get-tuple-element.15.refs_0_, bf16[1,6,16]{2,1,0:T(8,128)(2,1)} %get-tuple-element.16.refs_1_, ...), custom_call_target="tpu_custom_call" | custom-call | tf_op jit(solution)/shard_map/results/pallas_call | solution.py:776

commit v7 on v6

--- a/solution.py
+++ b/solution.py
@@ -397,6 +397,7 @@
     o_v[...] = jnp.zeros((128, 1024), F32)
 
     def statistics(d):
+        flipped = [jnp.transpose(v_win[d, half(h), :]) for h in range(2)]
         for t in range(2):
             cols = half(t)
             halves = key_halves(t, d)
@@ -413,7 +414,7 @@
                 kept_probs(d, h * 512, 512, cols)[...] = p.astype(BF)
             sum_v[:, cols] = sum_v[:, cols] * fade + sum(over_rows(p, jnp.add) for p in probs)
             o_v[:, cols] = o_v[:, cols] * fade[0:1] + sum(
-                mm(jnp.transpose(v_win[d, half(h), :]), p.astype(BF)) for h, p in zip(halves, probs))
+                mm(flipped[h], p.astype(BF)) for h, p in zip(halves, probs))
 
     def statistics_step(d, _):
         received(kv_copy(d, (c, e)))
@@ -587,10 +588,22 @@
             act(0, d, range(2))
             act(1, d, range(2))
 
-    def probs_step(d, _):
-        received(q_copy(d, (c, e)))
-        row_copy(lse_win, lse_ss, lse_rs, d).wait_recv()
-        query_tiles(1, lambda t, _, halves: key_probs(t, d, halves, False))
+    def nth(n):
+        return jnp.where(n < 3 - y, n + 1, 7 - y - n)
+
+    def probs_step(n, _):
+        d = nth(n)
+
+        @pl.when(d <= last_after)
+        def _():
+            received(q_copy(d, (c, e)))
+            row_copy(lse_win, lse_ss, lse_rs, d).wait_recv()
+            query_tiles(1, lambda t, _, halves: key_probs(t, d, halves, False))
+
+        @pl.when((d == 4) & (xl == 0))
+        def _():
+            row_copy(lse_win, lse_ss, lse_rs, 4).wait_recv()
+            query_tiles(4, lambda t, d, halves: key_probs(t, d, halves, False))
         return 0
 
     last_after = jnp.minimum(7 - c, 3)
@@ -600,7 +613,7 @@
     g_down2.wait_recv()
     project(2)
     pass_across(1)
-    lax.fori_loop(1, jnp.minimum(last_after, 1) + 1, probs_step, 0)
+    lax.fori_loop(0, 1, probs_step, 0)
     pass_on(2)
     pass_across(2)
 
@@ -611,16 +624,12 @@
     ones = jnp.ones((8, 128), BF)
     delta_win[0] = nt(ones, high) + nt(ones, low_part)
     before(lambda d: row_copy(delta_win, dl_ss, dl_rs, d).start())
-    lax.fori_loop(2, last_after + 1, probs_step, 0)
-
-    @pl.when(xl == 0)
-    def _():
-        row_copy(lse_win, lse_ss, lse_rs, 4).wait_recv()
-        query_tiles(4, lambda t, d, halves: key_probs(t, d, halves, False))
+    lax.fori_loop(1, 4, probs_step, 0)
 
     dq_v[...] = jnp.zeros((128, 1024), F32)
 
     def query_grads(d):
+        flipped = jnp.transpose(k_win[d])
         for t in range(2):
             cols = half(t)
             do = d_own[cols, :]
@@ -632,7 +641,7 @@
             dp = nt(v_win[d, rows, :], do)
             kept = kept_probs(d, rows.start, rows.stop - rows.start, cols)[...]
             ds = kept.astype(F32) * (dp * fade - faded_delta)
-            acc = acc + mm(jnp.transpose(k_win[d, rows, :]), ds.astype(BF))
+            acc = acc + mm(flipped[:, rows], ds.astype(BF))
             dq_v[:, cols] = acc
 
     def query_step(d, _):
@@ -650,9 +659,8 @@
     dk_v[...] = jnp.zeros((1024, 128), F32)
     dv_v[...] = jnp.zeros((1024, 128), F32)
 
-    def key_grads(t, d, halves):
+    def key_grads(t, d, halves, do_all):
         rows = half(t)
-        do_all = gradient_rows(d)
         cols = slice(halves[0] * 512, halves[-1] * 512 + 512)
         do = do_all[cols, :]
         p = pt_v[t, d, :, cols]
@@ -660,10 +668,10 @@
         ds = p.astype(F32) * (nt(v_win[0, rows, :], do) - delta_win[d, 0:1, cols])
         dk_v[rows, :] += mm(ds.astype(BF), q_win[d, cols, :])
 
-    query_tiles(0, key_grads)
+    query_tiles(0, functools.partial(key_grads, do_all=d_own))
 
     def grads_step(n, _):
-        d = 1 + 2 * n - 3 * (n // 2)
+        d = nth(n)
 
         @pl.when(d <= last_after)
         def _():
@@ -671,16 +679,16 @@
                 for i in range(4):
                     piece_along(g, i, d, y, 0).wait_recv()
             row_copy(delta_win, dl_ss, dl_rs, d).wait_recv()
-            query_tiles(1, lambda t, _, halves: key_grads(t, d, halves))
+            do_all = gradient_rows(d)
+            query_tiles(1, lambda t, _, halves: key_grads(t, d, halves, do_all))
+
+        @pl.when((d == 4) & (xl == 0))
+        def _():
+            row_copy(delta_win, dl_ss, dl_rs, 4).wait_recv()
+            query_tiles(4, functools.partial(key_grads, do_all=gradient_rows(4)))
         return 0
 
-    @pl.when(xl == 0)
-    def _():
-        row_copy(delta_win, dl_ss, dl_rs, 4).wait_recv()
-        query_tiles(4, key_grads)
-
-    lax.fori_loop(0, 3, grads_step, 0)
-
+    lax.fori_loop(0, 4, grads_step, 0)
     dk_out[...] = (dk_v[...] * SCALE).astype(BF)
     dv_out[...] = dv_v[...].astype(BF)
 

time: 85 us -> 85 us (level)
  no operation moved by 1% of the time
where the time goes in v7:
time: 85 us; the launch traced here: 84.5 us
  Pallas kernels  83.7 us (98%)
    pallas_call x1, Pallas kernels, per_device(): pl.pallas_call(kernel, out_shape=shapes, in_specs=[vm] * 5 + [hbm] * 7, o...  81.7 us
    pallas_call x1, Pallas kernels, per_device(): pl.pallas_call(hand_over, out_shape=shapes, in_specs=[hbm] * 5, out_specs...  2 us

profile of v7, /device:TPU:3, one launch (start us, length us, event | category | flops | bytes accessed | tf_op | source)
XLA Modules:
  0.0 84.5 jit_solution(135129581775048910)
XLA Ops:
  0.6 81.7 %backward.1 = (bf16[64,2048]{1,0:T(8,128)(2,1)}, bf16[1,6,16]{2,1,0:T(8,128)(2,1)}, bf16[1024,128]{1,0:T(8,128)(2,1)}, bf16[1024,128]{1,0:T(8,128)(2,1)}, bf16[1024,128]{1,0:T(8,128)(2,1)}) custom-call(bf16[64,2048]{1,0:T(8,128)(2,1)} %hidden.1, bf16[64,2048]{1,0:T(8,128)(2,1)} %grad.1, s32[6,1,16]{2,1,0:T(1,128)} %bitcast.11, bf16[1,6,16]{2,1,0:T(8,128)(2,1)} %bitcast.12, ...), custom_call_target="tpu_custom_call" | custom-call | tf_op jit(solution)/shard_map/backward/pallas_call | solution.py:758
  82.3 2.0 %results.1 = (bf16[64,2048]{1,0:T(8,128)(2,1)}, bf16[1,6,16]{2,1,0:T(8,128)(2,1)}, bf16[1024,128]{1,0:T(8,128)(2,1)}, bf16[1024,128]{1,0:T(8,128)(2,1)}, bf16[1024,128]{1,0:T(8,128)(2,1)}) custom-call(bf16[64,2048]{1,0:T(8,128)(2,1)} %get-tuple-element.15.refs_0_, bf16[1,6,16]{2,1,0:T(8,128)(2,1)} %get-tuple-element.16.refs_1_, ...), custom_call_target="tpu_custom_call" | custom-call | tf_op jit(solution)/shard_map/results/pallas_call | solution.py:784
